TPU v7x, 512 devices: a whole 4x4x16 slice. The times are simulated.
512 devices in a mesh: gx: 32 (over x, y, core), gy: 16 (over z).
Axes of the slice: x: 4, y: 4, z: 16, core: 2. Of those that a mesh axis runs over, the one named last changes fastest.
Arguments:
- iterate: float32 [512, 32, 2048], P('gx', None, 'gy'), may hold values from -6 to 6
- source: float32 [512, 32, 2048], P('gx', None, 'gy'), may hold values from -8 to 8
- labels: int32 [512, 32, 2048], P('gx', None, 'gy'), may hold values from 0 to 3
Outputs:
- corrected: float32 [512, 32, 2048], P('gx', None, 'gy')
- coarse_correction: float32 [256, 16, 1024], P('gx', 'gy')
All inputs are finite; a program needn't handle non-finite values.
Results may differ from a plain program's by a relative error of at most 0.00002.
Values sent between devices are 32-bit elements; how exact they have to be, the bound alone decides.
No kernel may reach another device: no remote copies, remote signals or barrier semaphores. Data moves between devices by JAX's collectives and lax.ppermute only.
A program may use at most 128 MiB of HBM per device.

v0:
```python
import jax
import jax.numpy as jnp
from jax import lax
from jax.sharding import PartitionSpec as P

SWEEPS = 4
COARSE_SWEEPS = 16


TABLE = (0.5, 1.0, 2.5, 6.0)
LOWER = 0.25
UPPER = 2.0


def extended(x, sides, width):
    for axis, dim in sides:
        devices, length = (lax.axis_size(axis), x.shape[dim])
        up = [(i, (i + 1) % devices) for i in range(devices - 1)]
        down = [(j, i) for i, j in up]
        last = lax.slice_in_dim(x, length - width, length, axis=dim)
        leading = lax.slice_in_dim(x, 0, width, axis=dim)
        before = lax.ppermute(last, axis, up)
        after = lax.ppermute(leading, axis, down)
        x = jnp.concatenate([before, x, after], axis=dim)
    return x


def conduct(labels):
    total = jnp.zeros(labels.shape, jnp.float32)
    for label_id, value in enumerate(TABLE):
        total = total + jnp.where(labels == label_id, jnp.float32(value), jnp.float32(0.0))
    return total


def neighbours(padded):
    return [
        padded[2:, 1:-1, 1:-1],
        padded[:-2, 1:-1, 1:-1],
        padded[1:-1, 2:, 1:-1],
        padded[1:-1, :-2, 1:-1],
        padded[1:-1, 1:-1, 2:],
        padded[1:-1, 1:-1, :-2],
    ]


def coefficients(conductance, padded, factor):
    face_coefs = [factor * (conductance + other) for other in neighbours(padded)]
    diagonal = face_coefs[0]
    for extra in face_coefs[1:]:
        diagonal = diagonal + extra
    return (face_coefs, diagonal)


def apply_op(field, padded, face_coefs):
    total = jnp.zeros(field.shape, jnp.float32)
    for coef, other in zip(face_coefs, neighbours(padded)):
        total = total + coef * (field - other)
    return total


def chebyshev(rhs, inverse, operate, sweeps):
    centre = (UPPER + LOWER) / 2.0
    radius = (UPPER - LOWER) / 2.0
    sigma = centre / radius
    weight = 1.0 / sigma
    remain = rhs
    step = inverse * remain / centre
    solution = step
    for sweep in range(1, sweeps):
        remain = remain - operate(step)
        weight_new = 1.0 / (2.0 * sigma - weight)
        step = weight_new * weight * step + 2.0 * weight_new / radius * inverse * remain
        solution = solution + step
        weight = weight_new
    return solution


def restrict(field):
    shape_in = field.shape
    parts = field.reshape(shape_in[0] // 2, 2, shape_in[1] // 2, 2, shape_in[2] // 2, 2)
    return parts.sum(axis=(1, 3, 5))


def prolong(field):
    shape_in = field.shape
    wide = jnp.broadcast_to(
        field[:, None, :, None, :, None], (shape_in[0], 2, shape_in[1], 2, shape_in[2], 2)
    )
    return wide.reshape(shape_in[0] * 2, shape_in[1] * 2, shape_in[2] * 2)


def fine_pad(field):
    padded = extended(field, (("gx", 0), ("gy", 2)), 1)
    return jnp.pad(padded, ((0, 0), (1, 1), (0, 0)))


def split_pad(field):
    padded = extended(field, (("gx", 0), ("gy", 1)), 1)
    return jnp.pad(padded, ((0, 0), (0, 0), (1, 1)))


def coarse_solve(coarse_rhs, coarse_cond, padder):
    coarse_coefs, coarse_diag = coefficients(coarse_cond, padder(coarse_cond), 2.0)

    def coarse_apply(field):
        return apply_op(field, padder(field), coarse_coefs)

    return chebyshev(coarse_rhs, 1.0 / coarse_diag, coarse_apply, COARSE_SWEEPS)


def on_device(iterate, source, labels):
    conductance = conduct(labels)
    face_coefs, diagonal = coefficients(conductance, fine_pad(conductance), 0.5)

    def fine_apply(field):
        return apply_op(field, fine_pad(field), face_coefs)

    residual = source - fine_apply(iterate)
    coarse_rhs = restrict(residual)
    coarse_cond = restrict(conductance) / 8.0
    owned_rhs, owned_cond = (
        lax.all_to_all(coarse_rhs, "gy", split_axis=1, concat_axis=2, tiled=True),
        lax.all_to_all(coarse_cond, "gy", split_axis=1, concat_axis=2, tiled=True),
    )
    coarse_out = coarse_solve(owned_rhs, owned_cond, split_pad)
    fine_fine = chebyshev(residual, 1.0 / diagonal, fine_apply, SWEEPS)
    parent = lax.all_to_all(coarse_out, "gy", split_axis=2, concat_axis=1, tiled=True)
    corrected = iterate + fine_fine + prolong(parent)
    return (corrected, coarse_out)


def solution(mesh):
    in_specs = (P("gx", None, "gy"), P("gx", None, "gy"), P("gx", None, "gy"))
    out_specs = (P("gx", None, "gy"), P("gx", "gy", None))
    return jax.shard_map(
        on_device, mesh=mesh, in_specs=in_specs, out_specs=out_specs, check_vma=False
    )
```

profile of v0, /device:TPU:2, one launch (start us, length us, event | category | flops | bytes accessed | tf_op | source)
XLA Modules:
  0.0 502.7 jit_solution(1355067892384560279)
XLA Ops:
  3.6 5.8 %collective-permute-start = (f32[1,32,128]{2,1,0:T(8,128)S(1)}, f32[1,32,128]{2,1,0:T(8,128)S(1)}, u32[]{:S(2)}, u32[]{:S(2)}) collective-permute-start(f32[1,32,128]{2,1,0:T(8,128)S(1)} %get-tuple-element.72), channel_id=1, source_target_pairs={{16,0},{32,16},{48,32},{64,48},{80,64},{96,80},{112,96},{128,112},... | collective-permute-start | bytes 49160 | tf_op jit(solution)/shard_map/ppermute | solution.py:23
  12.0 5.9 %collective-permute-start.4 = (f32[1,32,128]{2,1,0:T(8,128)S(1)}, f32[1,32,128]{2,1,0:T(8,128)S(1)}, u32[]{:S(2)}, u32[]{:S(2)}) collective-permute-start(f32[1,32,128]{2,1,0:T(8,128)S(1)} %get-tuple-element.70), channel_id=1, source_target_pairs={{16,0},{32,16},{48,32},{64,48},{80,64},{96,80},{112,96},{128,112},... | collective-permute-start | bytes 49160 | tf_op jit(solution)/shard_map/ppermute | solution.py:23
  17.9 18.1 %reshape.26 = f32[8,2,16,2,64,2]{5,4,3,2,1,0:T(8,128)} reshape(f32[16,32,128]{2,1,0:T(8,128)S(1)} %select_add_fusion) | data formatting | bytes 524288 | tf_op jit(solution)/shard_map/reshape | solution.py:80
  36.1 7.0 %reduce_sum.18 = f32[8,16,64]{2,1,0:T(8,128)S(1)} reduce(f32[8,2,16,2,64,2]{5,4,3,2,1,0:T(8,128)} %reshape.26, f32[]{:T(128)} %constant.40.clone.1), dimensions={1,3,5}, to_apply=%region_0.1 | reduce | flops 57344 | bytes 294916 | tf_op jit(solution)/shard_map/reduce_sum | solution.py:81
  43.8 15.2 %all-to-all-start = ((f32[16,1,512]{2,1,0:T(1,128)}), f32[16,1,512]{2,1,0:T(1,128)S(1)}, u32[]{:S(2)}, u32[]{:S(2)}) async-start(f32[16,1,512]{2,1,0:T(1,128)} %reshape.41), calls=%async_computation | async-start | bytes 65536 | tf_op jit(solution)/shard_map/all_to_all | solution.py:123
  59.3 3.8 collective-permute-start.6
  65.9 5.2 %collective-permute-start.2 = (f32[18,32,1]{2,1,0:T(8,128)S(1)}, f32[18,32,1]{2,1,0:T(8,128)S(1)}, u32[]{:S(2)}, u32[]{:S(2)}) collective-permute-start(f32[18,32,1]{2,1,0:T(8,128)S(1)} %get-tuple-element.60), channel_id=1, source_target_pairs={{0,1},{1,2},{2,3},{3,4},{4,5},{5,6},{6,7},{7,8},{8,9},{9,10},{10,1... | collective-permute-start | bytes 6920 | tf_op jit(solution)/shard_map/ppermute | solution.py:22
  81.3 5.7 %collective-permute-start.20 = (f32[1,1,1024]{2,0,1:T(1,128)S(1)}, f32[1,1,1024]{2,0,1:T(1,128)S(1)}, u32[]{:S(2)}, u32[]{:S(2)}) collective-permute-start(f32[1,1,1024]{2,0,1:T(1,128)S(1)} %slice.801), channel_id=1, source_target_pairs={{16,0},{32,16},{48,32},{64,48},{80,64},{96,80},{112,96},{128,112},... | collective-permute-start | bytes 12296 | tf_op jit(solution)/shard_map/ppermute | solution.py:23
  87.0 2.7 multiply_multiply_fusion
  89.8 18.1 %reshape.27 = f32[8,2,16,2,64,2]{5,4,3,2,1,0:T(8,128)} reshape(f32[16,32,128]{2,1,0:T(8,128)S(1)} %get-tuple-element.16) | data formatting | bytes 524288 | tf_op jit(solution)/shard_map/reshape | solution.py:80
  107.9 7.0 %reduce_sum.19 = f32[8,16,64]{2,1,0:T(8,128)S(1)} reduce(f32[8,2,16,2,64,2]{5,4,3,2,1,0:T(8,128)} %reshape.27, f32[]{:T(128)} %constant.40.clone.1), dimensions={1,3,5}, to_apply=%region_1.2 | reduce | flops 57344 | bytes 294916 | tf_op jit(solution)/shard_map/reduce_sum | solution.py:81
  115.7 13.6 %all-to-all-start.1 = ((f32[16,1,512]{2,1,0:T(1,128)}), f32[16,1,512]{2,1,0:T(1,128)S(1)}, u32[]{:S(2)}, u32[]{:S(2)}) async-start(f32[16,1,512]{2,1,0:T(1,128)} %reshape.43), calls=%async_computation.1 | async-start | bytes 65536 | tf_op jit(solution)/shard_map/all_to_all | solution.py:122
  130.7 4.5 collective-permute-start.23
  135.3 6.8 %all-to-all-done.1 = f32[16,1,512]{2,1,0:T(1,128)S(1)} async-done(((f32[16,1,512]{2,1,0:T(1,128)}), f32[16,1,512]{2,1,0:T(1,128)S(1)}, u32[]{:S(2)}, u32[]{:S(2)}) %all-to-all-start.1) | async-done | bytes 32800 | tf_op jit(solution)/shard_map/all_to_all | solution.py:122
  147.6 4.6 collective-permute-done.25
  153.5 4.5 collective-permute-start.27
  162.1 2.4 collective-permute-start.29
  164.5 4.6 collective-permute-done.29
  170.5 4.9 collective-permute-start.31
  179.4 2.4 collective-permute-start.33
  181.9 4.6 collective-permute-done.33
  187.8 4.9 collective-permute-start.35
  199.2 4.6 collective-permute-done.37
  205.1 4.9 collective-permute-start.39
  214.1 2.4 collective-permute-start.41
  216.5 4.6 collective-permute-done.41
  222.5 4.9 collective-permute-start.43
  231.4 2.4 collective-permute-start.45
  233.9 4.6 collective-permute-done.45
  239.8 5.1 %collective-permute-start.47 = (f32[10,1,1024]{2,0,1:T(8,128)S(1)}, f32[10,1,1024]{2,0,1:T(8,128)S(1)}, u32[]{:S(2)}, u32[]{:S(2)}) collective-permute-start(f32[10,1,1024]{2,0,1:T(8,128)S(1)} %pad_maximum_fusion.46), channel_id=1, source_target_pairs={{0,1},{1,2},{2,3},{3,4},{4,5},{5,6},{6,7},{7,8},{8,9},{9,10},{10,1... | collective-permute-start | bytes 122888 | tf_op jit(solution)/shard_map/ppermute | solution.py:22
  251.2 4.6 collective-permute-done.49
  257.1 5.1 %collective-permute-start.51 = (f32[10,1,1024]{2,0,1:T(8,128)S(1)}, f32[10,1,1024]{2,0,1:T(8,128)S(1)}, u32[]{:S(2)}, u32[]{:S(2)}) collective-permute-start(f32[10,1,1024]{2,0,1:T(8,128)S(1)} %pad_maximum_fusion.47), channel_id=1, source_target_pairs={{0,1},{1,2},{2,3},{3,4},{4,5},{5,6},{6,7},{7,8},{8,9},{9,10},{10,1... | collective-permute-start | bytes 122888 | tf_op jit(solution)/shard_map/ppermute | solution.py:22
  266.3 2.4 collective-permute-start.53
  268.7 4.6 collective-permute-done.53
  274.6 6.1 %collective-permute-start.55 = (f32[10,1,1024]{2,0,1:T(8,128)S(1)}, f32[10,1,1024]{2,0,1:T(8,128)S(1)}, u32[]{:S(2)}, u32[]{:S(2)}) collective-permute-start(f32[10,1,1024]{2,0,1:T(8,128)S(1)} %pad_maximum_fusion.48), channel_id=1, source_target_pairs={{0,1},{1,2},{2,3},{3,4},{4,5},{5,6},{6,7},{7,8},{8,9},{9,10},{10,1... | collective-permute-start | bytes 122888 | tf_op jit(solution)/shard_map/ppermute | solution.py:22
  284.8 2.4 collective-permute-start.57
  287.3 4.6 collective-permute-done.57
  293.2 6.1 %collective-permute-start.59 = (f32[10,1,1024]{2,0,1:T(8,128)S(1)}, f32[10,1,1024]{2,0,1:T(8,128)S(1)}, u32[]{:S(2)}, u32[]{:S(2)}) collective-permute-start(f32[10,1,1024]{2,0,1:T(8,128)S(1)} %pad_maximum_fusion.49), channel_id=1, source_target_pairs={{0,1},{1,2},{2,3},{3,4},{4,5},{5,6},{6,7},{7,8},{8,9},{9,10},{10,1... | collective-permute-start | bytes 122888 | tf_op jit(solution)/shard_map/ppermute | solution.py:22
  301.2 2.4 collective-permute-start.9
  304.0 5.3 %collective-permute-start.60 = (f32[1,1,1024]{2,0,1:T(1,128)S(1)}, f32[1,1,1024]{2,0,1:T(1,128)S(1)}, u32[]{:S(2)}, u32[]{:S(2)}) collective-permute-start(f32[1,1,1024]{2,0,1:T(1,128)S(1)} %get-tuple-element.85), channel_id=1, source_target_pairs={{16,0},{32,16},{48,32},{64,48},{80,64},{96,80},{112,96},{128,112},... | collective-permute-start | bytes 12296 | tf_op jit(solution)/shard_map/ppermute | solution.py:23
  311.2 5.0 %collective-permute-done.61 = f32[1,1,1024]{2,0,1:T(1,128)S(1)} collective-permute-done((f32[1,1,1024]{2,0,1:T(1,128)S(1)}, f32[1,1,1024]{2,0,1:T(1,128)S(1)}, u32[]{:S(2)}, u32[]{:S(2)}) %collective-permute-start.61) | collective-permute-done | bytes 4128 | tf_op jit(solution)/shard_map/ppermute | solution.py:22
  317.6 6.1 %collective-permute-start.63 = (f32[10,1,1024]{2,0,1:T(8,128)S(1)}, f32[10,1,1024]{2,0,1:T(8,128)S(1)}, u32[]{:S(2)}, u32[]{:S(2)}) collective-permute-start(f32[10,1,1024]{2,0,1:T(8,128)S(1)} %pad_maximum_fusion.50), channel_id=1, source_target_pairs={{0,1},{1,2},{2,3},{3,4},{4,5},{5,6},{6,7},{7,8},{8,9},{9,10},{10,1... | collective-permute-start | bytes 122888 | tf_op jit(solution)/shard_map/ppermute | solution.py:22
  323.9 5.5 %collective-permute-start.10 = (f32[18,32,1]{2,1,0:T(8,128)S(1)}, f32[18,32,1]{2,1,0:T(8,128)S(1)}, u32[]{:S(2)}, u32[]{:S(2)}) collective-permute-start(f32[18,32,1]{2,1,0:T(8,128)S(1)} %get-tuple-element.59), channel_id=1, source_target_pairs={{0,1},{1,2},{2,3},{3,4},{4,5},{5,6},{6,7},{7,8},{8,9},{9,10},{10,1... | collective-permute-start | bytes 6920 | tf_op jit(solution)/shard_map/ppermute | solution.py:22
  332.9 2.4 collective-permute-start.65
  335.3 4.2 collective-permute-done.11
  341.2 6.7 %collective-permute-start.67 = (f32[10,1,1024]{2,0,1:T(8,128)S(1)}, f32[10,1,1024]{2,0,1:T(8,128)S(1)}, u32[]{:S(2)}, u32[]{:S(2)}) collective-permute-start(f32[10,1,1024]{2,0,1:T(8,128)S(1)} %pad_maximum_fusion.51), channel_id=1, source_target_pairs={{0,1},{1,2},{2,3},{3,4},{4,5},{5,6},{6,7},{7,8},{8,9},{9,10},{10,1... | collective-permute-start | bytes 122888 | tf_op jit(solution)/shard_map/ppermute | solution.py:22
  354.5 5.3 %collective-permute-start.12 = (f32[1,32,128]{2,1,0:T(8,128)S(1)}, f32[1,32,128]{2,1,0:T(8,128)S(1)}, u32[]{:S(2)}, u32[]{:S(2)}) collective-permute-start(f32[1,32,128]{2,1,0:T(8,128)S(1)} %get-tuple-element.67), channel_id=1, source_target_pairs={{16,0},{32,16},{48,32},{64,48},{80,64},{96,80},{112,96},{128,112},... | collective-permute-start | bytes 49160 | tf_op jit(solution)/shard_map/ppermute | solution.py:23
  363.1 5.8 %collective-permute-start.71 = (f32[10,1,1024]{2,0,1:T(8,128)S(1)}, f32[10,1,1024]{2,0,1:T(8,128)S(1)}, u32[]{:S(2)}, u32[]{:S(2)}) collective-permute-start(f32[10,1,1024]{2,0,1:T(8,128)S(1)} %pad_maximum_fusion.52), channel_id=1, source_target_pairs={{0,1},{1,2},{2,3},{3,4},{4,5},{5,6},{6,7},{7,8},{8,9},{9,10},{10,1... | collective-permute-start | bytes 122888 | tf_op jit(solution)/shard_map/ppermute | solution.py:22
  371.0 4.9 collective-permute-start.72
  378.0 4.3 collective-permute-start.14
  384.9 6.0 %collective-permute-start.75 = (f32[10,1,1024]{2,0,1:T(8,128)S(1)}, f32[10,1,1024]{2,0,1:T(8,128)S(1)}, u32[]{:S(2)}, u32[]{:S(2)}) collective-permute-start(f32[10,1,1024]{2,0,1:T(8,128)S(1)} %pad_maximum_fusion.53), channel_id=1, source_target_pairs={{0,1},{1,2},{2,3},{3,4},{4,5},{5,6},{6,7},{7,8},{8,9},{9,10},{10,1... | collective-permute-start | bytes 122888 | tf_op jit(solution)/shard_map/ppermute | solution.py:22
  393.2 5.2 %collective-permute-start.76 = (f32[1,1,1024]{2,0,1:T(1,128)S(1)}, f32[1,1,1024]{2,0,1:T(1,128)S(1)}, u32[]{:S(2)}, u32[]{:S(2)}) collective-permute-start(f32[1,1,1024]{2,0,1:T(1,128)S(1)} %get-tuple-element.77), channel_id=1, source_target_pairs={{16,0},{32,16},{48,32},{64,48},{80,64},{96,80},{112,96},{128,112},... | collective-permute-start | bytes 12296 | tf_op jit(solution)/shard_map/ppermute | solution.py:23
  401.5 3.9 collective-permute-done.77
  406.7 6.1 %collective-permute-start.79 = (f32[10,1,1024]{2,0,1:T(8,128)S(1)}, f32[10,1,1024]{2,0,1:T(8,128)S(1)}, u32[]{:S(2)}, u32[]{:S(2)}) collective-permute-start(f32[10,1,1024]{2,0,1:T(8,128)S(1)} %pad_maximum_fusion.54), channel_id=1, source_target_pairs={{0,1},{1,2},{2,3},{3,4},{4,5},{5,6},{6,7},{7,8},{8,9},{9,10},{10,1... | collective-permute-start | bytes 122888 | tf_op jit(solution)/shard_map/ppermute | solution.py:22
  417.5 5.3 %collective-permute-start.80 = (f32[1,1,1024]{2,0,1:T(1,128)S(1)}, f32[1,1,1024]{2,0,1:T(1,128)S(1)}, u32[]{:S(2)}, u32[]{:S(2)}) collective-permute-start(f32[1,1,1024]{2,0,1:T(1,128)S(1)} %get-tuple-element.75), channel_id=1, source_target_pairs={{16,0},{32,16},{48,32},{64,48},{80,64},{96,80},{112,96},{128,112},... | collective-permute-start | bytes 12296 | tf_op jit(solution)/shard_map/ppermute | solution.py:23
  424.7 5.0 %collective-permute-done.81 = f32[1,1,1024]{2,0,1:T(1,128)S(1)} collective-permute-done((f32[1,1,1024]{2,0,1:T(1,128)S(1)}, f32[1,1,1024]{2,0,1:T(1,128)S(1)}, u32[]{:S(2)}, u32[]{:S(2)}) %collective-permute-start.81) | collective-permute-done | bytes 4128 | tf_op jit(solution)/shard_map/ppermute | solution.py:22
  431.1 5.8 %collective-permute-start.83 = (f32[10,1,1024]{2,0,1:T(8,128)S(1)}, f32[10,1,1024]{2,0,1:T(8,128)S(1)}, u32[]{:S(2)}, u32[]{:S(2)}) collective-permute-start(f32[10,1,1024]{2,0,1:T(8,128)S(1)} %pad_maximum_fusion.55), channel_id=1, source_target_pairs={{0,1},{1,2},{2,3},{3,4},{4,5},{5,6},{6,7},{7,8},{8,9},{9,10},{10,1... | collective-permute-start | bytes 122888 | tf_op jit(solution)/shard_map/ppermute | solution.py:22
  437.8 5.1 %collective-permute-start.18 = (f32[18,32,1]{2,1,0:T(8,128)}, f32[18,32,1]{2,1,0:T(8,128)S(1)}, u32[]{:S(2)}, u32[]{:S(2)}) collective-permute-start(f32[18,32,1]{2,1,0:T(8,128)} %get-tuple-element.55), channel_id=1, source_target_pairs={{0,1},{1,2},{2,3},{3,4},{4,5},{5,6},{6,7},{7,8},{8,9},{9,10},{10,1... | collective-permute-start | bytes 6920 | tf_op jit(solution)/shard_map/ppermute | solution.py:22
  445.7 3.7 reduce.10
  451.3 13.4 %all-to-all-start.2 = ((f32[16,1,512]{2,1,0:T(1,128)}), f32[16,1,512]{2,1,0:T(1,128)S(1)}, u32[]{:S(2)}, u32[]{:S(2)}) async-start(f32[16,1,512]{2,1,0:T(1,128)} %reshape.45), calls=%async_computation.2 | async-start | bytes 65536 | tf_op jit(solution)/shard_map/all_to_all | solution.py:127
  467.5 9.8 %all-to-all-done.2 = f32[16,1,512]{2,1,0:T(1,128)S(1)} async-done(((f32[16,1,512]{2,1,0:T(1,128)}), f32[16,1,512]{2,1,0:T(1,128)S(1)}, u32[]{:S(2)}, u32[]{:S(2)}) %all-to-all-start.2) | async-done | bytes 32800 | tf_op jit(solution)/shard_map/all_to_all | solution.py:127
  480.9 6.5 %broadcast_in_dim.31 = f32[8,2,16,2,64,2]{5,4,3,2,1,0:T(8,128)} broadcast(f32[8,16,64]{2,1,0:T(8,128)S(1)} %copy.21), dimensions={0,2,4} | broadcast | bytes 294912 | tf_op jit(solution)/shard_map/broadcast_in_dim | solution.py:86
  487.4 12.6 %reshape.28 = f32[16,32,128]{2,1,0:T(8,128)S(1)} reshape(f32[8,2,16,2,64,2]{5,4,3,2,1,0:T(8,128)} %broadcast_in_dim.31) | data formatting | bytes 524288 | tf_op jit(solution)/shard_map/reshape | solution.py:89
  500.0 2.7 fusion.9
  (236 shorter events, 129.5 us)
Async XLA Ops:
  1.7 62.7 %collective-permute-start.1 = (f32[1,32,128]{2,1,0:T(8,128)S(1)}, f32[1,32,128]{2,1,0:T(8,128)S(1)}, u32[]{:S(2)}, u32[]{:S(2)}) collective-permute-start(f32[1,32,128]{2,1,0:T(8,128)S(1)} %get-tuple-element.73), channel_id=1, source_target_pairs={{0,16},{16,32},{32,48},{48,64},{64,80},{80,96},{96,112},{112,128},... | collective-permute-start | bytes 49160 | tf_op jit(solution)/shard_map/ppermute | solution.py:22
  3.6 60.8 %collective-permute-start = (f32[1,32,128]{2,1,0:T(8,128)S(1)}, f32[1,32,128]{2,1,0:T(8,128)S(1)}, u32[]{:S(2)}, u32[]{:S(2)}) collective-permute-start(f32[1,32,128]{2,1,0:T(8,128)S(1)} %get-tuple-element.72), channel_id=1, source_target_pairs={{16,0},{32,16},{48,32},{64,48},{80,64},{96,80},{112,96},{128,112},... | collective-permute-start | bytes 49160 | tf_op jit(solution)/shard_map/ppermute | solution.py:23
  10.1 48.9 %collective-permute-start.5 = (f32[1,32,128]{2,1,0:T(8,128)S(1)}, f32[1,32,128]{2,1,0:T(8,128)S(1)}, u32[]{:S(2)}, u32[]{:S(2)}) collective-permute-start(f32[1,32,128]{2,1,0:T(8,128)S(1)} %get-tuple-element.71), channel_id=1, source_target_pairs={{0,16},{16,32},{32,48},{48,64},{64,80},{80,96},{96,112},{112,128},... | collective-permute-start | bytes 49160 | tf_op jit(solution)/shard_map/ppermute | solution.py:22
  12.0 47.0 %collective-permute-start.4 = (f32[1,32,128]{2,1,0:T(8,128)S(1)}, f32[1,32,128]{2,1,0:T(8,128)S(1)}, u32[]{:S(2)}, u32[]{:S(2)}) collective-permute-start(f32[1,32,128]{2,1,0:T(8,128)S(1)} %get-tuple-element.70), channel_id=1, source_target_pairs={{16,0},{32,16},{48,32},{64,48},{80,64},{96,80},{112,96},{128,112},... | collective-permute-start | bytes 49160 | tf_op jit(solution)/shard_map/ppermute | solution.py:23
  43.8 34.1 %all-to-all-start = ((f32[16,1,512]{2,1,0:T(1,128)}), f32[16,1,512]{2,1,0:T(1,128)S(1)}, u32[]{:S(2)}, u32[]{:S(2)}) async-start(f32[16,1,512]{2,1,0:T(1,128)} %reshape.41), calls=%async_computation | async-start | bytes 65536 | tf_op jit(solution)/shard_map/all_to_all | solution.py:123
  59.3 11.9 %collective-permute-start.6 = (f32[18,32,1]{2,1,0:T(8,128)S(1)}, f32[18,32,1]{2,1,0:T(8,128)S(1)}, u32[]{:S(2)}, u32[]{:S(2)}) collective-permute-start(f32[18,32,1]{2,1,0:T(8,128)S(1)} %get-tuple-element.63), channel_id=1, source_target_pairs={{0,1},{1,2},{2,3},{3,4},{4,5},{5,6},{6,7},{7,8},{8,9},{9,10},{10,1... | collective-permute-start | bytes 6920 | tf_op jit(solution)/shard_map/ppermute | solution.py:22
  63.1 10.4 %collective-permute-start.7 = (f32[18,32,1]{2,1,0:T(8,128)S(1)}, f32[18,32,1]{2,1,0:T(8,128)S(1)}, u32[]{:S(2)}, u32[]{:S(2)}) collective-permute-start(f32[18,32,1]{2,1,0:T(8,128)S(1)} %get-tuple-element.62), channel_id=1, source_target_pairs={{1,0},{2,1},{3,2},{4,3},{5,4},{6,5},{7,6},{8,7},{9,8},{10,9},{11,1... | collective-permute-start | bytes 6920 | tf_op jit(solution)/shard_map/ppermute | solution.py:23
  64.6 12.1 %collective-permute-start.3 = (f32[18,32,1]{2,1,0:T(8,128)S(1)}, f32[18,32,1]{2,1,0:T(8,128)S(1)}, u32[]{:S(2)}, u32[]{:S(2)}) collective-permute-start(f32[18,32,1]{2,1,0:T(8,128)S(1)} %get-tuple-element.61), channel_id=1, source_target_pairs={{1,0},{2,1},{3,2},{4,3},{5,4},{6,5},{7,6},{8,7},{9,8},{10,9},{11,1... | collective-permute-start | bytes 6920 | tf_op jit(solution)/shard_map/ppermute | solution.py:23
  65.9 10.8 %collective-permute-start.2 = (f32[18,32,1]{2,1,0:T(8,128)S(1)}, f32[18,32,1]{2,1,0:T(8,128)S(1)}, u32[]{:S(2)}, u32[]{:S(2)}) collective-permute-start(f32[18,32,1]{2,1,0:T(8,128)S(1)} %get-tuple-element.60), channel_id=1, source_target_pairs={{0,1},{1,2},{2,3},{3,4},{4,5},{5,6},{6,7},{7,8},{8,9},{9,10},{10,1... | collective-permute-start | bytes 6920 | tf_op jit(solution)/shard_map/ppermute | solution.py:22
  79.3 50.1 %collective-permute-start.21 = (f32[1,1,1024]{2,0,1:T(1,128)S(1)}, f32[1,1,1024]{2,0,1:T(1,128)S(1)}, u32[]{:S(2)}, u32[]{:S(2)}) collective-permute-start(f32[1,1,1024]{2,0,1:T(1,128)S(1)} %slice.804), channel_id=1, source_target_pairs={{0,16},{16,32},{32,48},{48,64},{64,80},{80,96},{96,112},{112,128},... | collective-permute-start | bytes 12296 | tf_op jit(solution)/shard_map/ppermute | solution.py:22
  81.3 48.1 %collective-permute-start.20 = (f32[1,1,1024]{2,0,1:T(1,128)S(1)}, f32[1,1,1024]{2,0,1:T(1,128)S(1)}, u32[]{:S(2)}, u32[]{:S(2)}) collective-permute-start(f32[1,1,1024]{2,0,1:T(1,128)S(1)} %slice.801), channel_id=1, source_target_pairs={{16,0},{32,16},{48,32},{64,48},{80,64},{96,80},{112,96},{128,112},... | collective-permute-start | bytes 12296 | tf_op jit(solution)/shard_map/ppermute | solution.py:23
  115.7 26.5 %all-to-all-start.1 = ((f32[16,1,512]{2,1,0:T(1,128)}), f32[16,1,512]{2,1,0:T(1,128)S(1)}, u32[]{:S(2)}, u32[]{:S(2)}) async-start(f32[16,1,512]{2,1,0:T(1,128)} %reshape.43), calls=%async_computation.1 | async-start | bytes 65536 | tf_op jit(solution)/shard_map/all_to_all | solution.py:122
  129.4 13.5 %collective-permute-start.22 = (f32[10,1,1024]{2,0,1:T(8,128)S(1)}, f32[10,1,1024]{2,0,1:T(8,128)S(1)}, u32[]{:S(2)}, u32[]{:S(2)}) collective-permute-start(f32[10,1,1024]{2,0,1:T(8,128)S(1)} %pad_maximum_fusion.40), channel_id=1, source_target_pairs={{1,0},{2,1},{3,2},{4,3},{5,4},{6,5},{7,6},{8,7},{9,8},{10,9},{11,1... | collective-permute-start | bytes 122888 | tf_op jit(solution)/shard_map/ppermute | solution.py:23
  130.7 12.2 %collective-permute-start.23 = (f32[10,1,1024]{2,0,1:T(8,128)S(1)}, f32[10,1,1024]{2,0,1:T(8,128)S(1)}, u32[]{:S(2)}, u32[]{:S(2)}) collective-permute-start(f32[10,1,1024]{2,0,1:T(8,128)S(1)} %pad_maximum_fusion.40), channel_id=1, source_target_pairs={{0,1},{1,2},{2,3},{3,4},{4,5},{5,6},{6,7},{7,8},{8,9},{9,10},{10,1... | collective-permute-start | bytes 122888 | tf_op jit(solution)/shard_map/ppermute | solution.py:22
  145.1 7.0 %collective-permute-start.25 = (f32[1,1,1024]{2,0,1:T(1,128)S(1)}, f32[1,1,1024]{2,0,1:T(1,128)S(1)}, u32[]{:S(2)}, u32[]{:S(2)}) collective-permute-start(f32[1,1,1024]{2,0,1:T(1,128)S(1)} %get-tuple-element.102), channel_id=1, source_target_pairs={{0,16},{16,32},{32,48},{48,64},{64,80},{80,96},{96,112},{112,128},... | collective-permute-start | bytes 12296 | tf_op jit(solution)/shard_map/ppermute | solution.py:22
  162.1 7.0 %collective-permute-start.29 = (f32[1,1,1024]{2,0,1:T(1,128)S(1)}, f32[1,1,1024]{2,0,1:T(1,128)S(1)}, u32[]{:S(2)}, u32[]{:S(2)}) collective-permute-start(f32[1,1,1024]{2,0,1:T(1,128)S(1)} %get-tuple-element.100), channel_id=1, source_target_pairs={{0,16},{16,32},{32,48},{48,64},{64,80},{80,96},{96,112},{112,128},... | collective-permute-start | bytes 12296 | tf_op jit(solution)/shard_map/ppermute | solution.py:22
  179.4 7.0 %collective-permute-start.33 = (f32[1,1,1024]{2,0,1:T(1,128)S(1)}, f32[1,1,1024]{2,0,1:T(1,128)S(1)}, u32[]{:S(2)}, u32[]{:S(2)}) collective-permute-start(f32[1,1,1024]{2,0,1:T(1,128)S(1)} %get-tuple-element.98), channel_id=1, source_target_pairs={{0,16},{16,32},{32,48},{48,64},{64,80},{80,96},{96,112},{112,128},... | collective-permute-start | bytes 12296 | tf_op jit(solution)/shard_map/ppermute | solution.py:22
  196.8 7.0 %collective-permute-start.37 = (f32[1,1,1024]{2,0,1:T(1,128)S(1)}, f32[1,1,1024]{2,0,1:T(1,128)S(1)}, u32[]{:S(2)}, u32[]{:S(2)}) collective-permute-start(f32[1,1,1024]{2,0,1:T(1,128)S(1)} %get-tuple-element.96), channel_id=1, source_target_pairs={{0,16},{16,32},{32,48},{48,64},{64,80},{80,96},{96,112},{112,128},... | collective-permute-start | bytes 12296 | tf_op jit(solution)/shard_map/ppermute | solution.py:22
  214.1 7.0 %collective-permute-start.41 = (f32[1,1,1024]{2,0,1:T(1,128)S(1)}, f32[1,1,1024]{2,0,1:T(1,128)S(1)}, u32[]{:S(2)}, u32[]{:S(2)}) collective-permute-start(f32[1,1,1024]{2,0,1:T(1,128)S(1)} %get-tuple-element.94), channel_id=1, source_target_pairs={{0,16},{16,32},{32,48},{48,64},{64,80},{80,96},{96,112},{112,128},... | collective-permute-start | bytes 12296 | tf_op jit(solution)/shard_map/ppermute | solution.py:22
  231.4 7.0 %collective-permute-start.45 = (f32[1,1,1024]{2,0,1:T(1,128)S(1)}, f32[1,1,1024]{2,0,1:T(1,128)S(1)}, u32[]{:S(2)}, u32[]{:S(2)}) collective-permute-start(f32[1,1,1024]{2,0,1:T(1,128)S(1)} %get-tuple-element.92), channel_id=1, source_target_pairs={{0,16},{16,32},{32,48},{48,64},{64,80},{80,96},{96,112},{112,128},... | collective-permute-start | bytes 12296 | tf_op jit(solution)/shard_map/ppermute | solution.py:22
  248.8 7.0 %collective-permute-start.49 = (f32[1,1,1024]{2,0,1:T(1,128)S(1)}, f32[1,1,1024]{2,0,1:T(1,128)S(1)}, u32[]{:S(2)}, u32[]{:S(2)}) collective-permute-start(f32[1,1,1024]{2,0,1:T(1,128)S(1)} %get-tuple-element.90), channel_id=1, source_target_pairs={{0,16},{16,32},{32,48},{48,64},{64,80},{80,96},{96,112},{112,128},... | collective-permute-start | bytes 12296 | tf_op jit(solution)/shard_map/ppermute | solution.py:22
  266.3 7.0 %collective-permute-start.53 = (f32[1,1,1024]{2,0,1:T(1,128)S(1)}, f32[1,1,1024]{2,0,1:T(1,128)S(1)}, u32[]{:S(2)}, u32[]{:S(2)}) collective-permute-start(f32[1,1,1024]{2,0,1:T(1,128)S(1)} %get-tuple-element.88), channel_id=1, source_target_pairs={{0,16},{16,32},{32,48},{48,64},{64,80},{80,96},{96,112},{112,128},... | collective-permute-start | bytes 12296 | tf_op jit(solution)/shard_map/ppermute | solution.py:22
  273.3 7.7 %collective-permute-start.54 = (f32[10,1,1024]{2,0,1:T(8,128)S(1)}, f32[10,1,1024]{2,0,1:T(8,128)S(1)}, u32[]{:S(2)}, u32[]{:S(2)}) collective-permute-start(f32[10,1,1024]{2,0,1:T(8,128)S(1)} %pad_maximum_fusion.48), channel_id=1, source_target_pairs={{1,0},{2,1},{3,2},{4,3},{5,4},{6,5},{7,6},{8,7},{9,8},{10,9},{11,1... | collective-permute-start | bytes 122888 | tf_op jit(solution)/shard_map/ppermute | solution.py:23
  274.6 8.0 %collective-permute-start.55 = (f32[10,1,1024]{2,0,1:T(8,128)S(1)}, f32[10,1,1024]{2,0,1:T(8,128)S(1)}, u32[]{:S(2)}, u32[]{:S(2)}) collective-permute-start(f32[10,1,1024]{2,0,1:T(8,128)S(1)} %pad_maximum_fusion.48), channel_id=1, source_target_pairs={{0,1},{1,2},{2,3},{3,4},{4,5},{5,6},{6,7},{7,8},{8,9},{9,10},{10,1... | collective-permute-start | bytes 122888 | tf_op jit(solution)/shard_map/ppermute | solution.py:22
  284.8 7.0 %collective-permute-start.57 = (f32[1,1,1024]{2,0,1:T(1,128)S(1)}, f32[1,1,1024]{2,0,1:T(1,128)S(1)}, u32[]{:S(2)}, u32[]{:S(2)}) collective-permute-start(f32[1,1,1024]{2,0,1:T(1,128)S(1)} %get-tuple-element.86), channel_id=1, source_target_pairs={{0,16},{16,32},{32,48},{48,64},{64,80},{80,96},{96,112},{112,128},... | collective-permute-start | bytes 12296 | tf_op jit(solution)/shard_map/ppermute | solution.py:22
  291.9 11.8 %collective-permute-start.58 = (f32[10,1,1024]{2,0,1:T(8,128)S(1)}, f32[10,1,1024]{2,0,1:T(8,128)S(1)}, u32[]{:S(2)}, u32[]{:S(2)}) collective-permute-start(f32[10,1,1024]{2,0,1:T(8,128)S(1)} %pad_maximum_fusion.49), channel_id=1, source_target_pairs={{1,0},{2,1},{3,2},{4,3},{5,4},{6,5},{7,6},{8,7},{9,8},{10,9},{11,1... | collective-permute-start | bytes 122888 | tf_op jit(solution)/shard_map/ppermute | solution.py:23
  293.2 10.5 %collective-permute-start.59 = (f32[10,1,1024]{2,0,1:T(8,128)S(1)}, f32[10,1,1024]{2,0,1:T(8,128)S(1)}, u32[]{:S(2)}, u32[]{:S(2)}) collective-permute-start(f32[10,1,1024]{2,0,1:T(8,128)S(1)} %pad_maximum_fusion.49), channel_id=1, source_target_pairs={{0,1},{1,2},{2,3},{3,4},{4,5},{5,6},{6,7},{7,8},{8,9},{9,10},{10,1... | collective-permute-start | bytes 122888 | tf_op jit(solution)/shard_map/ppermute | solution.py:22
  299.3 11.8 %collective-permute-start.8 = (f32[1,32,128]{2,1,0:T(8,128)S(1)}, f32[1,32,128]{2,1,0:T(8,128)S(1)}, u32[]{:S(2)}, u32[]{:S(2)}) collective-permute-start(f32[1,32,128]{2,1,0:T(8,128)S(1)} %get-tuple-element.69), channel_id=1, source_target_pairs={{16,0},{32,16},{48,32},{64,48},{80,64},{96,80},{112,96},{128,112},... | collective-permute-start | bytes 49160 | tf_op jit(solution)/shard_map/ppermute | solution.py:23
  301.2 9.9 %collective-permute-start.9 = (f32[1,32,128]{2,1,0:T(8,128)S(1)}, f32[1,32,128]{2,1,0:T(8,128)S(1)}, u32[]{:S(2)}, u32[]{:S(2)}) collective-permute-start(f32[1,32,128]{2,1,0:T(8,128)S(1)} %get-tuple-element.68), channel_id=1, source_target_pairs={{0,16},{16,32},{32,48},{48,64},{64,80},{80,96},{96,112},{112,128},... | collective-permute-start | bytes 49160 | tf_op jit(solution)/shard_map/ppermute | solution.py:22
  304.0 7.3 %collective-permute-start.60 = (f32[1,1,1024]{2,0,1:T(1,128)S(1)}, f32[1,1,1024]{2,0,1:T(1,128)S(1)}, u32[]{:S(2)}, u32[]{:S(2)}) collective-permute-start(f32[1,1,1024]{2,0,1:T(1,128)S(1)} %get-tuple-element.85), channel_id=1, source_target_pairs={{16,0},{32,16},{48,32},{64,48},{80,64},{96,80},{112,96},{128,112},... | collective-permute-start | bytes 12296 | tf_op jit(solution)/shard_map/ppermute | solution.py:23
  309.2 7.0 %collective-permute-start.61 = (f32[1,1,1024]{2,0,1:T(1,128)S(1)}, f32[1,1,1024]{2,0,1:T(1,128)S(1)}, u32[]{:S(2)}, u32[]{:S(2)}) collective-permute-start(f32[1,1,1024]{2,0,1:T(1,128)S(1)} %get-tuple-element.84), channel_id=1, source_target_pairs={{0,16},{16,32},{32,48},{48,64},{64,80},{80,96},{96,112},{112,128},... | collective-permute-start | bytes 12296 | tf_op jit(solution)/shard_map/ppermute | solution.py:22
  316.3 14.4 %collective-permute-start.62 = (f32[10,1,1024]{2,0,1:T(8,128)S(1)}, f32[10,1,1024]{2,0,1:T(8,128)S(1)}, u32[]{:S(2)}, u32[]{:S(2)}) collective-permute-start(f32[10,1,1024]{2,0,1:T(8,128)S(1)} %pad_maximum_fusion.50), channel_id=1, source_target_pairs={{1,0},{2,1},{3,2},{4,3},{5,4},{6,5},{7,6},{8,7},{9,8},{10,9},{11,1... | collective-permute-start | bytes 122888 | tf_op jit(solution)/shard_map/ppermute | solution.py:23
  317.6 13.1 %collective-permute-start.63 = (f32[10,1,1024]{2,0,1:T(8,128)S(1)}, f32[10,1,1024]{2,0,1:T(8,128)S(1)}, u32[]{:S(2)}, u32[]{:S(2)}) collective-permute-start(f32[10,1,1024]{2,0,1:T(8,128)S(1)} %pad_maximum_fusion.50), channel_id=1, source_target_pairs={{0,1},{1,2},{2,3},{3,4},{4,5},{5,6},{6,7},{7,8},{8,9},{9,10},{10,1... | collective-permute-start | bytes 122888 | tf_op jit(solution)/shard_map/ppermute | solution.py:22
  323.9 11.5 %collective-permute-start.10 = (f32[18,32,1]{2,1,0:T(8,128)S(1)}, f32[18,32,1]{2,1,0:T(8,128)S(1)}, u32[]{:S(2)}, u32[]{:S(2)}) collective-permute-start(f32[18,32,1]{2,1,0:T(8,128)S(1)} %get-tuple-element.59), channel_id=1, source_target_pairs={{0,1},{1,2},{2,3},{3,4},{4,5},{5,6},{6,7},{7,8},{8,9},{9,10},{10,1... | collective-permute-start | bytes 6920 | tf_op jit(solution)/shard_map/ppermute | solution.py:22
  329.4 10.2 %collective-permute-start.11 = (f32[18,32,1]{2,1,0:T(8,128)S(1)}, f32[18,32,1]{2,1,0:T(8,128)S(1)}, u32[]{:S(2)}, u32[]{:S(2)}) collective-permute-start(f32[18,32,1]{2,1,0:T(8,128)S(1)} %get-tuple-element.58), channel_id=1, source_target_pairs={{1,0},{2,1},{3,2},{4,3},{5,4},{6,5},{7,6},{8,7},{9,8},{10,9},{11,1... | collective-permute-start | bytes 6920 | tf_op jit(solution)/shard_map/ppermute | solution.py:23
  331.0 8.9 %collective-permute-start.64 = (f32[1,1,1024]{2,0,1:T(1,128)S(1)}, f32[1,1,1024]{2,0,1:T(1,128)S(1)}, u32[]{:S(2)}, u32[]{:S(2)}) collective-permute-start(f32[1,1,1024]{2,0,1:T(1,128)S(1)} %get-tuple-element.83), channel_id=1, source_target_pairs={{16,0},{32,16},{48,32},{64,48},{80,64},{96,80},{112,96},{128,112},... | collective-permute-start | bytes 12296 | tf_op jit(solution)/shard_map/ppermute | solution.py:23
  332.9 7.0 %collective-permute-start.65 = (f32[1,1,1024]{2,0,1:T(1,128)S(1)}, f32[1,1,1024]{2,0,1:T(1,128)S(1)}, u32[]{:S(2)}, u32[]{:S(2)}) collective-permute-start(f32[1,1,1024]{2,0,1:T(1,128)S(1)} %get-tuple-element.82), channel_id=1, source_target_pairs={{0,16},{16,32},{32,48},{48,64},{64,80},{80,96},{96,112},{112,128},... | collective-permute-start | bytes 12296 | tf_op jit(solution)/shard_map/ppermute | solution.py:22
  339.9 8.5 %collective-permute-start.66 = (f32[10,1,1024]{2,0,1:T(8,128)S(1)}, f32[10,1,1024]{2,0,1:T(8,128)S(1)}, u32[]{:S(2)}, u32[]{:S(2)}) collective-permute-start(f32[10,1,1024]{2,0,1:T(8,128)S(1)} %pad_maximum_fusion.51), channel_id=1, source_target_pairs={{1,0},{2,1},{3,2},{4,3},{5,4},{6,5},{7,6},{8,7},{9,8},{10,9},{11,1... | collective-permute-start | bytes 122888 | tf_op jit(solution)/shard_map/ppermute | solution.py:23
  341.2 8.6 %collective-permute-start.67 = (f32[10,1,1024]{2,0,1:T(8,128)S(1)}, f32[10,1,1024]{2,0,1:T(8,128)S(1)}, u32[]{:S(2)}, u32[]{:S(2)}) collective-permute-start(f32[10,1,1024]{2,0,1:T(8,128)S(1)} %pad_maximum_fusion.51), channel_id=1, source_target_pairs={{0,1},{1,2},{2,3},{3,4},{4,5},{5,6},{6,7},{7,8},{8,9},{9,10},{10,1... | collective-permute-start | bytes 122888 | tf_op jit(solution)/shard_map/ppermute | solution.py:22
  350.1 11.6 %collective-permute-start.68 = (f32[1,1,1024]{2,0,1:T(1,128)S(1)}, f32[1,1,1024]{2,0,1:T(1,128)S(1)}, u32[]{:S(2)}, u32[]{:S(2)}) collective-permute-start(f32[1,1,1024]{2,0,1:T(1,128)S(1)} %get-tuple-element.81), channel_id=1, source_target_pairs={{16,0},{32,16},{48,32},{64,48},{80,64},{96,80},{112,96},{128,112},... | collective-permute-start | bytes 12296 | tf_op jit(solution)/shard_map/ppermute | solution.py:23
  352.1 9.6 %collective-permute-start.69 = (f32[1,1,1024]{2,0,1:T(1,128)S(1)}, f32[1,1,1024]{2,0,1:T(1,128)S(1)}, u32[]{:S(2)}, u32[]{:S(2)}) collective-permute-start(f32[1,1,1024]{2,0,1:T(1,128)S(1)} %get-tuple-element.80), channel_id=1, source_target_pairs={{0,16},{16,32},{32,48},{48,64},{64,80},{80,96},{96,112},{112,128},... | collective-permute-start | bytes 12296 | tf_op jit(solution)/shard_map/ppermute | solution.py:22
  354.5 14.3 %collective-permute-start.12 = (f32[1,32,128]{2,1,0:T(8,128)S(1)}, f32[1,32,128]{2,1,0:T(8,128)S(1)}, u32[]{:S(2)}, u32[]{:S(2)}) collective-permute-start(f32[1,32,128]{2,1,0:T(8,128)S(1)} %get-tuple-element.67), channel_id=1, source_target_pairs={{16,0},{32,16},{48,32},{64,48},{80,64},{96,80},{112,96},{128,112},... | collective-permute-start | bytes 49160 | tf_op jit(solution)/shard_map/ppermute | solution.py:23
  359.8 9.1 %collective-permute-start.13 = (f32[1,32,128]{2,1,0:T(8,128)S(1)}, f32[1,32,128]{2,1,0:T(8,128)S(1)}, u32[]{:S(2)}, u32[]{:S(2)}) collective-permute-start(f32[1,32,128]{2,1,0:T(8,128)S(1)} %get-tuple-element.66), channel_id=1, source_target_pairs={{0,16},{16,32},{32,48},{48,64},{64,80},{80,96},{96,112},{112,128},... | collective-permute-start | bytes 49160 | tf_op jit(solution)/shard_map/ppermute | solution.py:22
  361.8 7.4 %collective-permute-start.70 = (f32[10,1,1024]{2,0,1:T(8,128)S(1)}, f32[10,1,1024]{2,0,1:T(8,128)S(1)}, u32[]{:S(2)}, u32[]{:S(2)}) collective-permute-start(f32[10,1,1024]{2,0,1:T(8,128)S(1)} %pad_maximum_fusion.52), channel_id=1, source_target_pairs={{1,0},{2,1},{3,2},{4,3},{5,4},{6,5},{7,6},{8,7},{9,8},{10,9},{11,1... | collective-permute-start | bytes 122888 | tf_op jit(solution)/shard_map/ppermute | solution.py:23
  363.1 7.7 %collective-permute-start.71 = (f32[10,1,1024]{2,0,1:T(8,128)S(1)}, f32[10,1,1024]{2,0,1:T(8,128)S(1)}, u32[]{:S(2)}, u32[]{:S(2)}) collective-permute-start(f32[10,1,1024]{2,0,1:T(8,128)S(1)} %pad_maximum_fusion.52), channel_id=1, source_target_pairs={{0,1},{1,2},{2,3},{3,4},{4,5},{5,6},{6,7},{7,8},{8,9},{9,10},{10,1... | collective-permute-start | bytes 122888 | tf_op jit(solution)/shard_map/ppermute | solution.py:22
  371.0 12.6 %collective-permute-start.72 = (f32[1,1,1024]{2,0,1:T(1,128)S(1)}, f32[1,1,1024]{2,0,1:T(1,128)S(1)}, u32[]{:S(2)}, u32[]{:S(2)}) collective-permute-start(f32[1,1,1024]{2,0,1:T(1,128)S(1)} %get-tuple-element.79), channel_id=1, source_target_pairs={{16,0},{32,16},{48,32},{64,48},{80,64},{96,80},{112,96},{128,112},... | collective-permute-start | bytes 12296 | tf_op jit(solution)/shard_map/ppermute | solution.py:23
  375.9 7.7 %collective-permute-start.73 = (f32[1,1,1024]{2,0,1:T(1,128)S(1)}, f32[1,1,1024]{2,0,1:T(1,128)S(1)}, u32[]{:S(2)}, u32[]{:S(2)}) collective-permute-start(f32[1,1,1024]{2,0,1:T(1,128)S(1)} %get-tuple-element.78), channel_id=1, source_target_pairs={{0,16},{16,32},{32,48},{48,64},{64,80},{80,96},{96,112},{112,128},... | collective-permute-start | bytes 12296 | tf_op jit(solution)/shard_map/ppermute | solution.py:22
  378.0 13.0 %collective-permute-start.14 = (f32[18,32,1]{2,1,0:T(8,128)S(1)}, f32[18,32,1]{2,1,0:T(8,128)S(1)}, u32[]{:S(2)}, u32[]{:S(2)}) collective-permute-start(f32[18,32,1]{2,1,0:T(8,128)S(1)} %get-tuple-element.57), channel_id=1, source_target_pairs={{0,1},{1,2},{2,3},{3,4},{4,5},{5,6},{6,7},{7,8},{8,9},{9,10},{10,1... | collective-permute-start | bytes 6920 | tf_op jit(solution)/shard_map/ppermute | solution.py:22
  382.3 9.9 %collective-permute-start.15 = (f32[18,32,1]{2,1,0:T(8,128)S(1)}, f32[18,32,1]{2,1,0:T(8,128)S(1)}, u32[]{:S(2)}, u32[]{:S(2)}) collective-permute-start(f32[18,32,1]{2,1,0:T(8,128)S(1)} %get-tuple-element.56), channel_id=1, source_target_pairs={{1,0},{2,1},{3,2},{4,3},{5,4},{6,5},{7,6},{8,7},{9,8},{10,9},{11,1... | collective-permute-start | bytes 6920 | tf_op jit(solution)/shard_map/ppermute | solution.py:23
  383.6 9.2 %collective-permute-start.74 = (f32[10,1,1024]{2,0,1:T(8,128)S(1)}, f32[10,1,1024]{2,0,1:T(8,128)S(1)}, u32[]{:S(2)}, u32[]{:S(2)}) collective-permute-start(f32[10,1,1024]{2,0,1:T(8,128)S(1)} %pad_maximum_fusion.53), channel_id=1, source_target_pairs={{1,0},{2,1},{3,2},{4,3},{5,4},{6,5},{7,6},{8,7},{9,8},{10,9},{11,1... | collective-permute-start | bytes 122888 | tf_op jit(solution)/shard_map/ppermute | solution.py:23
  384.9 7.9 %collective-permute-start.75 = (f32[10,1,1024]{2,0,1:T(8,128)S(1)}, f32[10,1,1024]{2,0,1:T(8,128)S(1)}, u32[]{:S(2)}, u32[]{:S(2)}) collective-permute-start(f32[10,1,1024]{2,0,1:T(8,128)S(1)} %pad_maximum_fusion.53), channel_id=1, source_target_pairs={{0,1},{1,2},{2,3},{3,4},{4,5},{5,6},{6,7},{7,8},{8,9},{9,10},{10,1... | collective-permute-start | bytes 122888 | tf_op jit(solution)/shard_map/ppermute | solution.py:22
  393.2 8.3 %collective-permute-start.76 = (f32[1,1,1024]{2,0,1:T(1,128)S(1)}, f32[1,1,1024]{2,0,1:T(1,128)S(1)}, u32[]{:S(2)}, u32[]{:S(2)}) collective-permute-start(f32[1,1,1024]{2,0,1:T(1,128)S(1)} %get-tuple-element.77), channel_id=1, source_target_pairs={{16,0},{32,16},{48,32},{64,48},{80,64},{96,80},{112,96},{128,112},... | collective-permute-start | bytes 12296 | tf_op jit(solution)/shard_map/ppermute | solution.py:23
  398.4 7.0 %collective-permute-start.77 = (f32[1,1,1024]{2,0,1:T(1,128)S(1)}, f32[1,1,1024]{2,0,1:T(1,128)S(1)}, u32[]{:S(2)}, u32[]{:S(2)}) collective-permute-start(f32[1,1,1024]{2,0,1:T(1,128)S(1)} %get-tuple-element.76), channel_id=1, source_target_pairs={{0,16},{16,32},{32,48},{48,64},{64,80},{80,96},{96,112},{112,128},... | collective-permute-start | bytes 12296 | tf_op jit(solution)/shard_map/ppermute | solution.py:22
  405.4 11.8 %collective-permute-start.78 = (f32[10,1,1024]{2,0,1:T(8,128)S(1)}, f32[10,1,1024]{2,0,1:T(8,128)S(1)}, u32[]{:S(2)}, u32[]{:S(2)}) collective-permute-start(f32[10,1,1024]{2,0,1:T(8,128)S(1)} %pad_maximum_fusion.54), channel_id=1, source_target_pairs={{1,0},{2,1},{3,2},{4,3},{5,4},{6,5},{7,6},{8,7},{9,8},{10,9},{11,1... | collective-permute-start | bytes 122888 | tf_op jit(solution)/shard_map/ppermute | solution.py:23
  406.7 10.5 %collective-permute-start.79 = (f32[10,1,1024]{2,0,1:T(8,128)S(1)}, f32[10,1,1024]{2,0,1:T(8,128)S(1)}, u32[]{:S(2)}, u32[]{:S(2)}) collective-permute-start(f32[10,1,1024]{2,0,1:T(8,128)S(1)} %pad_maximum_fusion.54), channel_id=1, source_target_pairs={{0,1},{1,2},{2,3},{3,4},{4,5},{5,6},{6,7},{7,8},{8,9},{9,10},{10,1... | collective-permute-start | bytes 122888 | tf_op jit(solution)/shard_map/ppermute | solution.py:22
  412.8 11.8 %collective-permute-start.16 = (f32[1,32,128]{2,1,0:T(8,128)S(1)}, f32[1,32,128]{2,1,0:T(8,128)S(1)}, u32[]{:S(2)}, u32[]{:S(2)}) collective-permute-start(f32[1,32,128]{2,1,0:T(8,128)S(1)} %get-tuple-element.65), channel_id=1, source_target_pairs={{16,0},{32,16},{48,32},{64,48},{80,64},{96,80},{112,96},{128,112},... | collective-permute-start | bytes 49160 | tf_op jit(solution)/shard_map/ppermute | solution.py:23
  414.8 9.9 %collective-permute-start.17 = (f32[1,32,128]{2,1,0:T(8,128)S(1)}, f32[1,32,128]{2,1,0:T(8,128)S(1)}, u32[]{:S(2)}, u32[]{:S(2)}) collective-permute-start(f32[1,32,128]{2,1,0:T(8,128)S(1)} %get-tuple-element.64), channel_id=1, source_target_pairs={{0,16},{16,32},{32,48},{48,64},{64,80},{80,96},{96,112},{112,128},... | collective-permute-start | bytes 49160 | tf_op jit(solution)/shard_map/ppermute | solution.py:22
  417.5 7.3 %collective-permute-start.80 = (f32[1,1,1024]{2,0,1:T(1,128)S(1)}, f32[1,1,1024]{2,0,1:T(1,128)S(1)}, u32[]{:S(2)}, u32[]{:S(2)}) collective-permute-start(f32[1,1,1024]{2,0,1:T(1,128)S(1)} %get-tuple-element.75), channel_id=1, source_target_pairs={{16,0},{32,16},{48,32},{64,48},{80,64},{96,80},{112,96},{128,112},... | collective-permute-start | bytes 12296 | tf_op jit(solution)/shard_map/ppermute | solution.py:23
  422.7 7.0 %collective-permute-start.81 = (f32[1,1,1024]{2,0,1:T(1,128)S(1)}, f32[1,1,1024]{2,0,1:T(1,128)S(1)}, u32[]{:S(2)}, u32[]{:S(2)}) collective-permute-start(f32[1,1,1024]{2,0,1:T(1,128)S(1)} %get-tuple-element.74), channel_id=1, source_target_pairs={{0,16},{16,32},{32,48},{48,64},{64,80},{80,96},{96,112},{112,128},... | collective-permute-start | bytes 12296 | tf_op jit(solution)/shard_map/ppermute | solution.py:22
  429.8 14.5 %collective-permute-start.82 = (f32[10,1,1024]{2,0,1:T(8,128)S(1)}, f32[10,1,1024]{2,0,1:T(8,128)S(1)}, u32[]{:S(2)}, u32[]{:S(2)}) collective-permute-start(f32[10,1,1024]{2,0,1:T(8,128)S(1)} %pad_maximum_fusion.55), channel_id=1, source_target_pairs={{1,0},{2,1},{3,2},{4,3},{5,4},{6,5},{7,6},{8,7},{9,8},{10,9},{11,1... | collective-permute-start | bytes 122888 | tf_op jit(solution)/shard_map/ppermute | solution.py:23
  431.1 13.2 %collective-permute-start.83 = (f32[10,1,1024]{2,0,1:T(8,128)S(1)}, f32[10,1,1024]{2,0,1:T(8,128)S(1)}, u32[]{:S(2)}, u32[]{:S(2)}) collective-permute-start(f32[10,1,1024]{2,0,1:T(8,128)S(1)} %pad_maximum_fusion.55), channel_id=1, source_target_pairs={{0,1},{1,2},{2,3},{3,4},{4,5},{5,6},{6,7},{7,8},{8,9},{9,10},{10,1... | collective-permute-start | bytes 122888 | tf_op jit(solution)/shard_map/ppermute | solution.py:22
  437.8 26.9 %collective-permute-start.18 = (f32[18,32,1]{2,1,0:T(8,128)}, f32[18,32,1]{2,1,0:T(8,128)S(1)}, u32[]{:S(2)}, u32[]{:S(2)}) collective-permute-start(f32[18,32,1]{2,1,0:T(8,128)} %get-tuple-element.55), channel_id=1, source_target_pairs={{0,1},{1,2},{2,3},{3,4},{4,5},{5,6},{6,7},{7,8},{8,9},{9,10},{10,1... | collective-permute-start | bytes 6920 | tf_op jit(solution)/shard_map/ppermute | solution.py:22
  443.0 21.7 %collective-permute-start.19 = (f32[18,32,1]{2,1,0:T(8,128)}, f32[18,32,1]{2,1,0:T(8,128)}, u32[]{:S(2)}, u32[]{:S(2)}) collective-permute-start(f32[18,32,1]{2,1,0:T(8,128)} %get-tuple-element.54), channel_id=1, source_target_pairs={{1,0},{2,1},{3,2},{4,3},{5,4},{6,5},{7,6},{8,7},{9,8},{10,9},{11,1... | collective-permute-start | bytes 6920 | tf_op jit(solution)/shard_map/ppermute | solution.py:23
  451.3 26.0 %all-to-all-start.2 = ((f32[16,1,512]{2,1,0:T(1,128)}), f32[16,1,512]{2,1,0:T(1,128)S(1)}, u32[]{:S(2)}, u32[]{:S(2)}) async-start(f32[16,1,512]{2,1,0:T(1,128)} %reshape.45), calls=%async_computation.2 | async-start | bytes 65536 | tf_op jit(solution)/shard_map/all_to_all | solution.py:127
  (26 other events, 188.0 us)
where the time goes:
time: 506 us; the launch traced here: 503 us
  starting transfers between devices  296 us (58%)
  waiting for transfers between devices  100 us (20%)
  local copies, waits for them, and re-layouts  66.9 us (13%)
  other arithmetic  37.6 us (7%)
    ppermute x42, starting transfers between devices, extended(): before = lax.ppermute(last, axis, up)  158 us
    ppermute x42, starting transfers between devices, extended(): after = lax.ppermute(leading, axis, down)  95.4 us
    ppermute x42, waiting for transfers between devices, extended(): before = lax.ppermute(last, axis, up)  71.2 us
    reshape x2, local copies, waits for them, and re-layouts, restrict(): field.reshape(shape_in[0] // 2, 2, shape_in[1] // 2, 2, shape_in[2] // 2, 2)  36.3 us
    all_to_all x1, starting transfers between devices, on_device(): lax.all_to_all(coarse_cond, 'gy', split_axis=1, concat_axis=2, tiled=True)  15.2 us
    reduce_sum x2, other arithmetic, restrict(): return parts.sum(axis=(1, 3, 5))  14 us
    all_to_all x1, starting transfers between devices, on_device(): lax.all_to_all(coarse_rhs, 'gy', split_axis=1, concat_axis=2, tiled=True)  13.6 us
    all_to_all x1, starting transfers between devices, on_device(): lax.all_to_all(coarse_out, 'gy', split_axis=2, concat_axis=1, tiled=True)  13.4 us
  transfers between devices with their start and end apart: 87, of which 38 were waited for; matrix products, arithmetic and copies ran while one was open for 15% of the time, Pallas kernels for 0%

commit v1 on v0

v1 whole, which is shorter than its diff:
```python
import jax
import jax.numpy as jnp
from jax import lax
from jax.experimental import pallas as pl
from jax.experimental.pallas import tpu as pltpu
from jax.sharding import PartitionSpec as P

SWEEPS = 4
COARSE_SWEEPS = 16
TABLE = (0.5, 1.0, 2.5, 6.0)
LOWER = 0.25
UPPER = 2.0
F32 = jnp.float32

ROWS, NZ, LANES = 16, 32, 128
CROWS, CZ, CLANES = 8, 16, 64
HALO = SWEEPS
EXT = ROWS + 2 * HALO
CEXT = CROWS + 2 * COARSE_SWEEPS


def weights(sweeps):
    centre = (UPPER + LOWER) / 2.0
    radius = (UPPER - LOWER) / 2.0
    sigma = centre / radius
    rho = 1.0 / sigma
    pairs = []
    for _ in range(1, sweeps):
        rho_new = 1.0 / (2.0 * sigma - rho)
        pairs.append((rho_new * rho, 2.0 * rho_new / radius))
        rho = rho_new
    return 1.0 / centre, pairs


def conduct(labels):
    total = jnp.zeros(labels.shape, F32)
    for label_id, value in enumerate(TABLE):
        total = jnp.where(labels == label_id, F32(value), total)
    return total


def roll(x, shift, axis):
    size = x.shape[axis]
    shift = shift % size
    return x if shift == 0 else pltpu.roll(x, shift, axis)


def iota(shape, axis):
    return lax.broadcasted_iota(jnp.int32, shape, axis)


def flux(k_a, k_b, v_a, v_b):
    return 0.5 * (k_a + k_b) * (v_a - v_b)


def dot(a, b):
    return jnp.dot(a, b, precision=lax.Precision.HIGHEST, preferred_element_type=F32)


def residual_kernel(flags, it, src, lab, sib, out, r_ref, k_ref, v_ref, c_ref, up_ref, dn_ref, pool):
    first = flags[0] == 0
    low, high = flags[1].astype(F32), flags[2].astype(F32)
    for i in range(HALO):
        v_ref[i] = jnp.where(first, out[0, i], sib[0, i]) * low
        v_ref[EXT - HALO + i] = jnp.where(first, sib[1, i], out[1, i]) * high
        k_ref[i] = jnp.where(first, out[0, 7 + i], sib[0, 7 + i]) * low
        k_ref[EXT - HALO + i] = jnp.where(first, sib[1, 7 + i], out[1, 7 + i]) * high
    for i in range(ROWS):
        v_ref[HALO + i] = it[i]
        k_ref[HALO + i] = conduct(lab[i])
    z, lane = iota((NZ, LANES), 0), iota((NZ, LANES), 1)
    zero = jnp.zeros((NZ, LANES), F32)
    r_ref[0] = zero
    r_ref[EXT - 1] = zero
    before = flux(k_ref[0], k_ref[1], v_ref[0], v_ref[1])
    for i in range(1, EXT - 1):
        k, v = k_ref[i], v_ref[i]
        if i < HALO:
            s = jnp.where(first, out[0, 3 + i], sib[0, 3 + i]) * low
        elif i < HALO + ROWS:
            s = src[i - HALO]
        else:
            j = 4 + i - HALO - ROWS
            s = jnp.where(first, sib[1, j], out[1, j]) * high
        after = flux(k, k_ref[i + 1], v, v_ref[i + 1])
        fy = jnp.where(lane < LANES - 1, flux(k, roll(k, -1, 1), v, roll(v, -1, 1)), 0.0)
        k_z = jnp.where(z < NZ - 1, roll(k, -1, 0), 0.0)
        v_z = jnp.where(z < NZ - 1, roll(v, -1, 0), 0.0)
        fz = flux(k, k_z, v, v_z)
        fz_in = jnp.where(z > 0, roll(fz, 1, 0), -0.5 * k * v)
        r = s - after + before - fy + roll(fy, 1, 1) - fz + fz_in
        r_ref[i] = r
        before = after
        if HALO <= i < HALO + ROWS:
            j = (i - HALO) // 2
            if i % 2 == 0:
                r_even, k_even = r, k
            else:
                pool[0, j] = r_even + r
                pool[1, j] = k_even + k
    tops = pool[:, :, pl.ds(0, CZ, stride=2), :] + pool[:, :, pl.ds(1, CZ, stride=2), :]
    child, parent = iota((LANES, LANES), 0) // 2, iota((LANES, LANES), 1)
    to_left = jnp.where(child == parent, F32(1.0), F32(0.0))
    to_right = jnp.where(child == parent - CLANES, F32(0.125), F32(0.0))
    coarse = dot(tops[0].reshape(CROWS * CZ, LANES), to_left) + dot(tops[1].reshape(CROWS * CZ, LANES), to_right)
    coarse = coarse.reshape(CROWS, CZ, LANES)
    c_ref[...] = coarse

    for t in range(2):
        up, dn = zero, zero
        for i in range(16 * t, min(16 * t + 16, EXT)):
            k, v, r = k_ref[i], v_ref[i], r_ref[i]
            off = (i % 16) * 8
            here = (lane >= off) & (lane < off + 8)
            top = jnp.where(lane >= 124, k, jnp.where(lane >= 121, roll(r, -4, 1), roll(v, -7, 1)))
            bottom = jnp.where(lane < 4, k, jnp.where(lane < 7, roll(r, 4, 1), roll(v, 7, 1)))
            up = jnp.where(here, roll(top, off - 120, 1), up)
            dn = jnp.where(here, roll(bottom, off, 1), dn)
        up_ref[NZ * t:NZ * (t + 1)] = up
        dn_ref[NZ * t:NZ * (t + 1)] = dn
    lane = iota((CZ, LANES), 1)
    for t in range(2):
        up = dn = jnp.zeros((CZ, LANES), F32)
        for j in range(4 * t, 4 * t + 4):
            row = coarse[j]
            off = (j % 4) * 32
            at_r = (lane >= off) & (lane < off + 16)
            at_k = (lane >= off + 16) & (lane < off + 32)
            up = jnp.where(at_r, roll(row, off - 48, 1), jnp.where(at_k, roll(row, off + 16 - 112, 1), up))
            dn = jnp.where(at_r, roll(row, off, 1), jnp.where(at_k, roll(row, off + 16 - 64, 1), dn))
        up_ref[2 * NZ + CZ * t:2 * NZ + CZ * (t + 1)] = up
        dn_ref[2 * NZ + CZ * t:2 * NZ + CZ * (t + 1)] = dn


def strip_flux(up, dn):
    lane = iota(up.shape, 1)
    face = flux(roll(up, -7, 1), dn, up, roll(dn, -7, 1))
    return jnp.where(lane % 8 == 0, face, 0.0)


def coarse_kernel(c_ref, ou, od, ru, rd, o_ref, pool):
    for n, (a, b) in enumerate(((ou, rd), (ru, od))):
        face = strip_flux(a[0:2 * NZ], b[0:2 * NZ])
        pool[n] = face + roll(face, -8, 1)
    sums = pool[:, pl.ds(0, NZ, stride=2), :] + pool[:, pl.ds(1, NZ, stride=2), :]
    lane = iota((CZ, LANES), 1)
    for j in range(CROWS):
        e = HALO + 2 * j
        rows = slice(CZ * (e // 16), CZ * (e // 16) + CZ)
        src = (e % 16) * 8
        right, left = sums[0, rows], sums[1, rows]
        own = c_ref[j]
        strip = slice(2 * NZ + CZ * (j // 4), 2 * NZ + CZ * (j // 4) + CZ)
        off = (j % 4) * 32
        up, dn = ru[strip], rd[strip]
        for n in range(2):
            value = jnp.where(lane < 64, roll(own, -64 * n, 1), 0.0)
            value = jnp.where((lane >= 64) & (lane < 80), roll(dn, 64 - off - 16 * n, 1), value)
            value = jnp.where(lane >= 112, roll(up, 112 - off - 16 * n, 1), value)
            if n == 0:
                value = value - jnp.where(lane == 63, roll(right, 63 - src, 1), 0.0)
                value = value + jnp.where(lane == 64, roll(right, 64 - src, 1), 0.0)
                value = value - jnp.where(lane == 127, roll(left, 127 - src, 1), 0.0)
                value = value + jnp.where(lane == 0, roll(left, -src, 1), 0.0)
            o_ref[n, j] = value


def coarse_solve_kernel(flags, pair, out, relay, o_ref, k_s, r_s, s_s, x_s, c_s):
    first = flags[0] == 0
    low, high = flags[3].astype(F32), flags[4].astype(F32)
    for n, dest in enumerate((r_s, k_s)):
        for j in range(CROWS):
            dest[j] = jnp.where(first, out[0, 0, n, j], relay[0, n, j]) * low
            dest[8 + j] = jnp.where(first, out[0, 1, n, j] * low, pair[0, n, j])
            dest[16 + j] = jnp.where(first, pair[0, n, j], pair[1, n, j])
            dest[24 + j] = jnp.where(first, pair[1, n, j], out[1, 0, n, j] * high)
            dest[32 + j] = jnp.where(first, relay[1, n, j], out[1, 1, n, j]) * high
    z = iota((CZ, LANES), 0)
    start, pairs = weights(COARSE_SWEEPS)
    zero = jnp.zeros((CZ, LANES), F32)
    s_s[0] = zero
    s_s[CEXT - 1] = zero
    below = 2.0 * (k_s[0] + k_s[1])
    for i in range(1, CEXT - 1):
        k = k_s[i]
        above = 2.0 * (k + k_s[i + 1])
        z_up = 2.0 * (k + jnp.where(z < CZ - 1, roll(k, -1, 0), 0.0))
        z_dn = 2.0 * (k + jnp.where(z > 0, roll(k, 1, 0), 0.0))
        y_up = 2.0 * (k + roll(k, -1, 1))
        y_dn = 2.0 * (k + roll(k, 1, 1))
        diagonal = above + below + z_up + z_dn + y_up + y_dn
        inverse = jnp.where(k > 0, 1.0 / jnp.where(k > 0, diagonal, 1.0), 0.0)
        c_s[0, i] = inverse * above
        c_s[1, i] = inverse * below
        c_s[2, i] = jnp.where(z < CZ - 1, inverse * z_up, 0.0)
        c_s[3, i] = jnp.where(z > 0, inverse * z_dn, 0.0)
        c_s[4, i] = inverse * y_up
        c_s[5, i] = inverse * y_dn
        r = inverse * r_s[i]
        r_s[i] = r
        s_s[i] = r * start
        if 16 <= i < 24:
            x_s[i - 16] = r * start
        below = above
    for n in range(1, COARSE_SWEEPS):
        keep, add = pairs[n - 1]
        prev, here = s_s[n], s_s[n + 1]
        for i in range(n + 1, CEXT - 1 - n):
            ahead = s_s[i + 1]
            total = c_s[0, i] * ahead + c_s[1, i] * prev
            total = total + c_s[2, i] * roll(here, -1, 0) + c_s[3, i] * roll(here, 1, 0)
            total = total + c_s[4, i] * roll(here, -1, 1) + c_s[5, i] * roll(here, 1, 1)
            r = r_s[i] - (here - total)
            step = keep * here + add * r
            r_s[i] = r
            s_s[i] = step
            if 16 <= i < 24:
                x_s[i - 16] = x_s[i - 16] + step
            prev, here = here, ahead
    o_ref[...] = x_s[...]


def fine_kernel(it, r_ref, k_ref, ou, od, ru, rd, x_ref, o_ref, k_s, r_s, s_s, x_s, c_s, p_s):
    lane = iota((NZ, LANES), 1)
    right = strip_flux(ou[0:2 * NZ], rd[0:2 * NZ])
    left = strip_flux(ru[0:2 * NZ], od[0:2 * NZ])
    dn = rd[0:2 * NZ] + roll(right, 4, 1)
    up = ru[0:2 * NZ] - roll(left, 3, 1)
    for i in range(EXT):
        t = slice(NZ * (i // 16), NZ * (i // 16) + NZ)
        off = (i % 16) * 8
        k_s[i, :, 0:LANES] = k_ref[i]
        k_s[i, :, LANES:] = jnp.where(lane < 4, roll(dn[t], -off, 1), jnp.where(lane >= 124, roll(up[t], 120 - off, 1), 0.0))
        r = r_ref[i] - jnp.where(lane == 127, roll(right[t], 127 - off, 1), 0.0)
        r_s[i, :, 0:LANES] = r + jnp.where(lane == 0, roll(left[t], -off, 1), 0.0)
        r_s[i, :, LANES:] = jnp.where(
            lane < 3, roll(dn[t], -off - 4, 1), jnp.where(lane >= 125, roll(up[t], 124 - off, 1), 0.0)
        )
    z = iota((NZ, 2 * LANES), 0)
    start, pairs = weights(SWEEPS)
    zero = jnp.zeros((NZ, 2 * LANES), F32)
    s_s[0] = zero
    s_s[EXT - 1] = zero
    below = 0.5 * (k_s[0] + k_s[1])
    for i in range(1, EXT - 1):
        k = k_s[i]
        above = 0.5 * (k + k_s[i + 1])
        z_up = 0.5 * (k + jnp.where(z < NZ - 1, roll(k, -1, 0), 0.0))
        z_dn = 0.5 * (k + jnp.where(z > 0, roll(k, 1, 0), 0.0))
        y_up = 0.5 * (k + roll(k, -1, 1))
        y_dn = 0.5 * (k + roll(k, 1, 1))
        diagonal = above + below + z_up + z_dn + y_up + y_dn
        inverse = jnp.where(k > 0, 1.0 / jnp.where(k > 0, diagonal, 1.0), 0.0)
        c_s[0, i] = inverse * above
        c_s[1, i] = inverse * below
        c_s[2, i] = jnp.where(z < NZ - 1, inverse * z_up, 0.0)
        c_s[3, i] = jnp.where(z > 0, inverse * z_dn, 0.0)
        c_s[4, i] = inverse * y_up
        c_s[5, i] = inverse * y_dn
        r = inverse * r_s[i]
        r_s[i] = r
        s_s[i] = r * start
        if HALO <= i < HALO + ROWS:
            x_s[i - HALO] = r[:, 0:LANES] * start
        below = above
    for n in range(1, SWEEPS):
        keep, add = pairs[n - 1]
        prev, here = s_s[n], s_s[n + 1]
        for i in range(n + 1, EXT - 1 - n):
            ahead = s_s[i + 1]
            total = c_s[0, i] * ahead + c_s[1, i] * prev
            total = total + c_s[2, i] * roll(here, -1, 0) + c_s[3, i] * roll(here, 1, 0)
            total = total + c_s[4, i] * roll(here, -1, 1) + c_s[5, i] * roll(here, 1, 1)
            r = r_s[i] - (here - total)
            step = keep * here + add * r
            r_s[i] = r
            s_s[i] = step
            if HALO <= i < HALO + ROWS:
                x_s[i - HALO] = x_s[i - HALO] + step[:, 0:LANES]
            prev, here = here, ahead
    child, parent = iota((LANES, LANES), 1) // 2, iota((LANES, LANES), 0)
    spread = jnp.where(child == parent, F32(1.0), F32(0.0))
    wide = dot(x_ref[...].reshape(CROWS * CZ, LANES), spread).reshape(CROWS, CZ, LANES)
    p_s[:, pl.ds(0, CZ, stride=2), :] = wide
    p_s[:, pl.ds(1, CZ, stride=2), :] = wide
    for i in range(ROWS):
        o_ref[i] = it[i] + x_s[i] + p_s[i // 2]


def call(kernel, outs, scratch, in_smem=False, operands=(), flops=1000000):
    vmem = pl.BlockSpec(memory_space=pltpu.VMEM)
    specs = [vmem] * len(operands)
    if in_smem:
        specs[0] = pl.BlockSpec(memory_space=pltpu.SMEM)
    size = sum(4 * x.size for x in operands) + sum(4 * o.size for o in outs)
    multiple = len(outs) > 1
    return pl.pallas_call(
        kernel,
        out_shape=outs if multiple else outs[0],
        in_specs=specs,
        out_specs=[vmem] * len(outs) if multiple else vmem,
        scratch_shapes=[pltpu.VMEM(s, F32) for s in scratch],
        compiler_params=pltpu.CompilerParams(vmem_limit_bytes=40 * 1024 * 1024),
        cost_estimate=pl.CostEstimate(flops=flops, bytes_accessed=size, transcendentals=0),
    )(*operands)


def shape(*dims):
    return jax.ShapeDtypeStruct(dims, F32)


def on_device(iterate, source, labels):
    n_gx, n_gy = lax.axis_size("gx"), lax.axis_size("gy")
    gx = lax.axis_index("gx")
    first = gx % 2 == 0
    flags = jnp.stack([gx % 2, gx > 0, gx < n_gx - 1, gx > 1, gx < n_gx - 2]).astype(jnp.int32)
    chips = [[i, i + 1] for i in range(0, n_gx, 2)]
    between = [[i, (i + 1) % n_gx] for i in range(1, n_gx, 2)]

    lower = jnp.concatenate([iterate[:4], source[:3], conduct(labels[:4])])
    upper = jnp.concatenate([iterate[-4:], source[-3:], conduct(labels[-4:])])
    sib = lax.all_gather(jnp.where(first, upper, lower), "gx", axis_index_groups=chips)
    out = lax.all_gather(jnp.where(first, lower, upper), "gx", axis_index_groups=between)
    full = shape(EXT, NZ, LANES)
    strip = shape(2 * NZ + 2 * CZ, LANES)
    resid, cond, _, coarse, up, dn = call(
        residual_kernel,
        [full, full, full, shape(CROWS, CZ, LANES), strip, strip],
        [(2, CROWS, NZ, LANES)],
        True,
        (flags, iterate, source, labels, sib, out),
    )
    onward = [(i, i + 1) for i in range(n_gy - 1)]
    back = [(i + 1, i) for i in range(n_gy - 1)]
    from_left = lax.ppermute(up, "gy", onward)
    from_right = lax.ppermute(dn, "gy", back)
    block = call(
        coarse_kernel,
        [shape(2, CROWS, CZ, LANES)],
        [(2, 2 * NZ, LANES)],
        False,
        (coarse, up, dn, from_left, from_right),
    )
    pair = lax.all_gather(block, "gx", axis_index_groups=chips)
    beyond = lax.all_gather(pair, "gx", axis_index_groups=between)
    near = jnp.where(first, beyond[0, 1], beyond[1, 0])
    relay = lax.all_gather(near, "gx", axis_index_groups=chips)
    rows = (CEXT, CZ, LANES)
    coarse_out = call(
        coarse_solve_kernel,
        [shape(CROWS, CZ, LANES)],
        [rows, rows, rows, (CROWS, CZ, LANES), (6, *rows)],
        True,
        (flags, pair, beyond, relay),
    )
    owned = lax.all_to_all(coarse_out[:, :, :CLANES], "gy", split_axis=1, concat_axis=2, tiled=True)
    wide = (EXT, NZ, 2 * LANES)
    corrected = call(
        fine_kernel,
        [shape(ROWS, NZ, LANES)],
        [wide, wide, wide, (ROWS, NZ, LANES), (6, *wide), (CROWS, NZ, LANES)],
        False,
        (iterate, resid, cond, up, dn, from_left, from_right, coarse_out),
        flops=20000000,
    )
    return corrected, owned


def solution(mesh):
    spec = P("gx", None, "gy")
    return jax.shard_map(
        on_device, mesh=mesh, in_specs=(spec, spec, spec), out_specs=(spec, P("gx", "gy", None)), check_vma=False
    )
```

time: 506 us -> 75.9 us (0.15)
  the two profiles are of different devices: /device:TPU:2 before, /device:TPU:1 now
where the time goes in v1:
time: 75.9 us; the launch traced here: 75.5 us
  blocking collectives  32.7 us (43%)
  starting transfers between devices  14.5 us (19%)
  waiting for transfers between devices  11.5 us (15%)
  Pallas kernels  11.4 us (15%)
  local copies, waits for them, and re-layouts  2.99 us (4%)
  other arithmetic  1.74 us (2%)
    all_to_all x1, starting transfers between devices, on_device(): lax.all_to_all(coarse_out[:, :, :CLANES], 'gy', split_axis=1, concat_axis...  11.9 us
    pallas_call x4, Pallas kernels, call(): pl.pallas_call(kernel, out_shape=outs if multiple else outs[0], in_specs=...  11.4 us
    all_gather x1, blocking collectives, on_device(): lax.all_gather(jnp.where(first, upper, lower), 'gx', axis_index_groups=ch...  8.71 us
    all_to_all x1, waiting for transfers between devices, on_device(): lax.all_to_all(coarse_out[:, :, :CLANES], 'gy', split_axis=1, concat_axis...  7.93 us
    all_gather x1, blocking collectives, on_device(): beyond = lax.all_gather(pair, 'gx', axis_index_groups=between)  6.76 us
    all_gather x1, blocking collectives, on_device(): pair = lax.all_gather(block, 'gx', axis_index_groups=chips)  6.18 us
    all_gather x1, blocking collectives, on_device(): lax.all_gather(jnp.where(first, lower, upper), 'gx', axis_index_groups=be...  6.01 us
    all_gather x1, blocking collectives, on_device(): relay = lax.all_gather(near, 'gx', axis_index_groups=chips)  5.02 us
  transfers between devices with their start and end apart: 3, of which 2 were waited for; matrix products, arithmetic and copies ran while one was open for 0% of the time, Pallas kernels for 5%

profile of v1, /device:TPU:1, one launch (start us, length us, event | category | flops | bytes accessed | tf_op | source)
XLA Modules:
  0.0 75.5 jit_solution(3905058600940481876)
XLA Ops:
  0.6 0.8 %slice_bitcast_fusion.3 = (f32[1,3,32,128]{3,2,1,0:T(8,128)S(1)}, f32[1,3,32,128]{3,2,1,0:T(8,128)S(1)}) fusion(f32[16,32,128]{2,1,0:T(8,128)} %src.1), kind=kLoop, calls=%fused_computation.10 | loop fusion | bytes 196608 | tf_op jit(solution)/shard_map/concatenate | solution.py:321
  1.5 1.0 %select_bitcast_fusion.1 = (f32[1,4,32,128]{3,2,1,0:T(8,128)S(1)}, f32[1,4,32,128]{3,2,1,0:T(8,128)S(1)}, f32[1,4,32,128]{3,2,1,0:T(8,128)S(1)}, f32[1,4,32,128]{3,2,1,0:T(8,128)S(1)}) fusion(s32[16,32,128]{2,1,0:T(8,128)} %lab.1, f32[16,32,128]{2,1,0:T(8,128)} %it.3), kind=kLoop, calls=%fused_computation.7 | loop fusion | flops 262144 | bytes 524288 | tf_op jit(solution)/shard_map/concatenate | solution.py:321
  2.5 0.0 copy-start.2
  2.5 8.7 %all_gather.24.sib = f32[2,11,32,128]{3,2,1,0:T(8,128)S(1)} all-gather(f32[1,11,32,128]{3,2,1,0:T(8,128)S(1)} %get-tuple-element.19), channel_id=1, replica_groups={{0,16},{32,48},{64,80},{96,112},{128,144},{160,176},{192,208},{224,240}..., dimensions={0}, use_global_device_ids=true | all-gather | bytes 540672 | tf_op jit(solution)/shard_map/all_gather | solution.py:322
  11.2 0.0 copy-start
  11.2 0.0 copy-start.1
  11.2 6.0 %all_gather.25.out = f32[2,11,32,128]{3,2,1,0:T(8,128)S(1)} all-gather(f32[1,11,32,128]{3,2,1,0:T(8,128)S(1)} %get-tuple-element.18), channel_id=1, replica_groups={{16,32},{48,64},{80,96},{112,128},{144,160},{176,192},{208,224},{240,25..., dimensions={0}, use_global_device_ids=true | all-gather | bytes 540672 | tf_op jit(solution)/shard_map/all_gather | solution.py:323
  17.2 0.1 stack.39.flags
  17.3 0.0 copy-done.2
  17.3 0.0 copy-done
  17.3 0.0 copy-done.1
  17.3 4.6 %shard_map.50 = (f32[24,32,128]{2,1,0:T(8,128)S(1)}, f32[24,32,128]{2,1,0:T(8,128)S(1)}, f32[24,32,128]{2,1,0:T(8,128)}, f32[8,16,128]{2,1,0:T(8,128)S(1)}, f32[...) custom-call(s32[5]{0:T(128)S(1)} %stack.39.flags, f32[16,32,128]{2,1,0:T(8,128)S(1)} %copy-done, f32[16,32,128]{2,1,0:T(8,128)S(1)} %copy-done.2, ...), custom_call_target="tpu_custom_call" | custom-call | flops 1000000 | bytes 2850836 | tf_op jit(solution)/shard_map/pallas_call | solution.py:297
  21.9 1.3 %collective-permute-start = (f32[96,128]{1,0:T(8,128)S(1)}, f32[96,128]{1,0:T(8,128)S(1)}, u32[]{:S(2)}, u32[]{:S(2)}) collective-permute-start(f32[96,128]{1,0:T(8,128)S(1)} %get-tuple-element.9.ou), channel_id=1, source_target_pairs={{0,1},{1,2},{2,3},{3,4},{4,5},{5,6},{6,7},{7,8},{8,9},{9,10},{10,1... | collective-permute-start | bytes 147464 | tf_op jit(solution)/shard_map/ppermute | solution.py:335
  23.2 1.3 %collective-permute-start.1 = (f32[96,128]{1,0:T(8,128)S(1)}, f32[96,128]{1,0:T(8,128)S(1)}, u32[]{:S(2)}, u32[]{:S(2)}) collective-permute-start(f32[96,128]{1,0:T(8,128)S(1)} %get-tuple-element.10.od), channel_id=1, source_target_pairs={{1,0},{2,1},{3,2},{4,3},{5,4},{6,5},{7,6},{8,7},{9,8},{10,9},{11,1... | collective-permute-start | bytes 147464 | tf_op jit(solution)/shard_map/ppermute | solution.py:336
  24.5 0.0 collective-permute-done.ru
  24.5 3.5 %collective-permute-done.1.rd = f32[96,128]{1,0:T(8,128)S(1)} collective-permute-done((f32[96,128]{1,0:T(8,128)S(1)}, f32[96,128]{1,0:T(8,128)S(1)}, u32[]{:S(2)}, u32[]{:S(2)}) %collective-permute-start.1) | collective-permute-done | bytes 49184 | tf_op jit(solution)/shard_map/ppermute | solution.py:336
  28.1 0.3 shard_map.51
  28.4 6.2 %all-gather = f32[4,8,16,128]{3,2,1,0:T(8,128)S(1)} all-gather(f32[2,8,16,128]{3,2,1,0:T(8,128)S(1)} %shard_map.51), channel_id=2, replica_groups={{0,16},{32,48},{64,80},{96,112},{128,144},{160,176},{192,208},{224,240}..., dimensions={0}, use_global_device_ids=true | all-gather | bytes 393216 | tf_op jit(solution)/shard_map/all_gather | solution.py:344
  34.6 6.8 %all-gather.1 = f32[4,2,8,16,128]{4,3,2,1,0:T(8,128)S(1)} all-gather(f32[2,2,8,16,128]{4,3,2,1,0:T(8,128)S(1)} %bitcast.27), channel_id=3, replica_groups={{16,32},{48,64},{80,96},{112,128},{144,160},{176,192},{208,224},{240,25..., dimensions={0}, use_global_device_ids=true | all-gather | bytes 786432 | tf_op jit(solution)/shard_map/all_gather | solution.py:345
  41.3 5.0 %all-gather.2 = f32[2,1,2,8,16,128]{5,4,3,2,1,0:T(8,128)S(1)} all-gather(f32[1,1,2,8,16,128]{5,4,3,2,1,0:T(8,128)S(1)} %slice_select_fusion), channel_id=4, replica_groups={{0,16},{32,48},{64,80},{96,112},{128,144},{160,176},{192,208},{224,240}..., dimensions={0}, use_global_device_ids=true | all-gather | bytes 393216 | tf_op jit(solution)/shard_map/all_gather | solution.py:347
  46.4 2.9 %shard_map.52.x_ref = f32[8,16,128]{2,1,0:T(8,128)S(1)} custom-call(s32[5]{0:T(128)S(1)} %stack.39.flags, f32[2,2,8,16,128]{4,3,2,1,0:T(8,128)S(1)} %bitcast.28, f32[2,2,2,8,16,128]{5,4,3,2,1,0:T(8,128)S(1)} %bitcast.26, f32[2,2,8,16,128]{4,3,2,1,0:T(8,128)S(1)} %bitcast.29), custom_call_target="tpu_custom_call" | custom-call | flops 1000000 | bytes 1114132 | tf_op jit(solution)/shard_map/pallas_call | solution.py:297
  49.3 0.7 reshape.195
  50.1 11.9 %all-to-all-start = ((f32[16,1,512]{2,1,0:T(1,128)}), f32[16,1,512]{2,1,0:T(1,128)S(1)}, u32[]{:S(2)}, u32[]{:S(2)}) async-start(f32[16,1,512]{2,1,0:T(1,128)} %reshape.195), calls=%async_computation | async-start | bytes 65536 | tf_op jit(solution)/shard_map/all_to_all | solution.py:356
  62.0 3.5 %shard_map.53 = f32[16,32,128]{2,1,0:T(8,128)} custom-call(f32[16,32,128]{2,1,0:T(8,128)S(1)} %copy-done, f32[24,32,128]{2,1,0:T(8,128)S(1)} %get-tuple-element.7.r_ref, f32[24,32,128]{2,1,0:T(8,128)S(1)} %get-tuple-element.8.k_ref, f32[96,128]{1,0:T(8,128)S(1)} %get-tuple-element.9.ou, f32[96,128]{1,0:T(8,128)S(1)} %get-tuple-element.10.od, ...), custom_call_target="tpu_custom_call" | custom-call | flops 20000000 | bytes 1572864 | tf_op jit(solution)/shard_map/pallas_call | solution.py:297
  65.5 7.9 %all-to-all-done = f32[16,1,512]{2,1,0:T(1,128)S(1)} async-done(((f32[16,1,512]{2,1,0:T(1,128)}), f32[16,1,512]{2,1,0:T(1,128)S(1)}, u32[]{:S(2)}, u32[]{:S(2)}) %all-to-all-start) | async-done | bytes 32800 | tf_op jit(solution)/shard_map/all_to_all | solution.py:356
  73.5 0.5 broadcast.54
  74.0 0.7 reduce
  74.7 0.1 reshape.196
  74.8 0.7 all_to_all.11
  (4 shorter events, 0.1 us)
Async XLA Ops:
  2.5 14.8 %copy-start.2 = (f32[16,32,128]{2,1,0:T(8,128)S(1)}, f32[16,32,128]{2,1,0:T(8,128)}, u32[]{:S(2)}) copy-start(f32[16,32,128]{2,1,0:T(8,128)} %src.1) | copy-start | bytes 786436
  11.2 6.1 %copy-start = (f32[16,32,128]{2,1,0:T(8,128)S(1)}, f32[16,32,128]{2,1,0:T(8,128)}, u32[]{:S(2)}) copy-start(f32[16,32,128]{2,1,0:T(8,128)} %it.3) | copy-start | bytes 786436
  11.2 6.1 %copy-start.1 = (s32[16,32,128]{2,1,0:T(8,128)S(1)}, s32[16,32,128]{2,1,0:T(8,128)}, u32[]{:S(2)}) copy-start(s32[16,32,128]{2,1,0:T(8,128)} %lab.1) | copy-start | bytes 786436
  21.9 2.6 %collective-permute-start = (f32[96,128]{1,0:T(8,128)S(1)}, f32[96,128]{1,0:T(8,128)S(1)}, u32[]{:S(2)}, u32[]{:S(2)}) collective-permute-start(f32[96,128]{1,0:T(8,128)S(1)} %get-tuple-element.9.ou), channel_id=1, source_target_pairs={{0,1},{1,2},{2,3},{3,4},{4,5},{5,6},{6,7},{7,8},{8,9},{9,10},{10,1... | collective-permute-start | bytes 147464 | tf_op jit(solution)/shard_map/ppermute | solution.py:335
  23.2 4.8 %collective-permute-start.1 = (f32[96,128]{1,0:T(8,128)S(1)}, f32[96,128]{1,0:T(8,128)S(1)}, u32[]{:S(2)}, u32[]{:S(2)}) collective-permute-start(f32[96,128]{1,0:T(8,128)S(1)} %get-tuple-element.10.od), channel_id=1, source_target_pairs={{1,0},{2,1},{3,2},{4,3},{5,4},{6,5},{7,6},{8,7},{9,8},{10,9},{11,1... | collective-permute-start | bytes 147464 | tf_op jit(solution)/shard_map/ppermute | solution.py:336
  50.1 23.4 %all-to-all-start = ((f32[16,1,512]{2,1,0:T(1,128)}), f32[16,1,512]{2,1,0:T(1,128)S(1)}, u32[]{:S(2)}, u32[]{:S(2)}) async-start(f32[16,1,512]{2,1,0:T(1,128)} %reshape.195), calls=%async_computation | async-start | bytes 65536 | tf_op jit(solution)/shard_map/all_to_all | solution.py:356

commit v2 on v1

--- a/solution.py
+++ b/solution.py
@@ -1,3 +1,5 @@
+import functools
+
 import jax
 import jax.numpy as jnp
 from jax import lax
@@ -165,7 +167,7 @@
             o_ref[n, j] = value
 
 
-def coarse_solve_kernel(flags, pair, out, relay, o_ref, k_s, r_s, s_s, x_s, c_s):
+def coarse_solve_kernel(flags, pair, out, relay, o_ref, p_ref, k_s, r_s, s_s, x_s, c_s):
     first = flags[0] == 0
     low, high = flags[3].astype(F32), flags[4].astype(F32)
     for n, dest in enumerate((r_s, k_s)):
@@ -218,6 +220,22 @@
                 x_s[i - 16] = x_s[i - 16] + step
             prev, here = here, ahead
     o_ref[...] = x_s[...]
+    lane = iota((CZ, LANES), 1)
+    for a in range(4):
+        p_ref[pl.ds(a, CZ, stride=4), :] = jnp.where(lane < CLANES, x_s[a], roll(x_s[a + 4], CLANES, 1))
+
+
+def planes_kernel(sources, planes, p_ref, o_ref):
+    half = sources // 2
+    lane = iota((half, LANES), 1)
+    for q in range(planes):
+        for a in range(4):
+            even = p_ref[pl.ds(4 * q + a, half, stride=8 * planes), :]
+            odd = p_ref[pl.ds(4 * (planes + q) + a, half, stride=8 * planes), :]
+            to = (a * planes + q) * half
+            o_ref[to:to + half] = jnp.where(lane < CLANES, even, roll(odd, CLANES, 1))
+            to = ((a + 4) * planes + q) * half
+            o_ref[to:to + half] = jnp.where(lane < CLANES, roll(even, CLANES, 1), odd)
 
 
 def fine_kernel(it, r_ref, k_ref, ou, od, ru, rd, x_ref, o_ref, k_s, r_s, s_s, x_s, c_s, p_s):
@@ -346,14 +364,15 @@
     near = jnp.where(first, beyond[0, 1], beyond[1, 0])
     relay = lax.all_gather(near, "gx", axis_index_groups=chips)
     rows = (CEXT, CZ, LANES)
-    coarse_out = call(
+    coarse_out, planes = call(
         coarse_solve_kernel,
-        [shape(CROWS, CZ, LANES)],
+        [shape(CROWS, CZ, LANES), shape(4 * CZ, LANES)],
         [rows, rows, rows, (CROWS, CZ, LANES), (6, *rows)],
         True,
         (flags, pair, beyond, relay),
     )
-    owned = lax.all_to_all(coarse_out[:, :, :CLANES], "gy", split_axis=1, concat_axis=2, tiled=True)
+    per = CZ // n_gy
+    planes = lax.all_to_all(planes.reshape(n_gy, 4 * per, LANES), "gy", split_axis=0, concat_axis=0, tiled=True)
     wide = (EXT, NZ, 2 * LANES)
     corrected = call(
         fine_kernel,
@@ -363,6 +382,13 @@
         (iterate, resid, cond, up, dn, from_left, from_right, coarse_out),
         flops=20000000,
     )
+    owned = call(
+        functools.partial(planes_kernel, n_gy, per),
+        [shape(4 * CZ, LANES)],
+        [],
+        False,
+        (planes.reshape(4 * CZ, LANES),),
+    ).reshape(CROWS, per, CLANES * n_gy)
     return corrected, owned
 
 

time: 75.9 us -> 74.4 us (0.980)
  local copies, waits for them, and re-layouts: 2.99 us -> 0.93 us
  Pallas kernels: 11.4 us -> 12.7 us
    all_gather x1, blocking collectives: 6.18 us -> 3.15 us  [on_device(): pair = lax.all_gather(block, 'gx', axis_index_groups=chips)]
    all_gather x1, blocking collectives: 8.71 us -> 11.1 us  [on_device(): lax.all_gather(jnp.where(first, upper, lower), 'gx', axis_index_groups=ch...]
    pallas_call x4 -> x5, Pallas kernels: 11.4 us -> 12.7 us  [call(): pl.pallas_call(kernel, out_shape=outs if multiple else outs[0], in_specs=...]
    all_to_all x3 -> x0, local copies, waits for them, and re-layouts: 1.24 us -> none  [on_device(): lax.all_to_all(coarse_out[:, :, :CLANES], 'gy', split_axis=1, concat_axis...]
    unnamed x8 -> x6, local copies, waits for them, and re-layouts: 0.81 us -> 0.01 us
where the time goes in v2:
time: 74.4 us; the launch traced here: 74 us
  blocking collectives  32.7 us (44%)
  starting transfers between devices  14.5 us (19%)
  Pallas kernels  12.7 us (17%)
  waiting for transfers between devices  11.5 us (15%)
  other arithmetic  1.02 us (1%)
  local copies, waits for them, and re-layouts  0.93 us (1%)
    pallas_call x5, Pallas kernels, call(): pl.pallas_call(kernel, out_shape=outs if multiple else outs[0], in_specs=...  12.7 us
    all_to_all x1, starting transfers between devices, on_device(): lax.all_to_all(planes.reshape(n_gy, 4 * per, LANES), 'gy', split_axis=0,...  11.9 us
    all_gather x1, blocking collectives, on_device(): lax.all_gather(jnp.where(first, upper, lower), 'gx', axis_index_groups=ch...  11.1 us
    all_to_all x1, waiting for transfers between devices, on_device(): lax.all_to_all(planes.reshape(n_gy, 4 * per, LANES), 'gy', split_axis=0,...  7.93 us
    all_gather x1, blocking collectives, on_device(): beyond = lax.all_gather(pair, 'gx', axis_index_groups=between)  6.76 us
    all_gather x1, blocking collectives, on_device(): lax.all_gather(jnp.where(first, lower, upper), 'gx', axis_index_groups=be...  6.66 us
    all_gather x1, blocking collectives, on_device(): relay = lax.all_gather(near, 'gx', axis_index_groups=chips)  5.02 us
    ppermute x1, waiting for transfers between devices, on_device(): from_right = lax.ppermute(dn, 'gy', back)  3.52 us
  transfers between devices with their start and end apart: 3, of which 2 were waited for; matrix products, arithmetic and copies ran while one was open for 0% of the time, Pallas kernels for 5%

profile of v2, /device:TPU:1, one launch (start us, length us, event | category | flops | bytes accessed | tf_op | source)
XLA Modules:
  0.0 74.0 jit_solution(15089573441146047949)
XLA Ops:
  0.7 0.8 %slice_bitcast_fusion.3 = (f32[1,3,32,128]{3,2,1,0:T(8,128)S(1)}, f32[1,3,32,128]{3,2,1,0:T(8,128)S(1)}) fusion(f32[16,32,128]{2,1,0:T(8,128)} %src.1), kind=kLoop, calls=%fused_computation.10 | loop fusion | bytes 196608 | tf_op jit(solution)/shard_map/concatenate | solution.py:339
  1.5 1.0 %select_bitcast_fusion.1 = (f32[1,4,32,128]{3,2,1,0:T(8,128)S(1)}, f32[1,4,32,128]{3,2,1,0:T(8,128)S(1)}, f32[1,4,32,128]{3,2,1,0:T(8,128)S(1)}, f32[1,4,32,128]{3,2,1,0:T(8,128)S(1)}) fusion(s32[16,32,128]{2,1,0:T(8,128)} %lab.1, f32[16,32,128]{2,1,0:T(8,128)} %it.3), kind=kLoop, calls=%fused_computation.7 | loop fusion | flops 262144 | bytes 524288 | tf_op jit(solution)/shard_map/concatenate | solution.py:339
  2.5 0.0 copy-start.2
  2.5 6.7 %all_gather.25.out = f32[2,11,32,128]{3,2,1,0:T(8,128)S(1)} all-gather(f32[1,11,32,128]{3,2,1,0:T(8,128)S(1)} %get-tuple-element.22), channel_id=1, replica_groups={{16,32},{48,64},{80,96},{112,128},{144,160},{176,192},{208,224},{240,25..., dimensions={0}, use_global_device_ids=true | all-gather | bytes 540672 | tf_op jit(solution)/shard_map/all_gather | solution.py:341
  9.2 0.0 copy-start
  9.2 0.0 copy-start.1
  9.2 11.1 %all_gather.24.sib = f32[2,11,32,128]{3,2,1,0:T(8,128)S(1)} all-gather(f32[1,11,32,128]{3,2,1,0:T(8,128)S(1)} %get-tuple-element.23), channel_id=1, replica_groups={{0,16},{32,48},{64,80},{96,112},{128,144},{160,176},{192,208},{224,240}..., dimensions={0}, use_global_device_ids=true | all-gather | bytes 540672 | tf_op jit(solution)/shard_map/all_gather | solution.py:340
  20.3 0.1 stack.39.flags
  20.3 0.0 copy-done.2
  20.3 0.0 copy-done
  20.3 0.0 copy-done.1
  20.4 4.6 %shard_map.50 = (f32[24,32,128]{2,1,0:T(8,128)S(1)}, f32[24,32,128]{2,1,0:T(8,128)S(1)}, f32[24,32,128]{2,1,0:T(8,128)}, f32[8,16,128]{2,1,0:T(8,128)S(1)}, f32[...) custom-call(s32[5]{0:T(128)S(1)} %stack.39.flags, f32[16,32,128]{2,1,0:T(8,128)S(1)} %copy-done, f32[16,32,128]{2,1,0:T(8,128)S(1)} %copy-done.2, ...), custom_call_target="tpu_custom_call" | custom-call | flops 1000000 | bytes 2850836 | tf_op jit(solution)/shard_map/pallas_call | solution.py:315
  25.0 1.3 %collective-permute-start = (f32[96,128]{1,0:T(8,128)S(1)}, f32[96,128]{1,0:T(8,128)S(1)}, u32[]{:S(2)}, u32[]{:S(2)}) collective-permute-start(f32[96,128]{1,0:T(8,128)S(1)} %get-tuple-element.11.ou), channel_id=1, source_target_pairs={{0,1},{1,2},{2,3},{3,4},{4,5},{5,6},{6,7},{7,8},{8,9},{9,10},{10,1... | collective-permute-start | bytes 147464 | tf_op jit(solution)/shard_map/ppermute | solution.py:353
  26.3 1.3 %collective-permute-start.1 = (f32[96,128]{1,0:T(8,128)S(1)}, f32[96,128]{1,0:T(8,128)S(1)}, u32[]{:S(2)}, u32[]{:S(2)}) collective-permute-start(f32[96,128]{1,0:T(8,128)S(1)} %get-tuple-element.12.od), channel_id=1, source_target_pairs={{1,0},{2,1},{3,2},{4,3},{5,4},{6,5},{7,6},{8,7},{9,8},{10,9},{11,1... | collective-permute-start | bytes 147464 | tf_op jit(solution)/shard_map/ppermute | solution.py:354
  27.6 0.0 collective-permute-done.ru
  27.6 3.5 %collective-permute-done.1.rd = f32[96,128]{1,0:T(8,128)S(1)} collective-permute-done((f32[96,128]{1,0:T(8,128)S(1)}, f32[96,128]{1,0:T(8,128)S(1)}, u32[]{:S(2)}, u32[]{:S(2)}) %collective-permute-start.1) | collective-permute-done | bytes 49184 | tf_op jit(solution)/shard_map/ppermute | solution.py:354
  31.1 0.3 shard_map.51
  31.4 3.2 %all-gather = f32[4,8,16,128]{3,2,1,0:T(8,128)S(1)} all-gather(f32[2,8,16,128]{3,2,1,0:T(8,128)S(1)} %shard_map.51), channel_id=2, replica_groups={{0,16},{32,48},{64,80},{96,112},{128,144},{160,176},{192,208},{224,240}..., dimensions={0}, use_global_device_ids=true | all-gather | bytes 393216 | tf_op jit(solution)/shard_map/all_gather | solution.py:362
  34.6 6.8 %all-gather.1 = f32[4,2,8,16,128]{4,3,2,1,0:T(8,128)S(1)} all-gather(f32[2,2,8,16,128]{4,3,2,1,0:T(8,128)S(1)} %bitcast.25), channel_id=3, replica_groups={{16,32},{48,64},{80,96},{112,128},{144,160},{176,192},{208,224},{240,25..., dimensions={0}, use_global_device_ids=true | all-gather | bytes 786432 | tf_op jit(solution)/shard_map/all_gather | solution.py:363
  41.3 5.0 %all-gather.2 = f32[2,1,2,8,16,128]{5,4,3,2,1,0:T(8,128)S(1)} all-gather(f32[1,1,2,8,16,128]{5,4,3,2,1,0:T(8,128)S(1)} %slice_select_fusion), channel_id=4, replica_groups={{0,16},{32,48},{64,80},{96,112},{128,144},{160,176},{192,208},{224,240}..., dimensions={0}, use_global_device_ids=true | all-gather | bytes 393216 | tf_op jit(solution)/shard_map/all_gather | solution.py:365
  46.4 3.6 %shard_map.52 = (f32[8,16,128]{2,1,0:T(8,128)S(1)}, f32[64,128]{1,0:T(8,128)}) custom-call(s32[5]{0:T(128)S(1)} %stack.39.flags, f32[2,2,8,16,128]{4,3,2,1,0:T(8,128)S(1)} %bitcast.26, f32[2,2,2,8,16,128]{5,4,3,2,1,0:T(8,128)S(1)} %bitcast.24, f32[2,2,8,16,128]{4,3,2,1,0:T(8,128)S(1)} %bitcast.27), custom_call_target="tpu_custom_call" | custom-call | flops 1000000 | bytes 1146900 | tf_op jit(solution)/shard_map/pallas_call | solution.py:315
  49.9 11.9 %all-to-all-start = ((f32[16,4,128]{2,1,0:T(4,128)}), f32[16,4,128]{2,1,0:T(4,128)S(1)}, u32[]{:S(2)}, u32[]{:S(2)}) async-start(f32[16,4,128]{2,1,0:T(4,128)} %bitcast.14), calls=%async_computation | async-start | bytes 65536 | tf_op jit(solution)/shard_map/all_to_all | solution.py:375
  61.9 3.5 %shard_map.53 = f32[16,32,128]{2,1,0:T(8,128)} custom-call(f32[16,32,128]{2,1,0:T(8,128)S(1)} %copy-done, f32[24,32,128]{2,1,0:T(8,128)S(1)} %get-tuple-element.9.r_ref, f32[24,32,128]{2,1,0:T(8,128)S(1)} %get-tuple-element.10.k_ref, f32[96,128]{1,0:T(8,128)S(1)} %get-tuple-element.11.ou, f32[96,128]{1,0:T(8,128)S(1)} %get-tuple-element.12.od, ...), custom_call_target="tpu_custom_call" | custom-call | flops 20000000 | bytes 1572864 | tf_op jit(solution)/shard_map/pallas_call | solution.py:315
  65.4 7.9 %all-to-all-done = f32[16,4,128]{2,1,0:T(4,128)S(1)} async-done(((f32[16,4,128]{2,1,0:T(4,128)}), f32[16,4,128]{2,1,0:T(4,128)S(1)}, u32[]{:S(2)}, u32[]{:S(2)}) %all-to-all-start) | async-done | bytes 32800 | tf_op jit(solution)/shard_map/all_to_all | solution.py:375
  73.4 0.7 shard_map.54
  (2 shorter events, 0.0 us)
Async XLA Ops:
  2.5 17.8 %copy-start.2 = (f32[16,32,128]{2,1,0:T(8,128)S(1)}, f32[16,32,128]{2,1,0:T(8,128)}, u32[]{:S(2)}) copy-start(f32[16,32,128]{2,1,0:T(8,128)} %src.1) | copy-start | bytes 786436
  9.2 11.2 %copy-start = (f32[16,32,128]{2,1,0:T(8,128)S(1)}, f32[16,32,128]{2,1,0:T(8,128)}, u32[]{:S(2)}) copy-start(f32[16,32,128]{2,1,0:T(8,128)} %it.3) | copy-start | bytes 786436
  9.2 11.2 %copy-start.1 = (s32[16,32,128]{2,1,0:T(8,128)S(1)}, s32[16,32,128]{2,1,0:T(8,128)}, u32[]{:S(2)}) copy-start(s32[16,32,128]{2,1,0:T(8,128)} %lab.1) | copy-start | bytes 786436
  25.0 2.6 %collective-permute-start = (f32[96,128]{1,0:T(8,128)S(1)}, f32[96,128]{1,0:T(8,128)S(1)}, u32[]{:S(2)}, u32[]{:S(2)}) collective-permute-start(f32[96,128]{1,0:T(8,128)S(1)} %get-tuple-element.11.ou), channel_id=1, source_target_pairs={{0,1},{1,2},{2,3},{3,4},{4,5},{5,6},{6,7},{7,8},{8,9},{9,10},{10,1... | collective-permute-start | bytes 147464 | tf_op jit(solution)/shard_map/ppermute | solution.py:353
  26.3 4.8 %collective-permute-start.1 = (f32[96,128]{1,0:T(8,128)S(1)}, f32[96,128]{1,0:T(8,128)S(1)}, u32[]{:S(2)}, u32[]{:S(2)}) collective-permute-start(f32[96,128]{1,0:T(8,128)S(1)} %get-tuple-element.12.od), channel_id=1, source_target_pairs={{1,0},{2,1},{3,2},{4,3},{5,4},{6,5},{7,6},{8,7},{9,8},{10,9},{11,1... | collective-permute-start | bytes 147464 | tf_op jit(solution)/shard_map/ppermute | solution.py:354
  49.9 23.4 %all-to-all-start = ((f32[16,4,128]{2,1,0:T(4,128)}), f32[16,4,128]{2,1,0:T(4,128)S(1)}, u32[]{:S(2)}, u32[]{:S(2)}) async-start(f32[16,4,128]{2,1,0:T(4,128)} %bitcast.14), calls=%async_computation | async-start | bytes 65536 | tf_op jit(solution)/shard_map/all_to_all | solution.py:375

commit v3 on v1

v3 whole, which is shorter than its diff:
```python
import functools

import jax
import jax.numpy as jnp
from jax import lax
from jax.experimental import pallas as pl
from jax.experimental.pallas import tpu as pltpu
from jax.sharding import PartitionSpec as P

SWEEPS = 4
COARSE_SWEEPS = 16
TABLE = (0.5, 1.0, 2.5, 6.0)
LOWER = 0.25
UPPER = 2.0
F32 = jnp.float32

ROWS, NZ, LANES = 16, 32, 128
CROWS, CZ, CLANES = 8, 16, 64
HALO = SWEEPS
EXT = ROWS + 2 * HALO
CEXT = CROWS + 2 * COARSE_SWEEPS
BLOCK = CROWS * CZ


def weights(sweeps):
    centre = (UPPER + LOWER) / 2.0
    radius = (UPPER - LOWER) / 2.0
    sigma = centre / radius
    rho = 1.0 / sigma
    pairs = []
    for _ in range(1, sweeps):
        rho_new = 1.0 / (2.0 * sigma - rho)
        pairs.append((rho_new * rho, 2.0 * rho_new / radius))
        rho = rho_new
    return 1.0 / centre, pairs


def conduct(labels):
    total = jnp.zeros(labels.shape, F32)
    for label_id, value in enumerate(TABLE):
        total = jnp.where(labels == label_id, F32(value), total)
    return total


def roll(x, shift, axis):
    size = x.shape[axis]
    shift = shift % size
    return x if shift == 0 else pltpu.roll(x, shift, axis)


def iota(shape, axis):
    return lax.broadcasted_iota(jnp.int32, shape, axis)


def flux(k_a, k_b, v_a, v_b):
    return 0.5 * (k_a + k_b) * (v_a - v_b)


def dot(a, b):
    return jnp.dot(a, b, precision=lax.Precision.HIGHEST, preferred_element_type=F32)


def residual_kernel(it, src, lab, r_ref, k_ref, c_ref, up_ref, dn_ref, pool):
    for i in range(ROWS):
        k_ref[i] = conduct(lab[i])
    z, lane = iota((NZ, LANES), 0), iota((NZ, LANES), 1)
    zero = jnp.zeros((NZ, LANES), F32)
    before = zero
    up = dn = zero
    for i in range(ROWS):
        k, v = k_ref[i], it[i]
        after = flux(k, k_ref[i + 1], v, it[i + 1]) if i < ROWS - 1 else zero
        fy = jnp.where(lane < LANES - 1, flux(k, roll(k, -1, 1), v, roll(v, -1, 1)), 0.0)
        k_z = jnp.where(z < NZ - 1, roll(k, -1, 0), 0.0)
        v_z = jnp.where(z < NZ - 1, roll(v, -1, 0), 0.0)
        fz = flux(k, k_z, v, v_z)
        fz_in = jnp.where(z > 0, roll(fz, 1, 0), -0.5 * k * v)
        r = src[i] - after + before - fy + roll(fy, 1, 1) - fz + fz_in
        r_ref[i] = r
        before = after
        j = i // 2
        if i % 2 == 0:
            r_even, k_even = r, k
        else:
            pool[0, j] = r_even + r
            pool[1, j] = k_even + k
        off = 8 * i
        here = (lane >= off) & (lane < off + 8)
        top = jnp.where(lane >= 124, k, jnp.where(lane >= 121, roll(r, -4, 1), roll(v, -7, 1)))
        bottom = jnp.where(lane < 4, k, jnp.where(lane < 7, roll(r, 4, 1), roll(v, 7, 1)))
        up = jnp.where(here, roll(top, off - 120, 1), up)
        dn = jnp.where(here, roll(bottom, off, 1), dn)
    up_ref[0:NZ] = up
    dn_ref[0:NZ] = dn
    up = dn = zero
    for g, edge in enumerate((k_ref[0], it[0], k_ref[ROWS - 1], it[ROWS - 1])):
        here = (lane >= 32 * g) & (lane < 32 * g + 32)
        up = jnp.where(here, roll(edge, 32 * g - 96, 1), up)
        dn = jnp.where(here, roll(edge, 32 * g, 1), dn)
    up_ref[NZ:2 * NZ] = up
    dn_ref[NZ:2 * NZ] = dn
    tops = pool[:, :, pl.ds(0, CZ, stride=2), :] + pool[:, :, pl.ds(1, CZ, stride=2), :]
    child, parent = iota((LANES, LANES), 0) // 2, iota((LANES, LANES), 1)
    to_left = jnp.where(child == parent, F32(1.0), F32(0.0))
    to_right = jnp.where(child == parent - CLANES, F32(0.125), F32(0.0))
    coarse = dot(tops[0].reshape(CROWS * CZ, LANES), to_left) + dot(tops[1].reshape(CROWS * CZ, LANES), to_right)
    coarse = coarse.reshape(CROWS, CZ, LANES)
    c_ref[...] = coarse
    lane = iota((CZ, LANES), 1)
    for t in range(2):
        up = dn = jnp.zeros((CZ, LANES), F32)
        for j in range(4 * t, 4 * t + 4):
            row = coarse[j]
            off = (j % 4) * 32
            at_r = (lane >= off) & (lane < off + 16)
            at_k = (lane >= off + 16) & (lane < off + 32)
            up = jnp.where(at_r, roll(row, off - 48, 1), jnp.where(at_k, roll(row, off + 16 - 112, 1), up))
            dn = jnp.where(at_r, roll(row, off, 1), jnp.where(at_k, roll(row, off + 16 - 64, 1), dn))
        up_ref[2 * NZ + CZ * t:2 * NZ + CZ * (t + 1)] = up
        dn_ref[2 * NZ + CZ * t:2 * NZ + CZ * (t + 1)] = dn


def strip_flux(up, dn):
    lane = iota(up.shape, 1)
    face = flux(roll(up, -7, 1), dn, up, roll(dn, -7, 1))
    return jnp.where(lane % 8 == 0, face, 0.0)


def completed(ou, od, ru, rd):
    right = strip_flux(ou[0:NZ], rd[0:NZ])
    left = strip_flux(ru[0:NZ], od[0:NZ])
    return rd[0:NZ] + roll(right, 4, 1), ru[0:NZ] - roll(left, 3, 1), right, left


def block_kernel(flags, it, r_in, k_in, c_ref, ou, od, ru, rd, m_ref, n_ref, pool):
    dn, up, right, left = completed(ou, od, ru, rd)
    pool[0] = right + roll(right, -8, 1)
    pool[1] = left + roll(left, -8, 1)
    sums = pool[:, pl.ds(0, CZ, stride=2), :] + pool[:, pl.ds(1, CZ, stride=2), :]
    lane = iota((CZ, LANES), 1)
    for j in range(CROWS):
        own = c_ref[j]
        strip = slice(2 * NZ + CZ * (j // 4), 2 * NZ + CZ * (j // 4) + CZ)
        off = (j % 4) * 32
        src = 16 * j
        for n in range(2):
            value = jnp.where(lane < 64, roll(own, -64 * n, 1), 0.0)
            value = jnp.where((lane >= 64) & (lane < 80), roll(rd[strip], 64 - off - 16 * n, 1), value)
            value = jnp.where(lane >= 112, roll(ru[strip], 112 - off - 16 * n, 1), value)
            if n == 0:
                value = value - jnp.where(lane == 63, roll(sums[0], 63 - src, 1), 0.0)
                value = value + jnp.where(lane == 64, roll(sums[0], 64 - src, 1), 0.0)
                value = value - jnp.where(lane == 127, roll(sums[1], 127 - src, 1), 0.0)
                value = value + jnp.where(lane == 0, roll(sums[1], -src, 1), 0.0)
            at = CZ * (CROWS * n + j)
            m_ref[at:at + CZ] = value
    lane = iota((NZ, LANES), 1)
    first = flags[0] == 0

    def near(base, top):
        tiles = []
        k_row, r_row, v_row = (12, 13, 15) if top else (0, 0, 0)
        for t in range(4):
            tiles.append(k_in[k_row + t])
        for t in range(3):
            i = r_row + t
            r = r_in[i] - jnp.where(lane == 127, roll(right, 127 - 8 * i, 1), 0.0)
            tiles.append(r + jnp.where(lane == 0, roll(left, -8 * i, 1), 0.0))
        tiles.append(it[v_row])
        tiles.append(jnp.where(lane < 32, roll(dn, -8 * k_row, 1), roll(up, 32 - 8 * k_row, 1)))
        shift = 64 if top else 0
        tiles.append(jnp.where(lane < 64, roll(rd[NZ:2 * NZ], -shift, 1), roll(ru[NZ:2 * NZ], 64 - shift, 1)))
        return tiles

    low, high = near(0, False), near(0, True)
    for t in range(10):
        m_ref[2 * BLOCK + NZ * t:2 * BLOCK + NZ * (t + 1)] = jnp.where(first, high[t], low[t])
        n_ref[NZ * t:NZ * (t + 1)] = jnp.where(first, low[t], high[t])


def edge_flux(a, b, pool):
    pool[0] = flux(a(3), b(0), a(7), b(7))
    u, w = a(9), b(9)
    pool[1] = flux(u, w, roll(u, -32, 1), roll(w, -32, 1))
    sums = pool[:, pl.ds(0, CZ, stride=2), :] + pool[:, pl.ds(1, CZ, stride=2), :]
    child, parent = iota((LANES, LANES), 0), iota((LANES, LANES), 1)
    own = jnp.where(child // 2 == parent, F32(1.0), F32(0.0))
    right = (child < 32) & (child // 2 + 64 == parent)
    left = (child >= 64) & (child < 96) & (child // 2 + 80 == parent)
    beyond = jnp.where(right | left, F32(1.0), F32(0.0))
    return dot(sums[0], own) + dot(sums[1], beyond)


def chip_kernel(pair, near, o_ref, pool):
    def tile(n):
        return lambda t: pair[n, 2 * BLOCK + NZ * t:2 * BLOCK + NZ * (t + 1)]

    inner = edge_flux(tile(0), tile(1), pool)
    for n in range(2):
        o_ref[2 * BLOCK * n:2 * BLOCK * (n + 1)] = pair[n, 0:2 * BLOCK]
    last = BLOCK - CZ
    o_ref[last:BLOCK] = pair[0, last:BLOCK] - inner
    o_ref[2 * BLOCK:2 * BLOCK + CZ] = pair[1, 0:CZ] + inner
    o_ref[4 * BLOCK:] = near[...]


def relay_kernel(flags, out, o_ref, pool):
    first = flags[0] == 0
    low, high = flags[1].astype(F32), flags[2].astype(F32)

    def tile(n, valid):
        return lambda t: out[n, 4 * BLOCK + NZ * t:4 * BLOCK + NZ * (t + 1)] * valid

    outer = edge_flux(tile(0, low), tile(1, high), pool)
    o_ref[0:2 * BLOCK] = jnp.where(first, out[0, 2 * BLOCK:4 * BLOCK] * low, out[1, 0:2 * BLOCK] * high)
    o_ref[2 * BLOCK:] = outer


def sweep(lo, hi, mid, shift, sweeps, r_s, s_s, x_s, c_s, width):
    start, pairs = weights(sweeps)
    for n in range(1, sweeps):
        keep, add = pairs[n - 1]
        prev, here = s_s[lo + n - 1], s_s[lo + n]
        for i in range(lo + n, hi - n):
            ahead = s_s[i + 1]
            total = c_s[0, i] * ahead + c_s[1, i] * prev
            total = total + c_s[2, i] * roll(here, -1, 0) + c_s[3, i] * roll(here, 1, 0)
            total = total + c_s[4, i] * roll(here, -1, 1) + c_s[5, i] * roll(here, 1, 1)
            r = r_s[i] - (here - total)
            step = keep * here + add * r
            r_s[i] = r
            s_s[i] = step
            if shift <= i < shift + mid:
                x_s[i - shift] = x_s[i - shift] + (step[:, 0:width] if width else step)
            prev, here = here, ahead


def prepare(rows, mid, shift, sweeps, factor, k_s, r_s, s_s, x_s, c_s, width):
    depth = k_s.shape[1]
    z = iota(k_s.shape[1:], 0)
    start, _ = weights(sweeps)
    below = factor * (k_s[0] + k_s[1])
    for i in range(1, rows - 1):
        k = k_s[i]
        above = factor * (k + k_s[i + 1])
        z_up = factor * (k + jnp.where(z < depth - 1, roll(k, -1, 0), 0.0))
        z_dn = factor * (k + jnp.where(z > 0, roll(k, 1, 0), 0.0))
        y_up = factor * (k + roll(k, -1, 1))
        y_dn = factor * (k + roll(k, 1, 1))
        diagonal = above + below + z_up + z_dn + y_up + y_dn
        inverse = jnp.where(k > 0, 1.0 / jnp.where(k > 0, diagonal, 1.0), 0.0)
        c_s[0, i] = inverse * above
        c_s[1, i] = inverse * below
        c_s[2, i] = jnp.where(z < depth - 1, inverse * z_up, 0.0)
        c_s[3, i] = jnp.where(z > 0, inverse * z_dn, 0.0)
        c_s[4, i] = inverse * y_up
        c_s[5, i] = inverse * y_dn
        r = inverse * r_s[i]
        r_s[i] = r
        s_s[i] = r * start
        if shift <= i < shift + mid:
            x_s[i - shift] = (r[:, 0:width] if width else r) * start
        below = above


def coarse_part(flags, chip, out, near, x_s, k_s, r_s, s_s, c_s):
    first = flags[0] == 0
    low, high = flags[3].astype(F32), flags[4].astype(F32)
    own = near[flags[0], 2 * BLOCK:]
    other = near[1 - flags[0], 2 * BLOCK:]
    f_low = jnp.where(first, own, other)
    f_high = jnp.where(first, other, own)
    for n, dest in enumerate((r_s, k_s)):
        for j in range(CROWS):
            at = slice(BLOCK * n + CZ * j, BLOCK * n + CZ * (j + 1))
            up = slice(2 * BLOCK + BLOCK * n + CZ * j, 2 * BLOCK + BLOCK * n + CZ * (j + 1))
            rows = (
                jnp.where(first, out[0, at] * low, near[0, at]),
                jnp.where(first, out[0, up] * low, chip[at]),
                jnp.where(first, chip[at], chip[up]),
                jnp.where(first, chip[up], out[1, at] * high),
                jnp.where(first, near[1, at], out[1, up] * high),
            )
            for b in range(5):
                dest[CROWS * b + j] = rows[b]
    low_at, high_at = jnp.where(first, 16, 8), jnp.where(first, 32, 24)
    r_s[low_at - 1] = r_s[low_at - 1] - f_low
    r_s[low_at] = r_s[low_at] + f_low
    r_s[high_at - 1] = r_s[high_at - 1] - f_high
    r_s[high_at] = r_s[high_at] + f_high
    zero = jnp.zeros((CZ, LANES), F32)
    s_s[0] = zero
    s_s[CEXT - 1] = zero
    prepare(CEXT, CROWS, COARSE_SWEEPS, COARSE_SWEEPS, 2.0, k_s, r_s, s_s, x_s, c_s, 0)
    sweep(1, CEXT - 1, CROWS, COARSE_SWEEPS, COARSE_SWEEPS, r_s, s_s, x_s, c_s, 0)


def fine_part(flags, it, r_in, k_in, pair, out, ou, od, ru, rd, x_s, k_s, r_s, s_s, c_s):
    first = flags[0] == 0
    low, high = flags[1].astype(F32), flags[2].astype(F32)
    lane = iota((NZ, LANES), 1)
    dn, up, right, left = completed(ou, od, ru, rd)

    def beside(rights, lefts, count):
        return jnp.where(lane < count, rights, jnp.where(lane >= LANES - count, lefts, 0.0))

    def join(a, b):
        return jnp.concatenate([a, b], axis=1)

    for i in range(ROWS):
        off = 8 * i
        e = HALO + i
        k_s[e, :, 0:LANES] = k_in[i]
        k_s[e, :, LANES:] = beside(roll(dn, -off, 1), roll(up, 120 - off, 1), 4)
        r = r_in[i] - jnp.where(lane == 127, roll(right, 127 - off, 1), 0.0)
        r_s[e, :, 0:LANES] = r + jnp.where(lane == 0, roll(left, -off, 1), 0.0)
        r_s[e, :, LANES:] = beside(roll(dn, -off - 4, 1), roll(up, 124 - off, 1), 3)
    edges = rd[NZ:2 * NZ], ru[NZ:2 * NZ]
    for side in range(2):
        def tile(t, side=side):
            at = slice(4 * BLOCK + NZ * t, 4 * BLOCK + NZ * (t + 1))
            by = slice(2 * BLOCK + NZ * t, 2 * BLOCK + NZ * (t + 1))
            if side == 0:
                return jnp.where(first, out[0, at], pair[0, by]) * low
            return jnp.where(first, pair[1, by], out[1, at]) * high

        base = 0 if side == 0 else HALO + ROWS
        halo, face = tile(8), tile(9)
        for q in range(4):
            k_s[base + q, :, 0:LANES] = tile(q)
            k_s[base + q, :, LANES:] = beside(roll(halo, -8 * q, 1), roll(halo, 88 - 8 * q, 1), 4)
        for t in range(3):
            q = t + 1 - side
            r_s[base + q, :, 0:LANES] = tile(4 + t)
            r_s[base + q, :, LANES:] = beside(roll(halo, -8 * q - 4, 1), roll(halo, 92 - 8 * q, 1), 3)
        v_out = join(tile(7), beside(roll(face, -32, 1), face, 4))
        if side == 0:
            v_in = join(it[0], beside(roll(edges[0], -32, 1), roll(edges[1], 64, 1), 4))
            through = flux(k_s[HALO - 1], k_s[HALO], v_out, v_in)
            r_s[HALO - 1] = r_s[HALO - 1] - through
            r_s[HALO] = r_s[HALO] + through
        else:
            v_in = join(it[ROWS - 1], beside(roll(edges[0], -96, 1), edges[1], 4))
            through = flux(k_s[HALO + ROWS - 1], k_s[HALO + ROWS], v_in, v_out)
            r_s[HALO + ROWS - 1] = r_s[HALO + ROWS - 1] - through
            r_s[HALO + ROWS] = r_s[HALO + ROWS] + through
    zero = jnp.zeros((NZ, 2 * LANES), F32)
    s_s[0] = zero
    s_s[EXT - 1] = zero
    prepare(EXT, ROWS, HALO, SWEEPS, 0.5, k_s, r_s, s_s, x_s, c_s, LANES)
    sweep(1, EXT - 1, ROWS, HALO, SWEEPS, r_s, s_s, x_s, c_s, LANES)


def final_kernel(
    flags, it, r_in, k_in, ou, od, ru, rd, pair, chip, out, near, o_ref, p_ref,
    x_c, k_c, r_c, s_c, c_c, x_f, k_f, r_f, s_f, c_f, wide_s,
):
    coarse_part(flags, chip, out, near, x_c, k_c, r_c, s_c, c_c)
    lane = iota((CZ, LANES), 1)
    for a in range(4):
        p_ref[pl.ds(a, CZ, stride=4), :] = jnp.where(lane < CLANES, x_c[a], roll(x_c[a + 4], CLANES, 1))
    fine_part(flags, it, r_in, k_in, pair, out, ou, od, ru, rd, x_f, k_f, r_f, s_f, c_f)
    child, parent = iota((LANES, LANES), 1) // 2, iota((LANES, LANES), 0)
    spread = jnp.where(child == parent, F32(1.0), F32(0.0))
    wide = dot(x_c[...].reshape(CROWS * CZ, LANES), spread).reshape(CROWS, CZ, LANES)
    wide_s[:, pl.ds(0, CZ, stride=2), :] = wide
    wide_s[:, pl.ds(1, CZ, stride=2), :] = wide
    for i in range(ROWS):
        o_ref[i] = it[i] + x_f[i] + wide_s[i // 2]


def planes_kernel(sources, planes, p_ref, o_ref):
    half = sources // 2
    lane = iota((half, LANES), 1)
    for q in range(planes):
        for a in range(4):
            even = p_ref[pl.ds(4 * q + a, half, stride=8 * planes), :]
            odd = p_ref[pl.ds(4 * (planes + q) + a, half, stride=8 * planes), :]
            to = (a * planes + q) * half
            o_ref[to:to + half] = jnp.where(lane < CLANES, even, roll(odd, CLANES, 1))
            to = ((a + 4) * planes + q) * half
            o_ref[to:to + half] = jnp.where(lane < CLANES, roll(even, CLANES, 1), odd)


def call(kernel, outs, scratch, in_smem=False, operands=(), flops=1000000):
    vmem = pl.BlockSpec(memory_space=pltpu.VMEM)
    specs = [vmem] * len(operands)
    if in_smem:
        specs[0] = pl.BlockSpec(memory_space=pltpu.SMEM)
    size = sum(4 * x.size for x in operands) + sum(4 * o.size for o in outs)
    multiple = len(outs) > 1
    return pl.pallas_call(
        kernel,
        out_shape=outs if multiple else outs[0],
        in_specs=specs,
        out_specs=[vmem] * len(outs) if multiple else vmem,
        scratch_shapes=[pltpu.VMEM(s, F32) for s in scratch],
        compiler_params=pltpu.CompilerParams(vmem_limit_bytes=40 * 1024 * 1024),
        cost_estimate=pl.CostEstimate(flops=flops, bytes_accessed=size, transcendentals=0),
    )(*operands)


def shape(*dims):
    return jax.ShapeDtypeStruct(dims, F32)


def on_device(iterate, source, labels):
    n_gx, n_gy = lax.axis_size("gx"), lax.axis_size("gy")
    gx = lax.axis_index("gx")
    flags = jnp.stack([gx % 2, gx > 0, gx < n_gx - 1, gx > 1, gx < n_gx - 2]).astype(jnp.int32)
    chips = [[i, i + 1] for i in range(0, n_gx, 2)]
    between = [[i, (i + 1) % n_gx] for i in range(1, n_gx, 2)]
    own = shape(ROWS, NZ, LANES)
    strip = shape(3 * NZ, LANES)
    resid, cond, coarse, up, dn = call(
        residual_kernel,
        [own, own, shape(CROWS, CZ, LANES), strip, strip],
        [(2, CROWS, NZ, LANES)],
        False,
        (iterate, source, labels),
    )
    onward = [(i, i + 1) for i in range(n_gy - 1)]
    back = [(i + 1, i) for i in range(n_gy - 1)]
    from_left = lax.ppermute(up, "gy", onward)
    from_right = lax.ppermute(dn, "gy", back)
    strips = (up, dn, from_left, from_right)
    block, near = call(
        block_kernel,
        [shape(2 * BLOCK + 10 * NZ, LANES), shape(10 * NZ, LANES)],
        [(2, NZ, LANES)],
        True,
        (flags, iterate, resid, cond, coarse, *strips),
    )
    pair = lax.all_gather(block, "gx", axis_index_groups=chips)
    chip = call(chip_kernel, [shape(4 * BLOCK + 10 * NZ, LANES)], [(2, NZ, LANES)], False, (pair, near))
    beyond = lax.all_gather(chip, "gx", axis_index_groups=between)
    relay = call(relay_kernel, [shape(2 * BLOCK + CZ, LANES)], [(2, NZ, LANES)], True, (flags, beyond))
    relay = lax.all_gather(relay, "gx", axis_index_groups=chips)
    rows, wide = (CEXT, CZ, LANES), (EXT, NZ, 2 * LANES)
    corrected, planes = call(
        final_kernel,
        [own, shape(4 * CZ, LANES)],
        [(CROWS, CZ, LANES), rows, rows, rows, (6, *rows)]
        + [(ROWS, NZ, LANES), wide, wide, wide, (6, *wide), (CROWS, NZ, LANES)],
        True,
        (flags, iterate, resid, cond, *strips, pair, chip, beyond, relay),
    )
    per = CZ // n_gy
    planes = lax.all_to_all(planes.reshape(n_gy, 4 * per, LANES), "gy", split_axis=0, concat_axis=0, tiled=True)
    owned = call(
        functools.partial(planes_kernel, n_gy, per),
        [shape(4 * CZ, LANES)],
        [],
        False,
        (planes.reshape(4 * CZ, LANES),),
    ).reshape(CROWS, per, CLANES * n_gy)
    return corrected, owned


def solution(mesh):
    spec = P("gx", None, "gy")
    return jax.shard_map(
        on_device, mesh=mesh, in_specs=(spec, spec, spec), out_specs=(spec, P("gx", "gy", None)), check_vma=False
    )
```

time: 75.9 us -> 67.9 us (0.89)
  blocking collectives: 32.7 us -> 43.5 us
  starting transfers between devices: 14.5 us -> 5.67 us
  waiting for transfers between devices: 11.5 us -> 3.61 us
  other arithmetic: 1.74 us -> 0 us
    all_to_all x0 -> x1, blocking collectives: none -> 23.2 us  [on_device(): lax.all_to_all(planes.reshape(n_gy, 4 * per, LANES), 'gy', split_axis=0,...]
    all_gather x4 -> x2, blocking collectives: 26.5 us -> 13.6 us  [the longest x1 8.56 us: on_device(): beyond = lax.all_gather(chip, 'gx', axis_index_groups=between)]
    all_to_all x1 -> x0, starting transfers between devices: 11.9 us -> none  [on_device(): lax.all_to_all(coarse_out[:, :, :CLANES], 'gy', split_axis=1, concat_axis...]
    all_to_all x1 -> x0, waiting for transfers between devices: 7.93 us -> none  [on_device(): lax.all_to_all(coarse_out[:, :, :CLANES], 'gy', split_axis=1, concat_axis...]
    ppermute x1, starting transfers between devices: 1.28 us -> 4.37 us  [on_device(): from_left = lax.ppermute(up, 'gy', onward)]
    unnamed x8, local copies, waits for them, and re-layouts: 0.81 us -> 2.85 us
    all_to_all x3 -> x0, local copies, waits for them, and re-layouts: 1.24 us -> none  [on_device(): lax.all_to_all(coarse_out[:, :, :CLANES], 'gy', split_axis=1, concat_axis...]
    concatenate x1 -> x0, other arithmetic: 0.97 us -> none  [on_device(): upper = jnp.concatenate([iterate[-4:], source[-3:], conduct(labels[-4:])])]
  transfers between devices with their start and end apart: 3 -> 2, of which waited for: 2 -> 1; matrix products, arithmetic and copies ran while one was open for 0% -> 0% of each run, Pallas kernels for 5% -> 0%
where the time goes in v3:
time: 67.9 us; the launch traced here: 67.6 us
  blocking collectives  43.5 us (64%)
  Pallas kernels  11.2 us (16%)
  starting transfers between devices  5.67 us (8%)
  waiting for transfers between devices  3.61 us (5%)
  local copies, waits for them, and re-layouts  2.93 us (4%)
  between operations  0.7 us (1%)
    all_to_all x1, blocking collectives, on_device(): lax.all_to_all(planes.reshape(n_gy, 4 * per, LANES), 'gy', split_axis=0,...  23.2 us
    pallas_call x6, Pallas kernels, call(): pl.pallas_call(kernel, out_shape=outs if multiple else outs[0], in_specs=...  11.2 us
    all_gather x1, blocking collectives, on_device(): beyond = lax.all_gather(chip, 'gx', axis_index_groups=between)  8.56 us
    all_gather x1, blocking collectives, on_device(): pair = lax.all_gather(block, 'gx', axis_index_groups=chips)  6.62 us
    all_gather x1, blocking collectives, on_device(): relay = lax.all_gather(relay, 'gx', axis_index_groups=chips)  5.09 us
    ppermute x1, starting transfers between devices, on_device(): from_left = lax.ppermute(up, 'gy', onward)  4.37 us
    ppermute x1, waiting for transfers between devices, on_device(): from_right = lax.ppermute(dn, 'gy', back)  3.61 us
    unnamed x8, local copies, waits for them, and re-layouts  2.85 us
  transfers between devices with their start and end apart: 2, of which 1 were waited for; matrix products, arithmetic and copies ran while one was open for 0% of the time, Pallas kernels for 0%

profile of v3, /device:TPU:1, one launch (start us, length us, event | category | flops | bytes accessed | tf_op | source)
XLA Modules:
  0.0 67.6 jit_solution(643782501412725444)
XLA Ops:
  0.6 0.0 copy-start
  0.6 0.9 %copy-done = f32[16,32,128]{2,1,0:T(8,128)S(1)} copy-done((f32[16,32,128]{2,1,0:T(8,128)S(1)}, f32[16,32,128]{2,1,0:T(8,128)}, u32[]{:S(2)}) %copy-start) | copy-done | bytes 262168
  1.6 0.0 copy-start.2
  1.6 0.9 %copy-done.2 = f32[16,32,128]{2,1,0:T(8,128)S(1)} copy-done((f32[16,32,128]{2,1,0:T(8,128)S(1)}, f32[16,32,128]{2,1,0:T(8,128)}, u32[]{:S(2)}) %copy-start.2) | copy-done | bytes 262168
  2.5 0.0 copy-start.3
  2.5 0.9 %copy-done.3 = s32[16,32,128]{2,1,0:T(8,128)S(1)} copy-done((s32[16,32,128]{2,1,0:T(8,128)S(1)}, s32[16,32,128]{2,1,0:T(8,128)}, u32[]{:S(2)}) %copy-start.3) | copy-done | bytes 262168
  3.5 0.0 copy-start.1
  3.5 2.0 %shard_map.50 = (f32[16,32,128]{2,1,0:T(8,128)S(1)}, f32[16,32,128]{2,1,0:T(8,128)S(1)}, f32[8,16,128]{2,1,0:T(8,128)S(1)}, f32[96,128]{1,0:T(8,128)S(1)}, f32[96,128]{1,0:T(8,128)S(1)}) custom-call(f32[16,32,128]{2,1,0:T(8,128)S(1)} %copy-done, f32[16,32,128]{2,1,0:T(8,128)S(1)} %copy-done.2, s32[16,32,128]{2,1,0:T(8,128)S(1)} %copy-done.3), custom_call_target="tpu_custom_call" | custom-call | flops 1000000 | bytes 1474560 | tf_op jit(solution)/shard_map/pallas_call | solution.py:392
  5.5 4.4 %collective-permute-start = (f32[96,128]{1,0:T(8,128)S(1)}, f32[96,128]{1,0:T(8,128)S(1)}, u32[]{:S(2)}, u32[]{:S(2)}) collective-permute-start(f32[96,128]{1,0:T(8,128)S(1)} %get-tuple-element.13.ou), channel_id=1, source_target_pairs={{0,1},{1,2},{2,3},{3,4},{4,5},{5,6},{6,7},{7,8},{8,9},{9,10},{10,1... | collective-permute-start | bytes 147464 | tf_op jit(solution)/shard_map/ppermute | solution.py:424
  9.9 1.3 %collective-permute-start.1 = (f32[96,128]{1,0:T(8,128)S(1)}, f32[96,128]{1,0:T(8,128)S(1)}, u32[]{:S(2)}, u32[]{:S(2)}) collective-permute-start(f32[96,128]{1,0:T(8,128)S(1)} %get-tuple-element.14.od), channel_id=1, source_target_pairs={{1,0},{2,1},{3,2},{4,3},{5,4},{6,5},{7,6},{8,7},{9,8},{10,9},{11,1... | collective-permute-start | bytes 147464 | tf_op jit(solution)/shard_map/ppermute | solution.py:425
  11.2 0.1 stack.39.flags
  11.3 0.0 collective-permute-done.ru
  11.3 3.6 %collective-permute-done.1.rd = f32[96,128]{1,0:T(8,128)S(1)} collective-permute-done((f32[96,128]{1,0:T(8,128)S(1)}, f32[96,128]{1,0:T(8,128)S(1)}, u32[]{:S(2)}, u32[]{:S(2)}) %collective-permute-start.1) | collective-permute-done | bytes 49184 | tf_op jit(solution)/shard_map/ppermute | solution.py:425
  14.9 0.0 copy-done.1
  14.9 0.9 %shard_map.51 = (f32[576,128]{1,0:T(8,128)S(1)}, f32[320,128]{1,0:T(8,128)S(1)}) custom-call(s32[5]{0:T(128)S(1)} %stack.39.flags, f32[16,32,128]{2,1,0:T(8,128)S(1)} %copy-done.1, f32[16,32,128]{2,1,0:T(8,128)S(1)} %get-tuple-element.11.r_in, f32[16,32,128]{2,1,0:T(8,128)S(1)} %get-tuple-element.12.k_in, f32[8,16,128]{2,1,0:T(8,128)S(1)} %get-tuple-element.15.c_ref, ...), custom_call_target="tpu_custom_call" | custom-call | flops 1000000 | bytes 1507348 | tf_op jit(solution)/shard_map/pallas_call | solution.py:392
  15.8 6.6 %all-gather = f32[1152,128]{1,0:T(8,128)S(1)} all-gather(f32[576,128]{1,0:T(8,128)S(1)} %get-tuple-element.16), channel_id=2, replica_groups={{0,16},{32,48},{64,80},{96,112},{128,144},{160,176},{192,208},{224,240}..., dimensions={0}, use_global_device_ids=true | all-gather | bytes 884736 | tf_op jit(solution)/shard_map/all_gather | solution.py:434
  22.4 0.2 shard_map.52.chip
  22.7 8.6 %all-gather.1 = f32[1664,128]{1,0:T(8,128)S(1)} all-gather(f32[832,128]{1,0:T(8,128)S(1)} %shard_map.52.chip), channel_id=3, replica_groups={{16,32},{48,64},{80,96},{112,128},{144,160},{176,192},{208,224},{240,25..., dimensions={0}, use_global_device_ids=true | all-gather | bytes 1277952 | tf_op jit(solution)/shard_map/all_gather | solution.py:436
  31.2 0.8 %shard_map.53 = f32[272,128]{1,0:T(8,128)S(1)} custom-call(s32[5]{0:T(128)S(1)} %stack.39.flags, f32[2,832,128]{2,1,0:T(8,128)S(1)} %bitcast.11), custom_call_target="tpu_custom_call" | custom-call | flops 1000000 | bytes 991252 | tf_op jit(solution)/shard_map/pallas_call | solution.py:392
  32.0 5.1 %all-gather.2 = f32[544,128]{1,0:T(8,128)S(1)} all-gather(f32[272,128]{1,0:T(8,128)S(1)} %shard_map.53), channel_id=4, replica_groups={{0,16},{32,48},{64,80},{96,112},{128,144},{160,176},{192,208},{224,240}..., dimensions={0}, use_global_device_ids=true | all-gather | bytes 417792 | tf_op jit(solution)/shard_map/all_gather | solution.py:438
  37.1 6.6 %shard_map.54 = (f32[16,32,128]{2,1,0:T(8,128)}, f32[64,128]{1,0:T(8,128)S(1)}) custom-call(s32[5]{0:T(128)S(1)} %stack.39.flags, f32[16,32,128]{2,1,0:T(8,128)S(1)} %copy-done.1, f32[16,32,128]{2,1,0:T(8,128)S(1)} %get-tuple-element.11.r_in, f32[16,32,128]{2,1,0:T(8,128)S(1)} %get-tuple-element.12.k_in, f32[96,128]{1,0:T(8,128)S(1)} %get-tuple-element.13.ou, ...), custom_call_target="tpu_custom_call" | custom-call | flops 1000000 | bytes 3424276 | tf_op jit(solution)/shard_map/pallas_call | solution.py:392
  43.7 23.2 %all_to_all.5 = f32[16,4,128]{2,1,0:T(4,128)S(1)} all-to-all(f32[16,4,128]{2,1,0:T(4,128)S(1)} %bitcast.17), channel_id=1, replica_groups=mesh['gx'=32,'gy'=16] {'gy'}, dimensions={0} | all-to-all | bytes 65536 | tf_op jit(solution)/shard_map/all_to_all | solution.py:449
  66.9 0.7 %shard_map.55 = f32[64,128]{1,0:T(8,128)} custom-call(f32[64,128]{1,0:T(8,128)S(1)} %bitcast.16), custom_call_target="tpu_custom_call" | custom-call | flops 1000000 | bytes 65536 | tf_op jit(solution)/shard_map/pallas_call | solution.py:392
Async XLA Ops:
  0.6 1.0 %copy-start = (f32[16,32,128]{2,1,0:T(8,128)S(1)}, f32[16,32,128]{2,1,0:T(8,128)}, u32[]{:S(2)}) copy-start(f32[16,32,128]{2,1,0:T(8,128)} %it.5) | copy-start | bytes 786436
  1.6 0.9 %copy-start.2 = (f32[16,32,128]{2,1,0:T(8,128)S(1)}, f32[16,32,128]{2,1,0:T(8,128)}, u32[]{:S(2)}) copy-start(f32[16,32,128]{2,1,0:T(8,128)} %src.1) | copy-start | bytes 786436
  2.5 0.9 %copy-start.3 = (s32[16,32,128]{2,1,0:T(8,128)S(1)}, s32[16,32,128]{2,1,0:T(8,128)}, u32[]{:S(2)}) copy-start(s32[16,32,128]{2,1,0:T(8,128)} %lab.1) | copy-start | bytes 786436
  3.5 11.4 %copy-start.1 = (f32[16,32,128]{2,1,0:T(8,128)S(1)}, f32[16,32,128]{2,1,0:T(8,128)}, u32[]{:S(2)}) copy-start(f32[16,32,128]{2,1,0:T(8,128)} %it.5) | copy-start | bytes 786436
  5.5 5.8 %collective-permute-start = (f32[96,128]{1,0:T(8,128)S(1)}, f32[96,128]{1,0:T(8,128)S(1)}, u32[]{:S(2)}, u32[]{:S(2)}) collective-permute-start(f32[96,128]{1,0:T(8,128)S(1)} %get-tuple-element.13.ou), channel_id=1, source_target_pairs={{0,1},{1,2},{2,3},{3,4},{4,5},{5,6},{6,7},{7,8},{8,9},{9,10},{10,1... | collective-permute-start | bytes 147464 | tf_op jit(solution)/shard_map/ppermute | solution.py:424
  9.9 5.0 %collective-permute-start.1 = (f32[96,128]{1,0:T(8,128)S(1)}, f32[96,128]{1,0:T(8,128)S(1)}, u32[]{:S(2)}, u32[]{:S(2)}) collective-permute-start(f32[96,128]{1,0:T(8,128)S(1)} %get-tuple-element.14.od), channel_id=1, source_target_pairs={{1,0},{2,1},{3,2},{4,3},{5,4},{6,5},{7,6},{8,7},{9,8},{10,9},{11,1... | collective-permute-start | bytes 147464 | tf_op jit(solution)/shard_map/ppermute | solution.py:425

commit v4 on v3

--- a/solution.py
+++ b/solution.py
@@ -19,7 +19,10 @@
 HALO = SWEEPS
 EXT = ROWS + 2 * HALO
 CEXT = CROWS + 2 * COARSE_SWEEPS
-BLOCK = CROWS * CZ
+OWN = CROWS * CZ
+BLOCK = OWN + 4 * CZ
+NEAR = 10 * NZ
+PARTS = 4
 
 
 def weights(sweeps):
@@ -60,14 +63,33 @@
     return jnp.dot(a, b, precision=lax.Precision.HIGHEST, preferred_element_type=F32)
 
 
-def residual_kernel(it, src, lab, r_ref, k_ref, c_ref, up_ref, dn_ref, pool):
-    for i in range(ROWS):
-        k_ref[i] = conduct(lab[i])
+def residual_kernel(it_in, src_in, lab_in, r_ref, k_ref, c_ref, up_ref, dn_ref, pool, it, src, lab, sems):
+    copies = []
+    for part in range(PARTS):
+        rows = pl.ds(part * ROWS // PARTS, ROWS // PARTS)
+        copies.append(
+            [
+                pltpu.make_async_copy(a.at[rows], b.at[rows], sems.at[n, part])
+                for n, (a, b) in enumerate(((lab_in, lab), (it_in, it), (src_in, src)))
+            ]
+        )
+        for copy in copies[-1]:
+            copy.start()
+
+    def arrive(part):
+        for copy in copies[part]:
+            copy.wait()
+        for i in range(part * ROWS // PARTS, (part + 1) * ROWS // PARTS):
+            k_ref[i] = conduct(lab[i])
+
+    arrive(0)
     z, lane = iota((NZ, LANES), 0), iota((NZ, LANES), 1)
     zero = jnp.zeros((NZ, LANES), F32)
     before = zero
     up = dn = zero
     for i in range(ROWS):
+        if (i + 1) % (ROWS // PARTS) == 0 and i < ROWS - 1:
+            arrive((i + 1) // (ROWS // PARTS))
         k, v = k_ref[i], it[i]
         after = flux(k, k_ref[i + 1], v, it[i + 1]) if i < ROWS - 1 else zero
         fy = jnp.where(lane < LANES - 1, flux(k, roll(k, -1, 1), v, roll(v, -1, 1)), 0.0)
@@ -139,21 +161,17 @@
     sums = pool[:, pl.ds(0, CZ, stride=2), :] + pool[:, pl.ds(1, CZ, stride=2), :]
     lane = iota((CZ, LANES), 1)
     for j in range(CROWS):
-        own = c_ref[j]
-        strip = slice(2 * NZ + CZ * (j // 4), 2 * NZ + CZ * (j // 4) + CZ)
-        off = (j % 4) * 32
-        src = 16 * j
-        for n in range(2):
-            value = jnp.where(lane < 64, roll(own, -64 * n, 1), 0.0)
-            value = jnp.where((lane >= 64) & (lane < 80), roll(rd[strip], 64 - off - 16 * n, 1), value)
-            value = jnp.where(lane >= 112, roll(ru[strip], 112 - off - 16 * n, 1), value)
-            if n == 0:
-                value = value - jnp.where(lane == 63, roll(sums[0], 63 - src, 1), 0.0)
-                value = value + jnp.where(lane == 64, roll(sums[0], 64 - src, 1), 0.0)
-                value = value - jnp.where(lane == 127, roll(sums[1], 127 - src, 1), 0.0)
-                value = value + jnp.where(lane == 0, roll(sums[1], -src, 1), 0.0)
-            at = CZ * (CROWS * n + j)
-            m_ref[at:at + CZ] = value
+        value = c_ref[j] - jnp.where(lane == 63, roll(sums[0], 63 - 16 * j, 1), 0.0)
+        m_ref[CZ * j:CZ * (j + 1)] = value + jnp.where(lane == 0, roll(sums[1], -16 * j, 1), 0.0)
+    for t in range(2):
+        at = slice(2 * NZ + CZ * t, 2 * NZ + CZ * (t + 1))
+        more, less = rd[at], ru[at]
+        for q in range(4):
+            src = 16 * (4 * t + q)
+            more = more + jnp.where(lane == 32 * q, roll(sums[0], 32 * q - src, 1), 0.0)
+            less = less - jnp.where(lane == 32 * q + 15, roll(sums[1], 32 * q + 15 - src, 1), 0.0)
+        m_ref[OWN + CZ * t:OWN + CZ * (t + 1)] = more
+        m_ref[OWN + CZ * (2 + t):OWN + CZ * (3 + t)] = less
     lane = iota((NZ, LANES), 1)
     first = flags[0] == 0
 
@@ -174,7 +192,7 @@
 
     low, high = near(0, False), near(0, True)
     for t in range(10):
-        m_ref[2 * BLOCK + NZ * t:2 * BLOCK + NZ * (t + 1)] = jnp.where(first, high[t], low[t])
+        m_ref[BLOCK + NZ * t:BLOCK + NZ * (t + 1)] = jnp.where(first, high[t], low[t])
         n_ref[NZ * t:NZ * (t + 1)] = jnp.where(first, low[t], high[t])
 
 
@@ -193,15 +211,24 @@
 
 def chip_kernel(pair, near, o_ref, pool):
     def tile(n):
-        return lambda t: pair[n, 2 * BLOCK + NZ * t:2 * BLOCK + NZ * (t + 1)]
+        return lambda t: pair[n, BLOCK + NZ * t:BLOCK + NZ * (t + 1)]
 
     inner = edge_flux(tile(0), tile(1), pool)
     for n in range(2):
-        o_ref[2 * BLOCK * n:2 * BLOCK * (n + 1)] = pair[n, 0:2 * BLOCK]
-    last = BLOCK - CZ
-    o_ref[last:BLOCK] = pair[0, last:BLOCK] - inner
-    o_ref[2 * BLOCK:2 * BLOCK + CZ] = pair[1, 0:CZ] + inner
-    o_ref[4 * BLOCK:] = near[...]
+        o_ref[BLOCK * n:BLOCK * (n + 1)] = pair[n, 0:BLOCK]
+    lane = iota((CZ, LANES), 1)
+    for n, j in ((0, CROWS - 1), (1, 0)):
+        change = inner if n else -inner
+        off = 32 * (j % 4)
+        side = (lane >= off) & (lane < off + 16)
+        changes = (
+            (CZ * j, jnp.where(lane < CLANES, change, 0.0)),
+            (OWN + CZ * (j // 4), jnp.where(side, roll(change, off - 64, 1), 0.0)),
+            (OWN + CZ * (2 + j // 4), jnp.where(side, roll(change, off - 112, 1), 0.0)),
+        )
+        for at, part in changes:
+            o_ref[BLOCK * n + at:BLOCK * n + at + CZ] = pair[n, at:at + CZ] + part
+    o_ref[2 * BLOCK:] = near[...]
 
 
 def relay_kernel(flags, out, o_ref, pool):
@@ -209,11 +236,11 @@
     low, high = flags[1].astype(F32), flags[2].astype(F32)
 
     def tile(n, valid):
-        return lambda t: out[n, 4 * BLOCK + NZ * t:4 * BLOCK + NZ * (t + 1)] * valid
+        return lambda t: out[n, 2 * BLOCK + NZ * t:2 * BLOCK + NZ * (t + 1)] * valid
 
     outer = edge_flux(tile(0, low), tile(1, high), pool)
-    o_ref[0:2 * BLOCK] = jnp.where(first, out[0, 2 * BLOCK:4 * BLOCK] * low, out[1, 0:2 * BLOCK] * high)
-    o_ref[2 * BLOCK:] = outer
+    o_ref[0:BLOCK] = jnp.where(first, out[0, BLOCK:2 * BLOCK] * low, out[1, 0:BLOCK] * high)
+    o_ref[BLOCK:] = outer
 
 
 def sweep(lo, hi, mid, shift, sweeps, r_s, s_s, x_s, c_s, width):
@@ -266,23 +293,32 @@
 def coarse_part(flags, chip, out, near, x_s, k_s, r_s, s_s, c_s):
     first = flags[0] == 0
     low, high = flags[3].astype(F32), flags[4].astype(F32)
-    own = near[flags[0], 2 * BLOCK:]
-    other = near[1 - flags[0], 2 * BLOCK:]
+    own = near[flags[0], BLOCK:]
+    other = near[1 - flags[0], BLOCK:]
     f_low = jnp.where(first, own, other)
     f_high = jnp.where(first, other, own)
-    for n, dest in enumerate((r_s, k_s)):
-        for j in range(CROWS):
-            at = slice(BLOCK * n + CZ * j, BLOCK * n + CZ * (j + 1))
-            up = slice(2 * BLOCK + BLOCK * n + CZ * j, 2 * BLOCK + BLOCK * n + CZ * (j + 1))
-            rows = (
-                jnp.where(first, out[0, at] * low, near[0, at]),
-                jnp.where(first, out[0, up] * low, chip[at]),
-                jnp.where(first, chip[at], chip[up]),
-                jnp.where(first, chip[up], out[1, at] * high),
-                jnp.where(first, near[1, at], out[1, up] * high),
-            )
-            for b in range(5):
-                dest[CROWS * b + j] = rows[b]
+    lane = iota((CZ, LANES), 1)
+
+    def packed(at):
+        up = slice(BLOCK + at.start, BLOCK + at.stop)
+        return (
+            jnp.where(first, out[0, at] * low, near[0, at]),
+            jnp.where(first, out[0, up] * low, chip[at]),
+            jnp.where(first, chip[at], chip[up]),
+            jnp.where(first, chip[up], out[1, at] * high),
+            jnp.where(first, near[1, at], out[1, up] * high),
+        )
+
+    sides = [packed(slice(OWN + CZ * t, OWN + CZ * (t + 1))) for t in range(4)]
+    for j in range(CROWS):
+        off = 32 * (j % 4)
+        rows = packed(slice(CZ * j, CZ * (j + 1)))
+        for b in range(5):
+            more, less = sides[j // 4][b], sides[2 + j // 4][b]
+            for n, dest in enumerate((r_s, k_s)):
+                value = jnp.where(lane < CLANES, roll(rows[b], -CLANES * n, 1), 0.0)
+                value = jnp.where((lane >= 64) & (lane < 80), roll(more, 64 - off - 16 * n, 1), value)
+                dest[CROWS * b + j] = jnp.where(lane >= 112, roll(less, 112 - off - 16 * n, 1), value)
     low_at, high_at = jnp.where(first, 16, 8), jnp.where(first, 32, 24)
     r_s[low_at - 1] = r_s[low_at - 1] - f_low
     r_s[low_at] = r_s[low_at] + f_low
@@ -318,8 +354,8 @@
     edges = rd[NZ:2 * NZ], ru[NZ:2 * NZ]
     for side in range(2):
         def tile(t, side=side):
-            at = slice(4 * BLOCK + NZ * t, 4 * BLOCK + NZ * (t + 1))
-            by = slice(2 * BLOCK + NZ * t, 2 * BLOCK + NZ * (t + 1))
+            at = slice(2 * BLOCK + NZ * t, 2 * BLOCK + NZ * (t + 1))
+            by = slice(BLOCK + NZ * t, BLOCK + NZ * (t + 1))
             if side == 0:
                 return jnp.where(first, out[0, at], pair[0, by]) * low
             return jnp.where(first, pair[1, by], out[1, at]) * high
@@ -351,14 +387,16 @@
     sweep(1, EXT - 1, ROWS, HALO, SWEEPS, r_s, s_s, x_s, c_s, LANES)
 
 
-def final_kernel(
-    flags, it, r_in, k_in, ou, od, ru, rd, pair, chip, out, near, o_ref, p_ref,
-    x_c, k_c, r_c, s_c, c_c, x_f, k_f, r_f, s_f, c_f, wide_s,
-):
-    coarse_part(flags, chip, out, near, x_c, k_c, r_c, s_c, c_c)
+def coarse_kernel(flags, chip, out, near, x_ref, p_ref, k_s, r_s, s_s, c_s):
+    coarse_part(flags, chip, out, near, x_ref, k_s, r_s, s_s, c_s)
     lane = iota((CZ, LANES), 1)
     for a in range(4):
-        p_ref[pl.ds(a, CZ, stride=4), :] = jnp.where(lane < CLANES, x_c[a], roll(x_c[a + 4], CLANES, 1))
+        p_ref[pl.ds(a, CZ, stride=4), :] = jnp.where(lane < CLANES, x_ref[a], roll(x_ref[a + 4], CLANES, 1))
+
+
+def fine_kernel(
+    flags, it, r_in, k_in, ou, od, ru, rd, pair, out, x_c, o_ref, x_f, k_f, r_f, s_f, c_f, wide_s
+):
     fine_part(flags, it, r_in, k_in, pair, out, ou, od, ru, rd, x_f, k_f, r_f, s_f, c_f)
     child, parent = iota((LANES, LANES), 1) // 2, iota((LANES, LANES), 0)
     spread = jnp.where(child == parent, F32(1.0), F32(0.0))
@@ -382,20 +420,24 @@
             o_ref[to:to + half] = jnp.where(lane < CLANES, roll(even, CLANES, 1), odd)
 
 
-def call(kernel, outs, scratch, in_smem=False, operands=(), flops=1000000):
+def call(kernel, outs, scratch, in_smem=False, operands=(), flops=1000000, copies=False):
     vmem = pl.BlockSpec(memory_space=pltpu.VMEM)
-    specs = [vmem] * len(operands)
+    specs = [pl.BlockSpec(memory_space=pltpu.HBM) if copies else vmem] * len(operands)
     if in_smem:
         specs[0] = pl.BlockSpec(memory_space=pltpu.SMEM)
     size = sum(4 * x.size for x in operands) + sum(4 * o.size for o in outs)
     multiple = len(outs) > 1
+    held = [pltpu.VMEM(s, F32) for s in scratch]
+    if copies:
+        held += [pltpu.VMEM(x.shape, x.dtype) for x in operands]
+        held.append(pltpu.SemaphoreType.DMA((len(operands), PARTS)))
     return pl.pallas_call(
         kernel,
         out_shape=outs if multiple else outs[0],
         in_specs=specs,
         out_specs=[vmem] * len(outs) if multiple else vmem,
-        scratch_shapes=[pltpu.VMEM(s, F32) for s in scratch],
-        compiler_params=pltpu.CompilerParams(vmem_limit_bytes=40 * 1024 * 1024),
+        scratch_shapes=held,
+        compiler_params=pltpu.CompilerParams(vmem_limit_bytes=(54500 if copies else 40960) * 1024),
         cost_estimate=pl.CostEstimate(flops=flops, bytes_accessed=size, transcendentals=0),
     )(*operands)
 
@@ -418,6 +460,7 @@
         [(2, CROWS, NZ, LANES)],
         False,
         (iterate, source, labels),
+        copies=True,
     )
     onward = [(i, i + 1) for i in range(n_gy - 1)]
     back = [(i + 1, i) for i in range(n_gy - 1)]
@@ -426,27 +469,34 @@
     strips = (up, dn, from_left, from_right)
     block, near = call(
         block_kernel,
-        [shape(2 * BLOCK + 10 * NZ, LANES), shape(10 * NZ, LANES)],
+        [shape(BLOCK + NEAR, LANES), shape(NEAR, LANES)],
         [(2, NZ, LANES)],
         True,
         (flags, iterate, resid, cond, coarse, *strips),
     )
     pair = lax.all_gather(block, "gx", axis_index_groups=chips)
-    chip = call(chip_kernel, [shape(4 * BLOCK + 10 * NZ, LANES)], [(2, NZ, LANES)], False, (pair, near))
+    chip = call(chip_kernel, [shape(2 * BLOCK + NEAR, LANES)], [(2, NZ, LANES)], False, (pair, near))
     beyond = lax.all_gather(chip, "gx", axis_index_groups=between)
-    relay = call(relay_kernel, [shape(2 * BLOCK + CZ, LANES)], [(2, NZ, LANES)], True, (flags, beyond))
+    relay = call(relay_kernel, [shape(BLOCK + CZ, LANES)], [(2, NZ, LANES)], True, (flags, beyond))
     relay = lax.all_gather(relay, "gx", axis_index_groups=chips)
     rows, wide = (CEXT, CZ, LANES), (EXT, NZ, 2 * LANES)
-    corrected, planes = call(
-        final_kernel,
-        [own, shape(4 * CZ, LANES)],
-        [(CROWS, CZ, LANES), rows, rows, rows, (6, *rows)]
-        + [(ROWS, NZ, LANES), wide, wide, wide, (6, *wide), (CROWS, NZ, LANES)],
+    coarse_out, planes = call(
+        coarse_kernel,
+        [shape(CROWS, CZ, LANES), shape(4 * CZ, LANES)],
+        [rows, rows, rows, (6, *rows)],
         True,
-        (flags, iterate, resid, cond, *strips, pair, chip, beyond, relay),
+        (flags, chip, beyond, relay),
     )
     per = CZ // n_gy
     planes = lax.all_to_all(planes.reshape(n_gy, 4 * per, LANES), "gy", split_axis=0, concat_axis=0, tiled=True)
+    corrected = call(
+        fine_kernel,
+        [own],
+        [(ROWS, NZ, LANES), wide, wide, wide, (6, *wide), (CROWS, NZ, LANES)],
+        True,
+        (flags, iterate, resid, cond, *strips, pair, beyond, coarse_out),
+        flops=20000000,
+    )
     owned = call(
         functools.partial(planes_kernel, n_gy, per),
         [shape(4 * CZ, LANES)],

time: 67.9 us -> 62.2 us (0.916)
  blocking collectives: 43.5 us -> 19.4 us
  starting transfers between devices: 5.67 us -> 17.6 us
  waiting for transfers between devices: 3.61 us -> 11 us
  local copies, waits for them, and re-layouts: 2.93 us -> 0.09 us
  Pallas kernels: 11.2 us -> 13.1 us
    all_to_all x1 -> x0, blocking collectives: 23.2 us -> none  [on_device(): lax.all_to_all(planes.reshape(n_gy, 4 * per, LANES), 'gy', split_axis=0,...]
    all_to_all x0 -> x1, starting transfers between devices: none -> 11.9 us  [on_device(): lax.all_to_all(planes.reshape(n_gy, 4 * per, LANES), 'gy', split_axis=0,...]
    all_to_all x0 -> x1, waiting for transfers between devices: none -> 7.39 us  [on_device(): lax.all_to_all(planes.reshape(n_gy, 4 * per, LANES), 'gy', split_axis=0,...]
    unnamed x8 -> x2, local copies, waits for them, and re-layouts: 2.85 us -> 0.01 us
    pallas_call x6 -> x7, Pallas kernels: 11.2 us -> 13.1 us  [call(): pl.pallas_call(kernel, out_shape=outs if multiple else outs[0], in_specs=...]
    all_gather x1, blocking collectives: 8.56 us -> 7.82 us  [on_device(): beyond = lax.all_gather(chip, 'gx', axis_index_groups=between)]
  transfers between devices with their start and end apart: 2 -> 3, of which waited for: 1 -> 2; matrix products, arithmetic and copies ran while one was open for 0% -> 0% of each run, Pallas kernels for 0% -> 7%
where the time goes in v4:
time: 62.2 us; the launch traced here: 62 us
  blocking collectives  19.4 us (31%)
  starting transfers between devices  17.6 us (28%)
  Pallas kernels  13.1 us (21%)
  waiting for transfers between devices  11 us (18%)
  between operations  0.75 us (1%)
    pallas_call x7, Pallas kernels, call(): pl.pallas_call(kernel, out_shape=outs if multiple else outs[0], in_specs=...  13.1 us
    all_to_all x1, starting transfers between devices, on_device(): lax.all_to_all(planes.reshape(n_gy, 4 * per, LANES), 'gy', split_axis=0,...  11.9 us
    all_gather x1, blocking collectives, on_device(): beyond = lax.all_gather(chip, 'gx', axis_index_groups=between)  7.82 us
    all_to_all x1, waiting for transfers between devices, on_device(): lax.all_to_all(planes.reshape(n_gy, 4 * per, LANES), 'gy', split_axis=0,...  7.39 us
    all_gather x1, blocking collectives, on_device(): pair = lax.all_gather(block, 'gx', axis_index_groups=chips)  6.57 us
    all_gather x1, blocking collectives, on_device(): relay = lax.all_gather(relay, 'gx', axis_index_groups=chips)  5.04 us
    ppermute x1, starting transfers between devices, on_device(): from_left = lax.ppermute(up, 'gy', onward)  4.37 us
    ppermute x1, waiting for transfers between devices, on_device(): from_right = lax.ppermute(dn, 'gy', back)  3.61 us
  transfers between devices with their start and end apart: 3, of which 2 were waited for; matrix products, arithmetic and copies ran while one was open for 0% of the time, Pallas kernels for 7%

profile of v4, /device:TPU:1, one launch (start us, length us, event | category | flops | bytes accessed | tf_op | source)
XLA Modules:
  0.0 62.0 jit_solution(14364530876315985536)
XLA Ops:
  0.6 0.0 copy-start
  0.6 2.5 %shard_map.50 = (f32[16,32,128]{2,1,0:T(8,128)S(1)}, f32[16,32,128]{2,1,0:T(8,128)S(1)}, f32[8,16,128]{2,1,0:T(8,128)S(1)}, f32[96,128]{1,0:T(8,128)S(1)}, f32[96,128]{1,0:T(8,128)S(1)}) custom-call(f32[16,32,128]{2,1,0:T(8,128)} %it.3, f32[16,32,128]{2,1,0:T(8,128)} %src_in.1, s32[16,32,128]{2,1,0:T(8,128)} %lab_in.1), custom_call_target="tpu_custom_call" | custom-call | flops 1000000 | bytes 1474560 | tf_op jit(solution)/shard_map/pallas_call | solution.py:434
  3.2 4.4 %collective-permute-start = (f32[96,128]{1,0:T(8,128)S(1)}, f32[96,128]{1,0:T(8,128)S(1)}, u32[]{:S(2)}, u32[]{:S(2)}) collective-permute-start(f32[96,128]{1,0:T(8,128)S(1)} %get-tuple-element.13.ou), channel_id=1, source_target_pairs={{0,1},{1,2},{2,3},{3,4},{4,5},{5,6},{6,7},{7,8},{8,9},{9,10},{10,1... | collective-permute-start | bytes 147464 | tf_op jit(solution)/shard_map/ppermute | solution.py:467
  7.5 1.3 %collective-permute-start.1 = (f32[96,128]{1,0:T(8,128)S(1)}, f32[96,128]{1,0:T(8,128)S(1)}, u32[]{:S(2)}, u32[]{:S(2)}) collective-permute-start(f32[96,128]{1,0:T(8,128)S(1)} %get-tuple-element.14.od), channel_id=1, source_target_pairs={{1,0},{2,1},{3,2},{4,3},{5,4},{6,5},{7,6},{8,7},{9,8},{10,9},{11,1... | collective-permute-start | bytes 147464 | tf_op jit(solution)/shard_map/ppermute | solution.py:468
  8.9 0.1 stack.39.flags
  9.0 0.0 collective-permute-done.ru
  9.0 3.6 %collective-permute-done.1.rd = f32[96,128]{1,0:T(8,128)S(1)} collective-permute-done((f32[96,128]{1,0:T(8,128)S(1)}, f32[96,128]{1,0:T(8,128)S(1)}, u32[]{:S(2)}, u32[]{:S(2)}) %collective-permute-start.1) | collective-permute-done | bytes 49184 | tf_op jit(solution)/shard_map/ppermute | solution.py:468
  12.6 0.0 copy-done
  12.6 0.8 %shard_map.51 = (f32[512,128]{1,0:T(8,128)S(1)}, f32[320,128]{1,0:T(8,128)S(1)}) custom-call(s32[5]{0:T(128)S(1)} %stack.39.flags, f32[16,32,128]{2,1,0:T(8,128)S(1)} %copy-done, f32[16,32,128]{2,1,0:T(8,128)S(1)} %get-tuple-element.11.r_in, f32[16,32,128]{2,1,0:T(8,128)S(1)} %get-tuple-element.12.k_in, f32[8,16,128]{2,1,0:T(8,128)S(1)} %get-tuple-element.15.c_ref, ...), custom_call_target="tpu_custom_call" | custom-call | flops 1000000 | bytes 1474580 | tf_op jit(solution)/shard_map/pallas_call | solution.py:434
  13.4 6.6 %all-gather = f32[1024,128]{1,0:T(8,128)S(1)} all-gather(f32[512,128]{1,0:T(8,128)S(1)} %get-tuple-element.16), channel_id=2, replica_groups={{0,16},{32,48},{64,80},{96,112},{128,144},{160,176},{192,208},{224,240}..., dimensions={0}, use_global_device_ids=true | all-gather | bytes 786432 | tf_op jit(solution)/shard_map/all_gather | solution.py:477
  20.0 0.3 shard_map.52.chip
  20.4 7.8 %all-gather.1 = f32[1408,128]{1,0:T(8,128)S(1)} all-gather(f32[704,128]{1,0:T(8,128)S(1)} %shard_map.52.chip), channel_id=3, replica_groups={{16,32},{48,64},{80,96},{112,128},{144,160},{176,192},{208,224},{240,25..., dimensions={0}, use_global_device_ids=true | all-gather | bytes 1081344 | tf_op jit(solution)/shard_map/all_gather | solution.py:479
  28.2 0.8 %shard_map.53 = f32[208,128]{1,0:T(8,128)S(1)} custom-call(s32[5]{0:T(128)S(1)} %stack.39.flags, f32[2,704,128]{2,1,0:T(8,128)S(1)} %bitcast.11), custom_call_target="tpu_custom_call" | custom-call | flops 1000000 | bytes 827412 | tf_op jit(solution)/shard_map/pallas_call | solution.py:434
  29.0 5.0 %all-gather.2 = f32[416,128]{1,0:T(8,128)S(1)} all-gather(f32[208,128]{1,0:T(8,128)S(1)} %shard_map.53), channel_id=4, replica_groups={{0,16},{32,48},{64,80},{96,112},{128,144},{160,176},{192,208},{224,240}..., dimensions={0}, use_global_device_ids=true | all-gather | bytes 319488 | tf_op jit(solution)/shard_map/all_gather | solution.py:481
  34.0 3.9 %shard_map.54 = (f32[8,16,128]{2,1,0:T(8,128)S(1)}, f32[64,128]{1,0:T(8,128)}) custom-call(s32[5]{0:T(128)S(1)} %stack.39.flags, f32[704,128]{1,0:T(8,128)S(1)} %shard_map.52.chip, f32[2,704,128]{2,1,0:T(8,128)S(1)} %bitcast.12, f32[2,208,128]{2,1,0:T(8,128)S(1)} %bitcast.16), custom_call_target="tpu_custom_call" | custom-call | flops 1000000 | bytes 1392660 | tf_op jit(solution)/shard_map/pallas_call | solution.py:434
  37.9 11.9 %all-to-all-start = ((f32[16,4,128]{2,1,0:T(4,128)}), f32[16,4,128]{2,1,0:T(4,128)S(1)}, u32[]{:S(2)}, u32[]{:S(2)}) async-start(f32[16,4,128]{2,1,0:T(4,128)} %bitcast.8), calls=%async_computation | async-start | bytes 65536 | tf_op jit(solution)/shard_map/all_to_all | solution.py:491
  49.8 4.1 %shard_map.55 = f32[16,32,128]{2,1,0:T(8,128)} custom-call(s32[5]{0:T(128)S(1)} %stack.39.flags, f32[16,32,128]{2,1,0:T(8,128)S(1)} %copy-done, f32[16,32,128]{2,1,0:T(8,128)S(1)} %get-tuple-element.11.r_in, f32[16,32,128]{2,1,0:T(8,128)S(1)} %get-tuple-element.12.k_in, f32[96,128]{1,0:T(8,128)S(1)} %get-tuple-element.13.ou, ...), custom_call_target="tpu_custom_call" | custom-call | flops 20000000 | bytes 2555924 | tf_op jit(solution)/shard_map/pallas_call | solution.py:434
  53.9 7.4 %all-to-all-done = f32[16,4,128]{2,1,0:T(4,128)S(1)} async-done(((f32[16,4,128]{2,1,0:T(4,128)}), f32[16,4,128]{2,1,0:T(4,128)S(1)}, u32[]{:S(2)}, u32[]{:S(2)}) %all-to-all-start) | async-done | bytes 32800 | tf_op jit(solution)/shard_map/all_to_all | solution.py:491
  61.3 0.7 %shard_map.56 = f32[64,128]{1,0:T(8,128)} custom-call(f32[64,128]{1,0:T(8,128)S(1)} %bitcast.17), custom_call_target="tpu_custom_call" | custom-call | flops 1000000 | bytes 65536 | tf_op jit(solution)/shard_map/pallas_call | solution.py:434
Async XLA Ops:
  0.6 11.9 %copy-start = (f32[16,32,128]{2,1,0:T(8,128)S(1)}, f32[16,32,128]{2,1,0:T(8,128)}, u32[]{:S(2)}) copy-start(f32[16,32,128]{2,1,0:T(8,128)} %it.3) | copy-start | bytes 786436
  3.2 5.8 %collective-permute-start = (f32[96,128]{1,0:T(8,128)S(1)}, f32[96,128]{1,0:T(8,128)S(1)}, u32[]{:S(2)}, u32[]{:S(2)}) collective-permute-start(f32[96,128]{1,0:T(8,128)S(1)} %get-tuple-element.13.ou), channel_id=1, source_target_pairs={{0,1},{1,2},{2,3},{3,4},{4,5},{5,6},{6,7},{7,8},{8,9},{9,10},{10,1... | collective-permute-start | bytes 147464 | tf_op jit(solution)/shard_map/ppermute | solution.py:467
  7.5 5.0 %collective-permute-start.1 = (f32[96,128]{1,0:T(8,128)S(1)}, f32[96,128]{1,0:T(8,128)S(1)}, u32[]{:S(2)}, u32[]{:S(2)}) collective-permute-start(f32[96,128]{1,0:T(8,128)S(1)} %get-tuple-element.14.od), channel_id=1, source_target_pairs={{1,0},{2,1},{3,2},{4,3},{5,4},{6,5},{7,6},{8,7},{9,8},{10,9},{11,1... | collective-permute-start | bytes 147464 | tf_op jit(solution)/shard_map/ppermute | solution.py:468
  37.9 23.4 %all-to-all-start = ((f32[16,4,128]{2,1,0:T(4,128)}), f32[16,4,128]{2,1,0:T(4,128)S(1)}, u32[]{:S(2)}, u32[]{:S(2)}) async-start(f32[16,4,128]{2,1,0:T(4,128)} %bitcast.8), calls=%async_computation | async-start | bytes 65536 | tf_op jit(solution)/shard_map/all_to_all | solution.py:491

commit v5 on v4

--- a/solution.py
+++ b/solution.py
@@ -22,6 +22,9 @@
 OWN = CROWS * CZ
 BLOCK = OWN + 4 * CZ
 NEAR = 10 * NZ
+STRIP = 3 * NZ
+UP, DN, FACING = OWN, OWN + STRIP, OWN + 2 * STRIP
+SHARED = FACING + 8 * NZ
 PARTS = 4
 
 
@@ -63,7 +66,7 @@
     return jnp.dot(a, b, precision=lax.Precision.HIGHEST, preferred_element_type=F32)
 
 
-def residual_kernel(it_in, src_in, lab_in, r_ref, k_ref, c_ref, up_ref, dn_ref, pool, it, src, lab, sems):
+def residual_kernel(flags, it_in, src_in, lab_in, r_ref, k_ref, a_ref, pool, it, src, lab, sems):
     copies = []
     for part in range(PARTS):
         rows = pl.ds(part * ROWS // PARTS, ROWS // PARTS)
@@ -112,22 +115,22 @@
         bottom = jnp.where(lane < 4, k, jnp.where(lane < 7, roll(r, 4, 1), roll(v, 7, 1)))
         up = jnp.where(here, roll(top, off - 120, 1), up)
         dn = jnp.where(here, roll(bottom, off, 1), dn)
-    up_ref[0:NZ] = up
-    dn_ref[0:NZ] = dn
+    a_ref[UP:UP + NZ] = up
+    a_ref[DN:DN + NZ] = dn
     up = dn = zero
     for g, edge in enumerate((k_ref[0], it[0], k_ref[ROWS - 1], it[ROWS - 1])):
         here = (lane >= 32 * g) & (lane < 32 * g + 32)
         up = jnp.where(here, roll(edge, 32 * g - 96, 1), up)
         dn = jnp.where(here, roll(edge, 32 * g, 1), dn)
-    up_ref[NZ:2 * NZ] = up
-    dn_ref[NZ:2 * NZ] = dn
+    a_ref[UP + NZ:UP + 2 * NZ] = up
+    a_ref[DN + NZ:DN + 2 * NZ] = dn
     tops = pool[:, :, pl.ds(0, CZ, stride=2), :] + pool[:, :, pl.ds(1, CZ, stride=2), :]
     child, parent = iota((LANES, LANES), 0) // 2, iota((LANES, LANES), 1)
     to_left = jnp.where(child == parent, F32(1.0), F32(0.0))
     to_right = jnp.where(child == parent - CLANES, F32(0.125), F32(0.0))
     coarse = dot(tops[0].reshape(CROWS * CZ, LANES), to_left) + dot(tops[1].reshape(CROWS * CZ, LANES), to_right)
+    a_ref[0:OWN] = coarse
     coarse = coarse.reshape(CROWS, CZ, LANES)
-    c_ref[...] = coarse
     lane = iota((CZ, LANES), 1)
     for t in range(2):
         up = dn = jnp.zeros((CZ, LANES), F32)
@@ -138,8 +141,14 @@
             at_k = (lane >= off + 16) & (lane < off + 32)
             up = jnp.where(at_r, roll(row, off - 48, 1), jnp.where(at_k, roll(row, off + 16 - 112, 1), up))
             dn = jnp.where(at_r, roll(row, off, 1), jnp.where(at_k, roll(row, off + 16 - 64, 1), dn))
-        up_ref[2 * NZ + CZ * t:2 * NZ + CZ * (t + 1)] = up
-        dn_ref[2 * NZ + CZ * t:2 * NZ + CZ * (t + 1)] = dn
+        a_ref[UP + 2 * NZ + CZ * t:UP + 2 * NZ + CZ * (t + 1)] = up
+        a_ref[DN + 2 * NZ + CZ * t:DN + 2 * NZ + CZ * (t + 1)] = dn
+    first = flags[0] == 0
+    rows = [jnp.where(first, k_ref[ROWS - 4 + t], k_ref[t]) for t in range(4)]
+    rows += [jnp.where(first, r_ref[ROWS - 3 + t], r_ref[t]) for t in range(3)]
+    rows.append(jnp.where(first, it[ROWS - 1], it[0]))
+    for t in range(8):
+        a_ref[FACING + NZ * t:FACING + NZ * (t + 1)] = rows[t]
 
 
 def strip_flux(up, dn):
@@ -148,52 +157,38 @@
     return jnp.where(lane % 8 == 0, face, 0.0)
 
 
+def came(flags, strips, n, start, rows):
+    at = slice(STRIP * n + start, STRIP * n + start + rows)
+    rd = strips[flags[5], at] * flags[7].astype(F32)
+    return rd, strips[1 - flags[5], at] * flags[6].astype(F32)
+
+
 def completed(ou, od, ru, rd):
-    right = strip_flux(ou[0:NZ], rd[0:NZ])
-    left = strip_flux(ru[0:NZ], od[0:NZ])
-    return rd[0:NZ] + roll(right, 4, 1), ru[0:NZ] - roll(left, 3, 1), right, left
-
-
-def block_kernel(flags, it, r_in, k_in, c_ref, ou, od, ru, rd, m_ref, n_ref, pool):
-    dn, up, right, left = completed(ou, od, ru, rd)
-    pool[0] = right + roll(right, -8, 1)
-    pool[1] = left + roll(left, -8, 1)
-    sums = pool[:, pl.ds(0, CZ, stride=2), :] + pool[:, pl.ds(1, CZ, stride=2), :]
-    lane = iota((CZ, LANES), 1)
-    for j in range(CROWS):
-        value = c_ref[j] - jnp.where(lane == 63, roll(sums[0], 63 - 16 * j, 1), 0.0)
-        m_ref[CZ * j:CZ * (j + 1)] = value + jnp.where(lane == 0, roll(sums[1], -16 * j, 1), 0.0)
-    for t in range(2):
-        at = slice(2 * NZ + CZ * t, 2 * NZ + CZ * (t + 1))
-        more, less = rd[at], ru[at]
-        for q in range(4):
-            src = 16 * (4 * t + q)
-            more = more + jnp.where(lane == 32 * q, roll(sums[0], 32 * q - src, 1), 0.0)
-            less = less - jnp.where(lane == 32 * q + 15, roll(sums[1], 32 * q + 15 - src, 1), 0.0)
-        m_ref[OWN + CZ * t:OWN + CZ * (t + 1)] = more
-        m_ref[OWN + CZ * (2 + t):OWN + CZ * (3 + t)] = less
+    right = strip_flux(ou, rd)
+    left = strip_flux(ru, od)
+    return rd + roll(right, 4, 1), ru - roll(left, 3, 1), right, left
+
+
+def beside_rows(flags, strips, n, ks, rs, v, done, top):
     lane = iota((NZ, LANES), 1)
-    first = flags[0] == 0
-
-    def near(base, top):
-        tiles = []
-        k_row, r_row, v_row = (12, 13, 15) if top else (0, 0, 0)
-        for t in range(4):
-            tiles.append(k_in[k_row + t])
-        for t in range(3):
-            i = r_row + t
-            r = r_in[i] - jnp.where(lane == 127, roll(right, 127 - 8 * i, 1), 0.0)
-            tiles.append(r + jnp.where(lane == 0, roll(left, -8 * i, 1), 0.0))
-        tiles.append(it[v_row])
-        tiles.append(jnp.where(lane < 32, roll(dn, -8 * k_row, 1), roll(up, 32 - 8 * k_row, 1)))
-        shift = 64 if top else 0
-        tiles.append(jnp.where(lane < 64, roll(rd[NZ:2 * NZ], -shift, 1), roll(ru[NZ:2 * NZ], 64 - shift, 1)))
-        return tiles
-
-    low, high = near(0, False), near(0, True)
-    for t in range(10):
-        m_ref[BLOCK + NZ * t:BLOCK + NZ * (t + 1)] = jnp.where(first, high[t], low[t])
-        n_ref[NZ * t:NZ * (t + 1)] = jnp.where(first, low[t], high[t])
+    dn, up, right, left = done
+    k_row, r_row = (ROWS - 4, ROWS - 3) if top else (0, 0)
+    tiles = list(ks)
+    for t in range(3):
+        i = r_row + t
+        r = rs[t] - jnp.where(lane == 127, roll(right, 127 - 8 * i, 1), 0.0)
+        tiles.append(r + jnp.where(lane == 0, roll(left, -8 * i, 1), 0.0))
+    tiles.append(v)
+    tiles.append(jnp.where(lane < 32, roll(dn, -8 * k_row, 1), roll(up, 32 - 8 * k_row, 1)))
+    tiles.append(outermost(flags, strips, n, top))
+    return tiles
+
+
+def outermost(flags, strips, n, top):
+    lane = iota((NZ, LANES), 1)
+    shift = 64 if top else 0
+    rd, ru = came(flags, strips, n, NZ, NZ)
+    return jnp.where(lane < 64, roll(rd, -shift, 1), roll(ru, 64 - shift, 1))
 
 
 def edge_flux(a, b, pool):
@@ -209,14 +204,45 @@
     return dot(sums[0], own) + dot(sums[1], beyond)
 
 
-def chip_kernel(pair, near, o_ref, pool):
+def chip_kernel(flags, it, r_in, k_in, pair, strips, o_ref, pool):
+    first = flags[0] == 0
+    lane = iota((CZ, LANES), 1)
+    nears = []
+    for n in range(2):
+        rd, ru = came(flags, strips, n, 0, NZ)
+        done = completed(pair[n, UP:UP + NZ], pair[n, DN:DN + NZ], ru, rd)
+        pool[0] = done[2] + roll(done[2], -8, 1)
+        pool[1] = done[3] + roll(done[3], -8, 1)
+        sums = pool[:, pl.ds(0, CZ, stride=2), :] + pool[:, pl.ds(1, CZ, stride=2), :]
+        base = BLOCK * n
+        for j in range(CROWS):
+            value = pair[n, CZ * j:CZ * (j + 1)] - jnp.where(lane == 63, roll(sums[0], 63 - 16 * j, 1), 0.0)
+            value = value + jnp.where(lane == 0, roll(sums[1], -16 * j, 1), 0.0)
+            o_ref[base + CZ * j:base + CZ * (j + 1)] = value
+        for t in range(2):
+            more, less = came(flags, strips, n, 2 * NZ + CZ * t, CZ)
+            for q in range(4):
+                src = 16 * (4 * t + q)
+                more = more + jnp.where(lane == 32 * q, roll(sums[0], 32 * q - src, 1), 0.0)
+                less = less - jnp.where(lane == 32 * q + 15, roll(sums[1], 32 * q + 15 - src, 1), 0.0)
+            o_ref[base + OWN + CZ * t:base + OWN + CZ * (t + 1)] = more
+            o_ref[base + OWN + CZ * (2 + t):base + OWN + CZ * (3 + t)] = less
+        k_row, r_row, v_row = (ROWS - 4, ROWS - 3, ROWS - 1) if n else (0, 0, 0)
+        ks = [k_in[k_row + t] for t in range(4)]
+        rs = [r_in[r_row + t] for t in range(3)]
+        nears.append(beside_rows(flags, strips, n, ks, rs, it[v_row], done, n == 1))
+    for t in range(10):
+        o_ref[2 * BLOCK + NZ * t:2 * BLOCK + NZ * (t + 1)] = jnp.where(first, nears[0][t], nears[1][t])
+
     def tile(n):
-        return lambda t: pair[n, BLOCK + NZ * t:BLOCK + NZ * (t + 1)]
+        def get(t):
+            if t == 9:
+                return outermost(flags, strips, n, n == 0)
+            return pair[n, FACING + NZ * t:FACING + NZ * (t + 1)]
+
+        return get
 
     inner = edge_flux(tile(0), tile(1), pool)
-    for n in range(2):
-        o_ref[BLOCK * n:BLOCK * (n + 1)] = pair[n, 0:BLOCK]
-    lane = iota((CZ, LANES), 1)
     for n, j in ((0, CROWS - 1), (1, 0)):
         change = inner if n else -inner
         off = 32 * (j % 4)
@@ -227,8 +253,8 @@
             (OWN + CZ * (2 + j // 4), jnp.where(side, roll(change, off - 112, 1), 0.0)),
         )
         for at, part in changes:
-            o_ref[BLOCK * n + at:BLOCK * n + at + CZ] = pair[n, at:at + CZ] + part
-    o_ref[2 * BLOCK:] = near[...]
+            at = BLOCK * n + at
+            o_ref[at:at + CZ] = o_ref[at:at + CZ] + part
 
 
 def relay_kernel(flags, out, o_ref, pool):
@@ -331,11 +357,19 @@
     sweep(1, CEXT - 1, CROWS, COARSE_SWEEPS, COARSE_SWEEPS, r_s, s_s, x_s, c_s, 0)
 
 
-def fine_part(flags, it, r_in, k_in, pair, out, ou, od, ru, rd, x_s, k_s, r_s, s_s, c_s):
+def fine_part(flags, it, r_in, k_in, pair, strips, out, x_s, k_s, r_s, s_s, c_s):
     first = flags[0] == 0
     low, high = flags[1].astype(F32), flags[2].astype(F32)
     lane = iota((NZ, LANES), 1)
-    dn, up, right, left = completed(ou, od, ru, rd)
+    facing = []
+    for n in range(2):
+        rd, ru = came(flags, strips, n, 0, NZ)
+        done = completed(pair[n, UP:UP + NZ], pair[n, DN:DN + NZ], ru, rd)
+        rows = [pair[n, FACING + NZ * t:FACING + NZ * (t + 1)] for t in range(8)]
+        facing.append(beside_rows(flags, strips, n, rows[0:4], rows[4:7], rows[7], done, n == 0))
+    mine = flags[0]
+    rd, ru = (jnp.where(first, a, b) for a, b in zip(came(flags, strips, 0, 0, NZ), came(flags, strips, 1, 0, NZ)))
+    dn, up, right, left = completed(pair[mine, UP:UP + NZ], pair[mine, DN:DN + NZ], ru, rd)
 
     def beside(rights, lefts, count):
         return jnp.where(lane < count, rights, jnp.where(lane >= LANES - count, lefts, 0.0))
@@ -351,14 +385,13 @@
         r = r_in[i] - jnp.where(lane == 127, roll(right, 127 - off, 1), 0.0)
         r_s[e, :, 0:LANES] = r + jnp.where(lane == 0, roll(left, -off, 1), 0.0)
         r_s[e, :, LANES:] = beside(roll(dn, -off - 4, 1), roll(up, 124 - off, 1), 3)
-    edges = rd[NZ:2 * NZ], ru[NZ:2 * NZ]
+    edges = [jnp.where(first, a, b) for a, b in zip(came(flags, strips, 0, NZ, NZ), came(flags, strips, 1, NZ, NZ))]
     for side in range(2):
         def tile(t, side=side):
             at = slice(2 * BLOCK + NZ * t, 2 * BLOCK + NZ * (t + 1))
-            by = slice(BLOCK + NZ * t, BLOCK + NZ * (t + 1))
             if side == 0:
-                return jnp.where(first, out[0, at], pair[0, by]) * low
-            return jnp.where(first, pair[1, by], out[1, at]) * high
+                return jnp.where(first, out[0, at], facing[0][t]) * low
+            return jnp.where(first, facing[1][t], out[1, at]) * high
 
         base = 0 if side == 0 else HALO + ROWS
         halo, face = tile(8), tile(9)
@@ -395,9 +428,9 @@
 
 
 def fine_kernel(
-    flags, it, r_in, k_in, ou, od, ru, rd, pair, out, x_c, o_ref, x_f, k_f, r_f, s_f, c_f, wide_s
+    flags, it, r_in, k_in, pair, strips, out, x_c, o_ref, x_f, k_f, r_f, s_f, c_f, wide_s
 ):
-    fine_part(flags, it, r_in, k_in, pair, out, ou, od, ru, rd, x_f, k_f, r_f, s_f, c_f)
+    fine_part(flags, it, r_in, k_in, pair, strips, out, x_f, k_f, r_f, s_f, c_f)
     child, parent = iota((LANES, LANES), 1) // 2, iota((LANES, LANES), 0)
     spread = jnp.where(child == parent, F32(1.0), F32(0.0))
     wide = dot(x_c[...].reshape(CROWS * CZ, LANES), spread).reshape(CROWS, CZ, LANES)
@@ -429,8 +462,8 @@
     multiple = len(outs) > 1
     held = [pltpu.VMEM(s, F32) for s in scratch]
     if copies:
-        held += [pltpu.VMEM(x.shape, x.dtype) for x in operands]
-        held.append(pltpu.SemaphoreType.DMA((len(operands), PARTS)))
+        held += [pltpu.VMEM(x.shape, x.dtype) for x in operands[1:]]
+        held.append(pltpu.SemaphoreType.DMA((len(operands) - 1, PARTS)))
     return pl.pallas_call(
         kernel,
         out_shape=outs if multiple else outs[0],
@@ -449,33 +482,35 @@
 def on_device(iterate, source, labels):
     n_gx, n_gy = lax.axis_size("gx"), lax.axis_size("gy")
     gx = lax.axis_index("gx")
-    flags = jnp.stack([gx % 2, gx > 0, gx < n_gx - 1, gx > 1, gx < n_gx - 2]).astype(jnp.int32)
+    gy = lax.axis_index("gy")
+    flags = [gx % 2, gx > 0, gx < n_gx - 1, gx > 1, gx < n_gx - 2, gy % 2, gy > 0, gy < n_gy - 1]
+    flags = jnp.stack([jnp.int32(f) for f in flags])
     chips = [[i, i + 1] for i in range(0, n_gx, 2)]
     between = [[i, (i + 1) % n_gx] for i in range(1, n_gx, 2)]
+    along = [
+        [i * n_gy + j, i * n_gy + (j + 1) % n_gy] for i in range(n_gx) for j in range(i % 2, n_gy, 2)
+    ]
     own = shape(ROWS, NZ, LANES)
-    strip = shape(3 * NZ, LANES)
-    resid, cond, coarse, up, dn = call(
+    resid, cond, shared = call(
         residual_kernel,
-        [own, own, shape(CROWS, CZ, LANES), strip, strip],
+        [own, own, shape(SHARED, LANES)],
         [(2, CROWS, NZ, LANES)],
-        False,
-        (iterate, source, labels),
+        True,
+        (flags, iterate, source, labels),
         copies=True,
     )
-    onward = [(i, i + 1) for i in range(n_gy - 1)]
-    back = [(i + 1, i) for i in range(n_gy - 1)]
-    from_left = lax.ppermute(up, "gy", onward)
-    from_right = lax.ppermute(dn, "gy", back)
-    strips = (up, dn, from_left, from_right)
-    block, near = call(
-        block_kernel,
-        [shape(BLOCK + NEAR, LANES), shape(NEAR, LANES)],
+    pair = lax.all_gather(shared, "gx", axis_index_groups=chips)
+    lower = (gx + gy) % 2 == 0
+    strips = jnp.where(lower, pair[:, UP:DN], pair[:, DN:FACING]).reshape(2 * STRIP, LANES)
+    strips = lax.all_gather(strips, ("gx", "gy"), axis_index_groups=along)
+    strips = lax.all_gather(jnp.where(lower, strips[1], strips[0]), "gx", axis_index_groups=chips)
+    chip = call(
+        chip_kernel,
+        [shape(2 * BLOCK + NEAR, LANES)],
         [(2, NZ, LANES)],
         True,
-        (flags, iterate, resid, cond, coarse, *strips),
+        (flags, iterate, resid, cond, pair, strips),
     )
-    pair = lax.all_gather(block, "gx", axis_index_groups=chips)
-    chip = call(chip_kernel, [shape(2 * BLOCK + NEAR, LANES)], [(2, NZ, LANES)], False, (pair, near))
     beyond = lax.all_gather(chip, "gx", axis_index_groups=between)
     relay = call(relay_kernel, [shape(BLOCK + CZ, LANES)], [(2, NZ, LANES)], True, (flags, beyond))
     relay = lax.all_gather(relay, "gx", axis_index_groups=chips)
@@ -494,7 +529,7 @@
         [own],
         [(ROWS, NZ, LANES), wide, wide, wide, (6, *wide), (CROWS, NZ, LANES)],
         True,
-        (flags, iterate, resid, cond, *strips, pair, beyond, coarse_out),
+        (flags, iterate, resid, cond, pair, strips, beyond, coarse_out),
         flops=20000000,
     )
     owned = call(

time: 62.2 us -> 61.4 us (0.987)
  blocking collectives: 19.4 us -> 30.3 us
  starting transfers between devices: 17.6 us -> 8.45 us
  waiting for transfers between devices: 11 us -> 7.22 us
  Pallas kernels: 13.1 us -> 14.3 us
    all_gather x1 -> x3, blocking collectives: 6.57 us -> 17.5 us  [the longest x1 8.94 us: on_device(): pair = lax.all_gather(shared, 'gx', axis_index_groups=chips)]
    ppermute x2 -> x0, starting transfers between devices: 5.67 us -> none  [the longest x1 4.37 us: on_device(): from_left = lax.ppermute(up, 'gy', onward)]
    ppermute x2 -> x0, waiting for transfers between devices: 3.61 us -> none  [the longest x1 3.61 us: on_device(): from_right = lax.ppermute(dn, 'gy', back)]
    all_to_all x1, starting transfers between devices: 11.9 us -> 8.45 us  [on_device(): lax.all_to_all(planes.reshape(n_gy, 4 * per, LANES), 'gy', split_axis=0,...]
    pallas_call x7 -> x6, Pallas kernels: 13.1 us -> 14.3 us  [call(): pl.pallas_call(kernel, out_shape=outs if multiple else outs[0], in_specs=...]
  transfers between devices with their start and end apart: 3 -> 1, of which waited for: 2 -> 1; matrix products, arithmetic and copies ran while one was open for 0% -> 0% of each run, Pallas kernels for 7% -> 7%
where the time goes in v5:
time: 61.4 us; the launch traced here: 61.1 us
  blocking collectives  30.3 us (49%)
  Pallas kernels  14.3 us (23%)
  starting transfers between devices  8.45 us (14%)
  waiting for transfers between devices  7.22 us (12%)
  between operations  0.71 us (1%)
    pallas_call x6, Pallas kernels, call(): pl.pallas_call(kernel, out_shape=outs if multiple else outs[0], in_specs=...  14.3 us
    all_gather x1, blocking collectives, on_device(): pair = lax.all_gather(shared, 'gx', axis_index_groups=chips)  8.94 us
    all_to_all x1, starting transfers between devices, on_device(): lax.all_to_all(planes.reshape(n_gy, 4 * per, LANES), 'gy', split_axis=0,...  8.45 us
    all_gather x1, blocking collectives, on_device(): beyond = lax.all_gather(chip, 'gx', axis_index_groups=between)  7.82 us
    all_to_all x1, waiting for transfers between devices, on_device(): lax.all_to_all(planes.reshape(n_gy, 4 * per, LANES), 'gy', split_axis=0,...  7.22 us
    all_gather x1, blocking collectives, on_device(): strips = lax.all_gather(strips, ('gx', 'gy'), axis_index_groups=along)  6.5 us
    all_gather x1, blocking collectives, on_device(): relay = lax.all_gather(relay, 'gx', axis_index_groups=chips)  4.93 us
    all_gather x1, blocking collectives, on_device(): lax.all_gather(jnp.where(lower, strips[1], strips[0]), 'gx', axis_index_g...  2.08 us
  transfers between devices with their start and end apart: 1, of which 1 were waited for; matrix products, arithmetic and copies ran while one was open for 0% of the time, Pallas kernels for 7%

profile of v5, /device:TPU:1, one launch (start us, length us, event | category | flops | bytes accessed | tf_op | source)
XLA Modules:
  0.0 61.1 jit_solution(10476774814918500059)
XLA Ops:
  0.7 0.1 stack.59.flags
  0.8 3.7 %shard_map.50 = (f32[16,32,128]{2,1,0:T(8,128)S(1)}, f32[16,32,128]{2,1,0:T(8,128)S(1)}, f32[576,128]{1,0:T(8,128)}) custom-call(s32[8]{0:T(128)S(1)} %stack.59.flags, f32[16,32,128]{2,1,0:T(8,128)} %it.3, f32[16,32,128]{2,1,0:T(8,128)} %src_in.1, s32[16,32,128]{2,1,0:T(8,128)} %lab_in.1), custom_call_target="tpu_custom_call" | custom-call | flops 1000000 | bytes 1605664 | tf_op jit(solution)/shard_map/pallas_call | solution.py:467
  4.5 8.9 %all-gather = f32[1152,128]{1,0:T(8,128)S(1)} all-gather(f32[576,128]{1,0:T(8,128)} %get-tuple-element.9), channel_id=2, replica_groups={{0,16},{32,48},{64,80},{96,112},{128,144},{160,176},{192,208},{224,240}..., dimensions={0}, use_global_device_ids=true | all-gather | bytes 884736 | tf_op jit(solution)/shard_map/all_gather | solution.py:502
  13.5 6.5 %all_gather.27 = f32[2,192,128]{2,1,0:T(8,128)S(1)} all-gather(f32[1,192,128]{2,1,0:T(8,128)S(1)} %bitcast.23), channel_id=1, replica_groups={{0,1},{2,3},{4,5},{6,7},{8,9},{10,11},{12,13},{14,15},{17,18},{19,20},{..., dimensions={0}, use_global_device_ids=true | all-gather | bytes 294912 | tf_op jit(solution)/shard_map/all_gather | solution.py:505
  20.0 0.0 copy-start
  20.0 2.1 %all_gather.28.strips = f32[2,192,128]{2,1,0:T(8,128)S(1)} all-gather(f32[1,192,128]{2,1,0:T(8,128)S(1)} %slice_select_fusion), channel_id=1, replica_groups={{0,16},{32,48},{64,80},{96,112},{128,144},{160,176},{192,208},{224,240}..., dimensions={0}, use_global_device_ids=true | all-gather | bytes 294912 | tf_op jit(solution)/shard_map/all_gather | solution.py:506
  22.1 0.0 copy-done
  22.1 1.0 %shard_map.51.chip = f32[704,128]{1,0:T(8,128)S(1)} custom-call(s32[8]{0:T(128)S(1)} %stack.59.flags, f32[16,32,128]{2,1,0:T(8,128)S(1)} %copy-done, f32[16,32,128]{2,1,0:T(8,128)S(1)} %get-tuple-element.7.r_in, f32[16,32,128]{2,1,0:T(8,128)S(1)} %get-tuple-element.8.k_in, f32[2,576,128]{2,1,0:T(8,128)S(1)} %bitcast.19, f32[2,192,128]{2,1,0:T(8,128)S(1)} %all_gather.28.strips), custom_call_target="tpu_custom_call" | custom-call | flops 1000000 | bytes 1933344 | tf_op jit(solution)/shard_map/pallas_call | solution.py:467
  23.1 7.8 %all-gather.1 = f32[1408,128]{1,0:T(8,128)S(1)} all-gather(f32[704,128]{1,0:T(8,128)S(1)} %shard_map.51.chip), channel_id=3, replica_groups={{16,32},{48,64},{80,96},{112,128},{144,160},{176,192},{208,224},{240,25..., dimensions={0}, use_global_device_ids=true | all-gather | bytes 1081344 | tf_op jit(solution)/shard_map/all_gather | solution.py:514
  30.9 0.8 %shard_map.52 = f32[208,128]{1,0:T(8,128)S(1)} custom-call(s32[8]{0:T(128)S(1)} %stack.59.flags, f32[2,704,128]{2,1,0:T(8,128)S(1)} %bitcast.15), custom_call_target="tpu_custom_call" | custom-call | flops 1000000 | bytes 827424 | tf_op jit(solution)/shard_map/pallas_call | solution.py:467
  31.7 4.9 %all-gather.2 = f32[416,128]{1,0:T(8,128)S(1)} all-gather(f32[208,128]{1,0:T(8,128)S(1)} %shard_map.52), channel_id=4, replica_groups={{0,16},{32,48},{64,80},{96,112},{128,144},{160,176},{192,208},{224,240}..., dimensions={0}, use_global_device_ids=true | all-gather | bytes 319488 | tf_op jit(solution)/shard_map/all_gather | solution.py:516
  36.6 3.9 %shard_map.53 = (f32[8,16,128]{2,1,0:T(8,128)S(1)}, f32[64,128]{1,0:T(8,128)}) custom-call(s32[8]{0:T(128)S(1)} %stack.59.flags, f32[704,128]{1,0:T(8,128)S(1)} %shard_map.51.chip, f32[2,704,128]{2,1,0:T(8,128)S(1)} %bitcast.16, f32[2,208,128]{2,1,0:T(8,128)S(1)} %bitcast.21), custom_call_target="tpu_custom_call" | custom-call | flops 1000000 | bytes 1392672 | tf_op jit(solution)/shard_map/pallas_call | solution.py:467
  40.4 8.4 %all-to-all-start = ((f32[16,4,128]{2,1,0:T(4,128)}), f32[16,4,128]{2,1,0:T(4,128)S(1)}, u32[]{:S(2)}, u32[]{:S(2)}) async-start(f32[16,4,128]{2,1,0:T(4,128)} %bitcast.12), calls=%async_computation | async-start | bytes 65536 | tf_op jit(solution)/shard_map/all_to_all | solution.py:526
  48.9 4.3 %shard_map.54 = f32[16,32,128]{2,1,0:T(8,128)} custom-call(s32[8]{0:T(128)S(1)} %stack.59.flags, f32[16,32,128]{2,1,0:T(8,128)S(1)} %copy-done, f32[16,32,128]{2,1,0:T(8,128)S(1)} %get-tuple-element.7.r_in, f32[16,32,128]{2,1,0:T(8,128)S(1)} %get-tuple-element.8.k_in, f32[2,576,128]{2,1,0:T(8,128)S(1)} %bitcast.20, f32[2,192,128]{2,1,0:T(8,128)S(1)} %all_gather.28.strips, ...), custom_call_target="tpu_custom_call" | custom-call | flops 20000000 | bytes 2621472 | tf_op jit(solution)/shard_map/pallas_call | solution.py:467
  53.2 7.2 %all-to-all-done = f32[16,4,128]{2,1,0:T(4,128)S(1)} async-done(((f32[16,4,128]{2,1,0:T(4,128)}), f32[16,4,128]{2,1,0:T(4,128)S(1)}, u32[]{:S(2)}, u32[]{:S(2)}) %all-to-all-start) | async-done | bytes 32800 | tf_op jit(solution)/shard_map/all_to_all | solution.py:526
  60.4 0.7 %shard_map.55 = f32[64,128]{1,0:T(8,128)} custom-call(f32[64,128]{1,0:T(8,128)S(1)} %bitcast.22), custom_call_target="tpu_custom_call" | custom-call | flops 1000000 | bytes 65536 | tf_op jit(solution)/shard_map/pallas_call | solution.py:467
  (2 shorter events, 0.0 us)
Async XLA Ops:
  20.0 2.1 %copy-start = (f32[16,32,128]{2,1,0:T(8,128)S(1)}, f32[16,32,128]{2,1,0:T(8,128)}, u32[]{:S(2)}) copy-start(f32[16,32,128]{2,1,0:T(8,128)} %it.3) | copy-start | bytes 786436
  40.4 19.9 %all-to-all-start = ((f32[16,4,128]{2,1,0:T(4,128)}), f32[16,4,128]{2,1,0:T(4,128)S(1)}, u32[]{:S(2)}, u32[]{:S(2)}) async-start(f32[16,4,128]{2,1,0:T(4,128)} %bitcast.12), calls=%async_computation | async-start | bytes 65536 | tf_op jit(solution)/shard_map/all_to_all | solution.py:526

commit v6 on v5

--- a/solution.py
+++ b/solution.py
@@ -453,19 +453,31 @@
             o_ref[to:to + half] = jnp.where(lane < CLANES, roll(even, CLANES, 1), odd)
 
 
-def call(kernel, outs, scratch, in_smem=False, operands=(), flops=1000000, copies=False):
+def place():
+    gx, gy = lax.axis_index("gx"), lax.axis_index("gy")
+    n_gx, n_gy = lax.axis_size("gx"), lax.axis_size("gy")
+    marks = [gx % 2, gx > 0, gx < n_gx - 1, gx > 1, gx < n_gx - 2, gy % 2, gy > 0, gy < n_gy - 1]
+    return [m.astype(jnp.int32) for m in marks]
+
+
+def call(kernel, outs, scratch, placed=False, operands=(), flops=1000000, copies=False):
     vmem = pl.BlockSpec(memory_space=pltpu.VMEM)
     specs = [pl.BlockSpec(memory_space=pltpu.HBM) if copies else vmem] * len(operands)
-    if in_smem:
-        specs[0] = pl.BlockSpec(memory_space=pltpu.SMEM)
     size = sum(4 * x.size for x in operands) + sum(4 * o.size for o in outs)
     multiple = len(outs) > 1
     held = [pltpu.VMEM(s, F32) for s in scratch]
     if copies:
-        held += [pltpu.VMEM(x.shape, x.dtype) for x in operands[1:]]
-        held.append(pltpu.SemaphoreType.DMA((len(operands) - 1, PARTS)))
+        held += [pltpu.VMEM(x.shape, x.dtype) for x in operands]
+        held.append(pltpu.SemaphoreType.DMA((len(operands), PARTS)))
+
+    def body(*refs):
+        if placed:
+            kernel(place(), *refs)
+        else:
+            kernel(*refs)
+
     return pl.pallas_call(
-        kernel,
+        body,
         out_shape=outs if multiple else outs[0],
         in_specs=specs,
         out_specs=[vmem] * len(outs) if multiple else vmem,
@@ -483,8 +495,6 @@
     n_gx, n_gy = lax.axis_size("gx"), lax.axis_size("gy")
     gx = lax.axis_index("gx")
     gy = lax.axis_index("gy")
-    flags = [gx % 2, gx > 0, gx < n_gx - 1, gx > 1, gx < n_gx - 2, gy % 2, gy > 0, gy < n_gy - 1]
-    flags = jnp.stack([jnp.int32(f) for f in flags])
     chips = [[i, i + 1] for i in range(0, n_gx, 2)]
     between = [[i, (i + 1) % n_gx] for i in range(1, n_gx, 2)]
     along = [
@@ -496,7 +506,7 @@
         [own, own, shape(SHARED, LANES)],
         [(2, CROWS, NZ, LANES)],
         True,
-        (flags, iterate, source, labels),
+        (iterate, source, labels),
         copies=True,
     )
     pair = lax.all_gather(shared, "gx", axis_index_groups=chips)
@@ -509,10 +519,10 @@
         [shape(2 * BLOCK + NEAR, LANES)],
         [(2, NZ, LANES)],
         True,
-        (flags, iterate, resid, cond, pair, strips),
+        (iterate, resid, cond, pair, strips),
     )
     beyond = lax.all_gather(chip, "gx", axis_index_groups=between)
-    relay = call(relay_kernel, [shape(BLOCK + CZ, LANES)], [(2, NZ, LANES)], True, (flags, beyond))
+    relay = call(relay_kernel, [shape(BLOCK + CZ, LANES)], [(2, NZ, LANES)], True, (beyond,))
     relay = lax.all_gather(relay, "gx", axis_index_groups=chips)
     rows, wide = (CEXT, CZ, LANES), (EXT, NZ, 2 * LANES)
     coarse_out, planes = call(
@@ -520,7 +530,7 @@
         [shape(CROWS, CZ, LANES), shape(4 * CZ, LANES)],
         [rows, rows, rows, (6, *rows)],
         True,
-        (flags, chip, beyond, relay),
+        (chip, beyond, relay),
     )
     per = CZ // n_gy
     planes = lax.all_to_all(planes.reshape(n_gy, 4 * per, LANES), "gy", split_axis=0, concat_axis=0, tiled=True)
@@ -529,7 +539,7 @@
         [own],
         [(ROWS, NZ, LANES), wide, wide, wide, (6, *wide), (CROWS, NZ, LANES)],
         True,
-        (flags, iterate, resid, cond, pair, strips, beyond, coarse_out),
+        (iterate, resid, cond, pair, strips, beyond, coarse_out),
         flops=20000000,
     )
     owned = call(

time: 61.4 us -> 59.1 us (0.963)
  Pallas kernels: 14.3 us -> 11.6 us
    pallas_call x6, Pallas kernels: 14.3 us -> 11.6 us  [call(): pl.pallas_call(body, out_shape=outs if multiple else outs[0], in_specs=sp...]
  transfers between devices with their start and end apart: 1 -> 1, of which waited for: 1 -> 1; matrix products, arithmetic and copies ran while one was open for 0% -> 0% of each run, Pallas kernels for 7% -> 6%
where the time goes in v6:
time: 59.1 us; the launch traced here: 58.8 us
  blocking collectives  30.2 us (51%)
  Pallas kernels  11.6 us (20%)
  starting transfers between devices  8.45 us (14%)
  waiting for transfers between devices  7.76 us (13%)
  between operations  0.68 us (1%)
    pallas_call x6, Pallas kernels, call(): pl.pallas_call(body, out_shape=outs if multiple else outs[0], in_specs=sp...  11.6 us
    all_gather x1, blocking collectives, on_device(): pair = lax.all_gather(shared, 'gx', axis_index_groups=chips)  8.95 us
    all_to_all x1, starting transfers between devices, on_device(): lax.all_to_all(planes.reshape(n_gy, 4 * per, LANES), 'gy', split_axis=0,...  8.45 us
    all_gather x1, blocking collectives, on_device(): beyond = lax.all_gather(chip, 'gx', axis_index_groups=between)  7.82 us
    all_to_all x1, waiting for transfers between devices, on_device(): lax.all_to_all(planes.reshape(n_gy, 4 * per, LANES), 'gy', split_axis=0,...  7.76 us
    all_gather x1, blocking collectives, on_device(): strips = lax.all_gather(strips, ('gx', 'gy'), axis_index_groups=along)  6.5 us
    all_gather x1, blocking collectives, on_device(): relay = lax.all_gather(relay, 'gx', axis_index_groups=chips)  4.9 us
    all_gather x1, blocking collectives, on_device(): lax.all_gather(jnp.where(lower, strips[1], strips[0]), 'gx', axis_index_g...  2.08 us
  transfers between devices with their start and end apart: 1, of which 1 were waited for; matrix products, arithmetic and copies ran while one was open for 0% of the time, Pallas kernels for 6%

profile of v6, /device:TPU:1, one launch (start us, length us, event | category | flops | bytes accessed | tf_op | source)
XLA Modules:
  0.0 58.8 jit_solution(16894129381577101392)
XLA Ops:
  0.6 3.2 %shard_map.50 = (f32[16,32,128]{2,1,0:T(8,128)S(1)}, f32[16,32,128]{2,1,0:T(8,128)S(1)}, f32[576,128]{1,0:T(8,128)}) custom-call(f32[16,32,128]{2,1,0:T(8,128)} %refs_0_.5, f32[16,32,128]{2,1,0:T(8,128)} %refs_1_.1, s32[16,32,128]{2,1,0:T(8,128)} %refs_2_.1), custom_call_target="tpu_custom_call" | custom-call | flops 1000000 | bytes 1605632 | tf_op jit(solution)/shard_map/pallas_call | solution.py:479
  3.8 8.9 %all-gather = f32[1152,128]{1,0:T(8,128)S(1)} all-gather(f32[576,128]{1,0:T(8,128)} %get-tuple-element.9), channel_id=2, replica_groups={{0,16},{32,48},{64,80},{96,112},{128,144},{160,176},{192,208},{224,240}..., dimensions={0}, use_global_device_ids=true | all-gather | bytes 884736 | tf_op jit(solution)/shard_map/all_gather | solution.py:512
  12.8 6.5 %all_gather.27 = f32[2,192,128]{2,1,0:T(8,128)S(1)} all-gather(f32[1,192,128]{2,1,0:T(8,128)S(1)} %bitcast.15), channel_id=1, replica_groups={{0,1},{2,3},{4,5},{6,7},{8,9},{10,11},{12,13},{14,15},{17,18},{19,20},{..., dimensions={0}, use_global_device_ids=true | all-gather | bytes 294912 | tf_op jit(solution)/shard_map/all_gather | solution.py:515
  19.3 0.0 copy-start
  19.3 2.1 %all_gather.28.refs_4_ = f32[2,192,128]{2,1,0:T(8,128)S(1)} all-gather(f32[1,192,128]{2,1,0:T(8,128)S(1)} %slice_select_fusion), channel_id=1, replica_groups={{0,16},{32,48},{64,80},{96,112},{128,144},{160,176},{192,208},{224,240}..., dimensions={0}, use_global_device_ids=true | all-gather | bytes 294912 | tf_op jit(solution)/shard_map/all_gather | solution.py:516
  21.4 0.0 copy-done
  21.4 0.5 shard_map.51.refs_0_
  21.9 7.8 %all-gather.1 = f32[1408,128]{1,0:T(8,128)S(1)} all-gather(f32[704,128]{1,0:T(8,128)S(1)} %shard_map.51.refs_0_), channel_id=3, replica_groups={{16,32},{48,64},{80,96},{112,128},{144,160},{176,192},{208,224},{240,25..., dimensions={0}, use_global_device_ids=true | all-gather | bytes 1081344 | tf_op jit(solution)/shard_map/all_gather | solution.py:524
  29.7 0.3 shard_map.52
  30.0 4.9 %all-gather.2 = f32[416,128]{1,0:T(8,128)S(1)} all-gather(f32[208,128]{1,0:T(8,128)S(1)} %shard_map.52), channel_id=4, replica_groups={{0,16},{32,48},{64,80},{96,112},{128,144},{160,176},{192,208},{224,240}..., dimensions={0}, use_global_device_ids=true | all-gather | bytes 319488 | tf_op jit(solution)/shard_map/all_gather | solution.py:526
  34.9 3.3 %shard_map.53 = (f32[8,16,128]{2,1,0:T(8,128)S(1)}, f32[64,128]{1,0:T(8,128)}) custom-call(f32[704,128]{1,0:T(8,128)S(1)} %shard_map.51.refs_0_, f32[2,704,128]{2,1,0:T(8,128)S(1)} %bitcast.8, f32[2,208,128]{2,1,0:T(8,128)S(1)} %bitcast.13), custom_call_target="tpu_custom_call" | custom-call | flops 1000000 | bytes 1392640 | tf_op jit(solution)/shard_map/pallas_call | solution.py:479
  38.2 8.4 %all-to-all-start = ((f32[16,4,128]{2,1,0:T(4,128)}), f32[16,4,128]{2,1,0:T(4,128)S(1)}, u32[]{:S(2)}, u32[]{:S(2)}) async-start(f32[16,4,128]{2,1,0:T(4,128)} %bitcast.4), calls=%async_computation | async-start | bytes 65536 | tf_op jit(solution)/shard_map/all_to_all | solution.py:536
  46.6 3.7 %shard_map.54 = f32[16,32,128]{2,1,0:T(8,128)} custom-call(f32[16,32,128]{2,1,0:T(8,128)S(1)} %copy-done, f32[16,32,128]{2,1,0:T(8,128)S(1)} %get-tuple-element.7.refs_1_, f32[16,32,128]{2,1,0:T(8,128)S(1)} %get-tuple-element.8.refs_2_, f32[2,576,128]{2,1,0:T(8,128)S(1)} %bitcast.12, f32[2,192,128]{2,1,0:T(8,128)S(1)} %all_gather.28.refs_4_, ...), custom_call_target="tpu_custom_call" | custom-call | flops 20000000 | bytes 2621440 | tf_op jit(solution)/shard_map/pallas_call | solution.py:479
  50.3 7.8 %all-to-all-done = f32[16,4,128]{2,1,0:T(4,128)S(1)} async-done(((f32[16,4,128]{2,1,0:T(4,128)}), f32[16,4,128]{2,1,0:T(4,128)S(1)}, u32[]{:S(2)}, u32[]{:S(2)}) %all-to-all-start) | async-done | bytes 32800 | tf_op jit(solution)/shard_map/all_to_all | solution.py:536
  58.1 0.7 %shard_map.55 = f32[64,128]{1,0:T(8,128)} custom-call(f32[64,128]{1,0:T(8,128)S(1)} %bitcast.14), custom_call_target="tpu_custom_call" | custom-call | flops 1000000 | bytes 65536 | tf_op jit(solution)/shard_map/pallas_call | solution.py:479
  (2 shorter events, 0.0 us)
Async XLA Ops:
  19.3 2.1 %copy-start = (f32[16,32,128]{2,1,0:T(8,128)S(1)}, f32[16,32,128]{2,1,0:T(8,128)}, u32[]{:S(2)}) copy-start(f32[16,32,128]{2,1,0:T(8,128)} %refs_0_.5) | copy-start | bytes 786436
  38.2 19.9 %all-to-all-start = ((f32[16,4,128]{2,1,0:T(4,128)}), f32[16,4,128]{2,1,0:T(4,128)S(1)}, u32[]{:S(2)}, u32[]{:S(2)}) async-start(f32[16,4,128]{2,1,0:T(4,128)} %bitcast.4), calls=%async_computation | async-start | bytes 65536 | tf_op jit(solution)/shard_map/all_to_all | solution.py:536

commit v7 on v6

--- a/solution.py
+++ b/solution.py
@@ -66,7 +66,24 @@
     return jnp.dot(a, b, precision=lax.Precision.HIGHEST, preferred_element_type=F32)
 
 
-def residual_kernel(flags, it_in, src_in, lab_in, r_ref, k_ref, a_ref, pool, it, src, lab, sems):
+def residual_rows(k_ref, it, src, arrive=None):
+    z, lane = iota((NZ, LANES), 0), iota((NZ, LANES), 1)
+    before = zero = jnp.zeros((NZ, LANES), F32)
+    for i in range(ROWS):
+        if arrive:
+            arrive(i + 1)
+        k, v = k_ref[i], it[i]
+        after = flux(k, k_ref[i + 1], v, it[i + 1]) if i < ROWS - 1 else zero
+        fy = jnp.where(lane < LANES - 1, flux(k, roll(k, -1, 1), v, roll(v, -1, 1)), 0.0)
+        k_z = jnp.where(z < NZ - 1, roll(k, -1, 0), 0.0)
+        v_z = jnp.where(z < NZ - 1, roll(v, -1, 0), 0.0)
+        fz = flux(k, k_z, v, v_z)
+        fz_in = jnp.where(z > 0, roll(fz, 1, 0), -0.5 * k * v)
+        yield i, k, v, src[i] - after + before - fy + roll(fy, 1, 1) - fz + fz_in
+        before = after
+
+
+def residual_kernel(flags, it_in, src_in, lab_in, out_ref, n_ref, pool, k_ref, a_ref, it, src, lab, sems, done_sems):
     copies = []
     for part in range(PARTS):
         rows = pl.ds(part * ROWS // PARTS, ROWS // PARTS)
@@ -79,30 +96,25 @@
         for copy in copies[-1]:
             copy.start()
 
-    def arrive(part):
+    def arrive(row):
+        part, within = divmod(row, ROWS // PARTS)
+        if within or part == PARTS:
+            return
         for copy in copies[part]:
             copy.wait()
-        for i in range(part * ROWS // PARTS, (part + 1) * ROWS // PARTS):
+        for i in range(row, row + ROWS // PARTS):
             k_ref[i] = conduct(lab[i])
 
     arrive(0)
-    z, lane = iota((NZ, LANES), 0), iota((NZ, LANES), 1)
+    lane = iota((NZ, LANES), 1)
     zero = jnp.zeros((NZ, LANES), F32)
-    before = zero
     up = dn = zero
-    for i in range(ROWS):
-        if (i + 1) % (ROWS // PARTS) == 0 and i < ROWS - 1:
-            arrive((i + 1) // (ROWS // PARTS))
-        k, v = k_ref[i], it[i]
-        after = flux(k, k_ref[i + 1], v, it[i + 1]) if i < ROWS - 1 else zero
-        fy = jnp.where(lane < LANES - 1, flux(k, roll(k, -1, 1), v, roll(v, -1, 1)), 0.0)
-        k_z = jnp.where(z < NZ - 1, roll(k, -1, 0), 0.0)
-        v_z = jnp.where(z < NZ - 1, roll(v, -1, 0), 0.0)
-        fz = flux(k, k_z, v, v_z)
-        fz_in = jnp.where(z > 0, roll(fz, 1, 0), -0.5 * k * v)
-        r = src[i] - after + before - fy + roll(fy, 1, 1) - fz + fz_in
-        r_ref[i] = r
-        before = after
+    low, high = {}, {}
+    for i, k, v, r in residual_rows(k_ref, it, src, arrive):
+        if i < 3:
+            low[i] = r
+        if i >= ROWS - 3:
+            high[i - ROWS + 3] = r
         j = i // 2
         if i % 2 == 0:
             r_even, k_even = r, k
@@ -124,6 +136,22 @@
         dn = jnp.where(here, roll(edge, 32 * g, 1), dn)
     a_ref[UP + NZ:UP + 2 * NZ] = up
     a_ref[DN + NZ:DN + 2 * NZ] = dn
+    first = flags[0] == 0
+    lows = [k_ref[t] for t in range(4)] + [low[t] for t in range(3)] + [it[0]]
+    highs = [k_ref[ROWS - 4 + t] for t in range(4)] + [high[t] for t in range(3)] + [it[ROWS - 1]]
+    for t in range(8):
+        a_ref[FACING + NZ * t:FACING + NZ * (t + 1)] = jnp.where(first, highs[t], lows[t])
+        n_ref[NZ * t:NZ * (t + 1)] = jnp.where(first, lows[t], highs[t])
+    sent = []
+
+    def send(start, rows):
+        at = pl.ds(start, rows)
+        sent.append(pltpu.make_async_copy(a_ref.at[at], out_ref.at[at], done_sems.at[len(sent)]))
+        sent[-1].start()
+
+    send(FACING, 8 * NZ)
+    send(UP, 2 * NZ)
+    send(DN, 2 * NZ)
     tops = pool[:, :, pl.ds(0, CZ, stride=2), :] + pool[:, :, pl.ds(1, CZ, stride=2), :]
     child, parent = iota((LANES, LANES), 0) // 2, iota((LANES, LANES), 1)
     to_left = jnp.where(child == parent, F32(1.0), F32(0.0))
@@ -143,12 +171,11 @@
             dn = jnp.where(at_r, roll(row, off, 1), jnp.where(at_k, roll(row, off + 16 - 64, 1), dn))
         a_ref[UP + 2 * NZ + CZ * t:UP + 2 * NZ + CZ * (t + 1)] = up
         a_ref[DN + 2 * NZ + CZ * t:DN + 2 * NZ + CZ * (t + 1)] = dn
-    first = flags[0] == 0
-    rows = [jnp.where(first, k_ref[ROWS - 4 + t], k_ref[t]) for t in range(4)]
-    rows += [jnp.where(first, r_ref[ROWS - 3 + t], r_ref[t]) for t in range(3)]
-    rows.append(jnp.where(first, it[ROWS - 1], it[0]))
-    for t in range(8):
-        a_ref[FACING + NZ * t:FACING + NZ * (t + 1)] = rows[t]
+    send(0, OWN)
+    send(UP + 2 * NZ, 2 * CZ)
+    send(DN + 2 * NZ, 2 * CZ)
+    for copy in sent:
+        copy.wait()
 
 
 def strip_flux(up, dn):
@@ -204,7 +231,7 @@
     return dot(sums[0], own) + dot(sums[1], beyond)
 
 
-def chip_kernel(flags, it, r_in, k_in, pair, strips, o_ref, pool):
+def chip_kernel(flags, near, pair, strips, o_ref, pool):
     first = flags[0] == 0
     lane = iota((CZ, LANES), 1)
     nears = []
@@ -227,10 +254,8 @@
                 less = less - jnp.where(lane == 32 * q + 15, roll(sums[1], 32 * q + 15 - src, 1), 0.0)
             o_ref[base + OWN + CZ * t:base + OWN + CZ * (t + 1)] = more
             o_ref[base + OWN + CZ * (2 + t):base + OWN + CZ * (3 + t)] = less
-        k_row, r_row, v_row = (ROWS - 4, ROWS - 3, ROWS - 1) if n else (0, 0, 0)
-        ks = [k_in[k_row + t] for t in range(4)]
-        rs = [r_in[r_row + t] for t in range(3)]
-        nears.append(beside_rows(flags, strips, n, ks, rs, it[v_row], done, n == 1))
+        rows = [near[NZ * t:NZ * (t + 1)] for t in range(8)]
+        nears.append(beside_rows(flags, strips, n, rows[0:4], rows[4:7], rows[7], done, n == 1))
     for t in range(10):
         o_ref[2 * BLOCK + NZ * t:2 * BLOCK + NZ * (t + 1)] = jnp.where(first, nears[0][t], nears[1][t])
 
@@ -357,10 +382,14 @@
     sweep(1, CEXT - 1, CROWS, COARSE_SWEEPS, COARSE_SWEEPS, r_s, s_s, x_s, c_s, 0)
 
 
-def fine_part(flags, it, r_in, k_in, pair, strips, out, x_s, k_s, r_s, s_s, c_s):
+def fine_part(flags, it, src, lab, pair, strips, out, k_in, r_in, x_s, k_s, r_s, s_s, c_s):
     first = flags[0] == 0
     low, high = flags[1].astype(F32), flags[2].astype(F32)
     lane = iota((NZ, LANES), 1)
+    for i in range(ROWS):
+        k_in[i] = conduct(lab[i])
+    for i, _, _, r in residual_rows(k_in, it, src):
+        r_in[i] = r
     facing = []
     for n in range(2):
         rd, ru = came(flags, strips, n, 0, NZ)
@@ -428,9 +457,9 @@
 
 
 def fine_kernel(
-    flags, it, r_in, k_in, pair, strips, out, x_c, o_ref, x_f, k_f, r_f, s_f, c_f, wide_s
+    flags, it, src, lab, pair, strips, out, x_c, o_ref, k_in, r_in, x_f, k_f, r_f, s_f, c_f, wide_s
 ):
-    fine_part(flags, it, r_in, k_in, pair, strips, out, x_f, k_f, r_f, s_f, c_f)
+    fine_part(flags, it, src, lab, pair, strips, out, k_in, r_in, x_f, k_f, r_f, s_f, c_f)
     child, parent = iota((LANES, LANES), 1) // 2, iota((LANES, LANES), 0)
     spread = jnp.where(child == parent, F32(1.0), F32(0.0))
     wide = dot(x_c[...].reshape(CROWS * CZ, LANES), spread).reshape(CROWS, CZ, LANES)
@@ -466,9 +495,12 @@
     size = sum(4 * x.size for x in operands) + sum(4 * o.size for o in outs)
     multiple = len(outs) > 1
     held = [pltpu.VMEM(s, F32) for s in scratch]
+    out_specs = [vmem] * len(outs)
     if copies:
+        out_specs[0] = pl.BlockSpec(memory_space=pltpu.HBM)
         held += [pltpu.VMEM(x.shape, x.dtype) for x in operands]
         held.append(pltpu.SemaphoreType.DMA((len(operands), PARTS)))
+        held.append(pltpu.SemaphoreType.DMA((6,)))
 
     def body(*refs):
         if placed:
@@ -480,9 +512,9 @@
         body,
         out_shape=outs if multiple else outs[0],
         in_specs=specs,
-        out_specs=[vmem] * len(outs) if multiple else vmem,
+        out_specs=out_specs if multiple else out_specs[0],
         scratch_shapes=held,
-        compiler_params=pltpu.CompilerParams(vmem_limit_bytes=(54500 if copies else 40960) * 1024),
+        compiler_params=pltpu.CompilerParams(vmem_limit_bytes=(54900 if copies else 40960) * 1024),
         cost_estimate=pl.CostEstimate(flops=flops, bytes_accessed=size, transcendentals=0),
     )(*operands)
 
@@ -501,10 +533,10 @@
         [i * n_gy + j, i * n_gy + (j + 1) % n_gy] for i in range(n_gx) for j in range(i % 2, n_gy, 2)
     ]
     own = shape(ROWS, NZ, LANES)
-    resid, cond, shared = call(
+    shared, near = call(
         residual_kernel,
-        [own, own, shape(SHARED, LANES)],
-        [(2, CROWS, NZ, LANES)],
+        [shape(SHARED, LANES), shape(8 * NZ, LANES)],
+        [(2, CROWS, NZ, LANES), own.shape, (SHARED, LANES)],
         True,
         (iterate, source, labels),
         copies=True,
@@ -519,7 +551,7 @@
         [shape(2 * BLOCK + NEAR, LANES)],
         [(2, NZ, LANES)],
         True,
-        (iterate, resid, cond, pair, strips),
+        (near, pair, strips),
     )
     beyond = lax.all_gather(chip, "gx", axis_index_groups=between)
     relay = call(relay_kernel, [shape(BLOCK + CZ, LANES)], [(2, NZ, LANES)], True, (beyond,))
@@ -537,9 +569,9 @@
     corrected = call(
         fine_kernel,
         [own],
-        [(ROWS, NZ, LANES), wide, wide, wide, (6, *wide), (CROWS, NZ, LANES)],
+        [own.shape, own.shape, own.shape, wide, wide, wide, (6, *wide), (CROWS, NZ, LANES)],
         True,
-        (iterate, resid, cond, pair, strips, beyond, coarse_out),
+        (iterate, source, labels, pair, strips, beyond, coarse_out),
         flops=20000000,
     )
     owned = call(

time: 59.1 us -> 59 us (level)
  Pallas kernels: 11.6 us -> 12.6 us
  waiting for transfers between devices: 7.76 us -> 6.77 us
    all_to_all x1, waiting for transfers between devices: 7.76 us -> 6.77 us  [on_device(): lax.all_to_all(planes.reshape(n_gy, 4 * per, LANES), 'gy', split_axis=0,...]
    pallas_call x6, Pallas kernels: 11.6 us -> 12.6 us  [call(): pl.pallas_call(body, out_shape=outs if multiple else outs[0], in_specs=sp...]
  transfers between devices with their start and end apart: 1 -> 1, of which waited for: 1 -> 1; matrix products, arithmetic and copies ran while one was open for 0% -> 0% of each run, Pallas kernels for 6% -> 8%
where the time goes in v7:
time: 59 us; the launch traced here: 58.7 us
  blocking collectives  30.1 us (51%)
  Pallas kernels  12.6 us (21%)
  starting transfers between devices  8.45 us (14%)
  waiting for transfers between devices  6.77 us (11%)
  between operations  0.7 us (1%)
    pallas_call x6, Pallas kernels, call(): pl.pallas_call(body, out_shape=outs if multiple else outs[0], in_specs=sp...  12.6 us
    all_gather x1, blocking collectives, on_device(): pair = lax.all_gather(shared, 'gx', axis_index_groups=chips)  8.95 us
    all_to_all x1, starting transfers between devices, on_device(): lax.all_to_all(planes.reshape(n_gy, 4 * per, LANES), 'gy', split_axis=0,...  8.45 us
    all_gather x1, blocking collectives, on_device(): beyond = lax.all_gather(chip, 'gx', axis_index_groups=between)  7.82 us
    all_to_all x1, waiting for transfers between devices, on_device(): lax.all_to_all(planes.reshape(n_gy, 4 * per, LANES), 'gy', split_axis=0,...  6.77 us
    all_gather x1, blocking collectives, on_device(): strips = lax.all_gather(strips, ('gx', 'gy'), axis_index_groups=along)  6.5 us
    all_gather x1, blocking collectives, on_device(): relay = lax.all_gather(relay, 'gx', axis_index_groups=chips)  4.9 us
    all_gather x1, blocking collectives, on_device(): lax.all_gather(jnp.where(lower, strips[1], strips[0]), 'gx', axis_index_g...  1.95 us
  transfers between devices with their start and end apart: 1, of which 1 were waited for; matrix products, arithmetic and copies ran while one was open for 0% of the time, Pallas kernels for 8%

profile of v7, /device:TPU:1, one launch (start us, length us, event | category | flops | bytes accessed | tf_op | source)
XLA Modules:
  0.0 58.7 jit_solution(938985415435263295)
XLA Ops:
  0.6 3.2 %shard_map.50 = (f32[576,128]{1,0:T(8,128)}, f32[256,128]{1,0:T(8,128)S(1)}) custom-call(f32[16,32,128]{2,1,0:T(8,128)} %refs_0_.3, f32[16,32,128]{2,1,0:T(8,128)} %refs_1_.3, s32[16,32,128]{2,1,0:T(8,128)} %refs_2_.3), custom_call_target="tpu_custom_call" | custom-call | flops 1000000 | bytes 1212416 | tf_op jit(solution)/shard_map/pallas_call | solution.py:511
  3.8 8.9 %all-gather = f32[1152,128]{1,0:T(8,128)S(1)} all-gather(f32[576,128]{1,0:T(8,128)} %get-tuple-element.6), channel_id=2, replica_groups={{0,16},{32,48},{64,80},{96,112},{128,144},{160,176},{192,208},{224,240}..., dimensions={0}, use_global_device_ids=true | all-gather | bytes 884736 | tf_op jit(solution)/shard_map/all_gather | solution.py:544
  12.8 6.5 %all_gather.27 = f32[2,192,128]{2,1,0:T(8,128)S(1)} all-gather(f32[1,192,128]{2,1,0:T(8,128)S(1)} %bitcast.15), channel_id=1, replica_groups={{0,1},{2,3},{4,5},{6,7},{8,9},{10,11},{12,13},{14,15},{17,18},{19,20},{..., dimensions={0}, use_global_device_ids=true | all-gather | bytes 294912 | tf_op jit(solution)/shard_map/all_gather | solution.py:547
  19.3 1.9 %all_gather.28.refs_2_.refs_4_ = f32[2,192,128]{2,1,0:T(8,128)S(1)} all-gather(f32[1,192,128]{2,1,0:T(8,128)S(1)} %slice_select_fusion), channel_id=1, replica_groups={{0,16},{32,48},{64,80},{96,112},{128,144},{160,176},{192,208},{224,240}..., dimensions={0}, use_global_device_ids=true | all-gather | bytes 294912 | tf_op jit(solution)/shard_map/all_gather | solution.py:548
  21.3 0.5 shard_map.51.refs_0_
  21.7 7.8 %all-gather.1 = f32[1408,128]{1,0:T(8,128)S(1)} all-gather(f32[704,128]{1,0:T(8,128)S(1)} %shard_map.51.refs_0_), channel_id=3, replica_groups={{16,32},{48,64},{80,96},{112,128},{144,160},{176,192},{208,224},{240,25..., dimensions={0}, use_global_device_ids=true | all-gather | bytes 1081344 | tf_op jit(solution)/shard_map/all_gather | solution.py:556
  29.6 0.3 shard_map.52
  29.8 4.9 %all-gather.2 = f32[416,128]{1,0:T(8,128)S(1)} all-gather(f32[208,128]{1,0:T(8,128)S(1)} %shard_map.52), channel_id=4, replica_groups={{0,16},{32,48},{64,80},{96,112},{128,144},{160,176},{192,208},{224,240}..., dimensions={0}, use_global_device_ids=true | all-gather | bytes 319488 | tf_op jit(solution)/shard_map/all_gather | solution.py:558
  34.7 0.0 copy-start
  34.7 0.0 copy-start.1
  34.7 0.0 copy-start.2
  34.7 3.3 %shard_map.53 = (f32[8,16,128]{2,1,0:T(8,128)S(1)}, f32[64,128]{1,0:T(8,128)}) custom-call(f32[704,128]{1,0:T(8,128)S(1)} %shard_map.51.refs_0_, f32[2,704,128]{2,1,0:T(8,128)S(1)} %bitcast.8, f32[2,208,128]{2,1,0:T(8,128)S(1)} %bitcast.13), custom_call_target="tpu_custom_call" | custom-call | flops 1000000 | bytes 1392640 | tf_op jit(solution)/shard_map/pallas_call | solution.py:511
  38.0 8.4 %all-to-all-start = ((f32[16,4,128]{2,1,0:T(4,128)}), f32[16,4,128]{2,1,0:T(4,128)S(1)}, u32[]{:S(2)}, u32[]{:S(2)}) async-start(f32[16,4,128]{2,1,0:T(4,128)} %bitcast.4), calls=%async_computation | async-start | bytes 65536 | tf_op jit(solution)/shard_map/all_to_all | solution.py:568
  46.5 0.0 copy-done
  46.5 0.0 copy-done.1
  46.5 0.0 copy-done.2
  46.5 4.7 %shard_map.54 = f32[16,32,128]{2,1,0:T(8,128)} custom-call(f32[16,32,128]{2,1,0:T(8,128)S(1)} %copy-done, f32[16,32,128]{2,1,0:T(8,128)S(1)} %copy-done.1, s32[16,32,128]{2,1,0:T(8,128)S(1)} %copy-done.2, f32[2,576,128]{2,1,0:T(8,128)S(1)} %bitcast.12, f32[2,192,128]{2,1,0:T(8,128)S(1)} %all_gather.28.refs_2_.refs_4_, f32[2,704,128]{2,1,0:T(8,128)S(1)} %bitcast.9, ...), custom_call_target="tpu_custom_call" | custom-call | flops 20000000 | bytes 2621440 | tf_op jit(solution)/shard_map/pallas_call | solution.py:511
  51.2 6.8 %all-to-all-done = f32[16,4,128]{2,1,0:T(4,128)S(1)} async-done(((f32[16,4,128]{2,1,0:T(4,128)}), f32[16,4,128]{2,1,0:T(4,128)S(1)}, u32[]{:S(2)}, u32[]{:S(2)}) %all-to-all-start) | async-done | bytes 32800 | tf_op jit(solution)/shard_map/all_to_all | solution.py:568
  58.0 0.7 %shard_map.55 = f32[64,128]{1,0:T(8,128)} custom-call(f32[64,128]{1,0:T(8,128)S(1)} %bitcast.14), custom_call_target="tpu_custom_call" | custom-call | flops 1000000 | bytes 65536 | tf_op jit(solution)/shard_map/pallas_call | solution.py:511
  (2 shorter events, 0.0 us)
Async XLA Ops:
  34.7 11.8 %copy-start = (f32[16,32,128]{2,1,0:T(8,128)S(1)}, f32[16,32,128]{2,1,0:T(8,128)}, u32[]{:S(2)}) copy-start(f32[16,32,128]{2,1,0:T(8,128)} %refs_0_.3) | copy-start | bytes 786436
  34.7 11.8 %copy-start.1 = (f32[16,32,128]{2,1,0:T(8,128)S(1)}, f32[16,32,128]{2,1,0:T(8,128)}, u32[]{:S(2)}) copy-start(f32[16,32,128]{2,1,0:T(8,128)} %refs_1_.3) | copy-start | bytes 786436
  34.7 11.8 %copy-start.2 = (s32[16,32,128]{2,1,0:T(8,128)S(1)}, s32[16,32,128]{2,1,0:T(8,128)}, u32[]{:S(2)}) copy-start(s32[16,32,128]{2,1,0:T(8,128)} %refs_2_.3) | copy-start | bytes 786436
  38.0 19.9 %all-to-all-start = ((f32[16,4,128]{2,1,0:T(4,128)}), f32[16,4,128]{2,1,0:T(4,128)S(1)}, u32[]{:S(2)}, u32[]{:S(2)}) async-start(f32[16,4,128]{2,1,0:T(4,128)} %bitcast.4), calls=%async_computation | async-start | bytes 65536 | tf_op jit(solution)/shard_map/all_to_all | solution.py:568

commit v8 on v7

--- a/solution.py
+++ b/solution.py
@@ -156,7 +156,9 @@
     child, parent = iota((LANES, LANES), 0) // 2, iota((LANES, LANES), 1)
     to_left = jnp.where(child == parent, F32(1.0), F32(0.0))
     to_right = jnp.where(child == parent - CLANES, F32(0.125), F32(0.0))
-    coarse = dot(tops[0].reshape(CROWS * CZ, LANES), to_left) + dot(tops[1].reshape(CROWS * CZ, LANES), to_right)
+    held = tops[1].reshape(CROWS * CZ, LANES).astype(jnp.bfloat16)
+    coarse = jnp.dot(held, to_right.astype(jnp.bfloat16), preferred_element_type=F32)
+    coarse = dot(tops[0].reshape(CROWS * CZ, LANES), to_left) + coarse
     a_ref[0:OWN] = coarse
     coarse = coarse.reshape(CROWS, CZ, LANES)
     lane = iota((CZ, LANES), 1)

time: 59 us -> 58.9 us (level)
  no operation moved by 1% of the time
where the time goes in v8:
time: 58.9 us; the launch traced here: 58.6 us
  blocking collectives  30.1 us (51%)
  Pallas kernels  12.5 us (21%)
  starting transfers between devices  8.45 us (14%)
  waiting for transfers between devices  6.77 us (11%)
  between operations  0.7 us (1%)
    pallas_call x6, Pallas kernels, call(): pl.pallas_call(body, out_shape=outs if multiple else outs[0], in_specs=sp...  12.5 us
    all_gather x1, blocking collectives, on_device(): pair = lax.all_gather(shared, 'gx', axis_index_groups=chips)  8.95 us
    all_to_all x1, starting transfers between devices, on_device(): lax.all_to_all(planes.reshape(n_gy, 4 * per, LANES), 'gy', split_axis=0,...  8.45 us
    all_gather x1, blocking collectives, on_device(): beyond = lax.all_gather(chip, 'gx', axis_index_groups=between)  7.82 us
    all_to_all x1, waiting for transfers between devices, on_device(): lax.all_to_all(planes.reshape(n_gy, 4 * per, LANES), 'gy', split_axis=0,...  6.77 us
    all_gather x1, blocking collectives, on_device(): strips = lax.all_gather(strips, ('gx', 'gy'), axis_index_groups=along)  6.5 us
    all_gather x1, blocking collectives, on_device(): relay = lax.all_gather(relay, 'gx', axis_index_groups=chips)  4.9 us
    all_gather x1, blocking collectives, on_device(): lax.all_gather(jnp.where(lower, strips[1], strips[0]), 'gx', axis_index_g...  1.95 us
  transfers between devices with their start and end apart: 1, of which 1 were waited for; matrix products, arithmetic and copies ran while one was open for 0% of the time, Pallas kernels for 8%

profile of v8, /device:TPU:1, one launch (start us, length us, event | category | flops | bytes accessed | tf_op | source)
XLA Modules:
  0.0 58.6 jit_solution(16410587291167771259)
XLA Ops:
  0.6 3.1 %shard_map.50 = (f32[576,128]{1,0:T(8,128)}, f32[256,128]{1,0:T(8,128)S(1)}) custom-call(f32[16,32,128]{2,1,0:T(8,128)} %refs_0_.3, f32[16,32,128]{2,1,0:T(8,128)} %refs_1_.3, s32[16,32,128]{2,1,0:T(8,128)} %refs_2_.3), custom_call_target="tpu_custom_call" | custom-call | flops 1000000 | bytes 1212416 | tf_op jit(solution)/shard_map/pallas_call | solution.py:513
  3.8 8.9 %all-gather = f32[1152,128]{1,0:T(8,128)S(1)} all-gather(f32[576,128]{1,0:T(8,128)} %get-tuple-element.6), channel_id=2, replica_groups={{0,16},{32,48},{64,80},{96,112},{128,144},{160,176},{192,208},{224,240}..., dimensions={0}, use_global_device_ids=true | all-gather | bytes 884736 | tf_op jit(solution)/shard_map/all_gather | solution.py:546
  12.7 6.5 %all_gather.27 = f32[2,192,128]{2,1,0:T(8,128)S(1)} all-gather(f32[1,192,128]{2,1,0:T(8,128)S(1)} %bitcast.15), channel_id=1, replica_groups={{0,1},{2,3},{4,5},{6,7},{8,9},{10,11},{12,13},{14,15},{17,18},{19,20},{..., dimensions={0}, use_global_device_ids=true | all-gather | bytes 294912 | tf_op jit(solution)/shard_map/all_gather | solution.py:549
  19.3 1.9 %all_gather.28.refs_2_.refs_4_ = f32[2,192,128]{2,1,0:T(8,128)S(1)} all-gather(f32[1,192,128]{2,1,0:T(8,128)S(1)} %slice_select_fusion), channel_id=1, replica_groups={{0,16},{32,48},{64,80},{96,112},{128,144},{160,176},{192,208},{224,240}..., dimensions={0}, use_global_device_ids=true | all-gather | bytes 294912 | tf_op jit(solution)/shard_map/all_gather | solution.py:550
  21.2 0.5 shard_map.51.refs_0_
  21.7 7.8 %all-gather.1 = f32[1408,128]{1,0:T(8,128)S(1)} all-gather(f32[704,128]{1,0:T(8,128)S(1)} %shard_map.51.refs_0_), channel_id=3, replica_groups={{16,32},{48,64},{80,96},{112,128},{144,160},{176,192},{208,224},{240,25..., dimensions={0}, use_global_device_ids=true | all-gather | bytes 1081344 | tf_op jit(solution)/shard_map/all_gather | solution.py:558
  29.5 0.3 shard_map.52
  29.8 4.9 %all-gather.2 = f32[416,128]{1,0:T(8,128)S(1)} all-gather(f32[208,128]{1,0:T(8,128)S(1)} %shard_map.52), channel_id=4, replica_groups={{0,16},{32,48},{64,80},{96,112},{128,144},{160,176},{192,208},{224,240}..., dimensions={0}, use_global_device_ids=true | all-gather | bytes 319488 | tf_op jit(solution)/shard_map/all_gather | solution.py:560
  34.7 0.0 copy-start
  34.7 0.0 copy-start.1
  34.7 0.0 copy-start.2
  34.7 3.3 %shard_map.53 = (f32[8,16,128]{2,1,0:T(8,128)S(1)}, f32[64,128]{1,0:T(8,128)}) custom-call(f32[704,128]{1,0:T(8,128)S(1)} %shard_map.51.refs_0_, f32[2,704,128]{2,1,0:T(8,128)S(1)} %bitcast.8, f32[2,208,128]{2,1,0:T(8,128)S(1)} %bitcast.13), custom_call_target="tpu_custom_call" | custom-call | flops 1000000 | bytes 1392640 | tf_op jit(solution)/shard_map/pallas_call | solution.py:513
  38.0 8.4 %all-to-all-start = ((f32[16,4,128]{2,1,0:T(4,128)}), f32[16,4,128]{2,1,0:T(4,128)S(1)}, u32[]{:S(2)}, u32[]{:S(2)}) async-start(f32[16,4,128]{2,1,0:T(4,128)} %bitcast.4), calls=%async_computation | async-start | bytes 65536 | tf_op jit(solution)/shard_map/all_to_all | solution.py:570
  46.5 0.0 copy-done
  46.5 0.0 copy-done.1
  46.5 0.0 copy-done.2
  46.5 4.7 %shard_map.54 = f32[16,32,128]{2,1,0:T(8,128)} custom-call(f32[16,32,128]{2,1,0:T(8,128)S(1)} %copy-done, f32[16,32,128]{2,1,0:T(8,128)S(1)} %copy-done.1, s32[16,32,128]{2,1,0:T(8,128)S(1)} %copy-done.2, f32[2,576,128]{2,1,0:T(8,128)S(1)} %bitcast.12, f32[2,192,128]{2,1,0:T(8,128)S(1)} %all_gather.28.refs_2_.refs_4_, f32[2,704,128]{2,1,0:T(8,128)S(1)} %bitcast.9, ...), custom_call_target="tpu_custom_call" | custom-call | flops 20000000 | bytes 2621440 | tf_op jit(solution)/shard_map/pallas_call | solution.py:513
  51.2 6.8 %all-to-all-done = f32[16,4,128]{2,1,0:T(4,128)S(1)} async-done(((f32[16,4,128]{2,1,0:T(4,128)}), f32[16,4,128]{2,1,0:T(4,128)S(1)}, u32[]{:S(2)}, u32[]{:S(2)}) %all-to-all-start) | async-done | bytes 32800 | tf_op jit(solution)/shard_map/all_to_all | solution.py:570
  57.9 0.7 %shard_map.55 = f32[64,128]{1,0:T(8,128)} custom-call(f32[64,128]{1,0:T(8,128)S(1)} %bitcast.14), custom_call_target="tpu_custom_call" | custom-call | flops 1000000 | bytes 65536 | tf_op jit(solution)/shard_map/pallas_call | solution.py:513
  (2 shorter events, 0.0 us)
Async XLA Ops:
  34.7 11.8 %copy-start = (f32[16,32,128]{2,1,0:T(8,128)S(1)}, f32[16,32,128]{2,1,0:T(8,128)}, u32[]{:S(2)}) copy-start(f32[16,32,128]{2,1,0:T(8,128)} %refs_0_.3) | copy-start | bytes 786436
  34.7 11.8 %copy-start.1 = (f32[16,32,128]{2,1,0:T(8,128)S(1)}, f32[16,32,128]{2,1,0:T(8,128)}, u32[]{:S(2)}) copy-start(f32[16,32,128]{2,1,0:T(8,128)} %refs_1_.3) | copy-start | bytes 786436
  34.7 11.8 %copy-start.2 = (s32[16,32,128]{2,1,0:T(8,128)S(1)}, s32[16,32,128]{2,1,0:T(8,128)}, u32[]{:S(2)}) copy-start(s32[16,32,128]{2,1,0:T(8,128)} %refs_2_.3) | copy-start | bytes 786436
  38.0 19.9 %all-to-all-start = ((f32[16,4,128]{2,1,0:T(4,128)}), f32[16,4,128]{2,1,0:T(4,128)S(1)}, u32[]{:S(2)}, u32[]{:S(2)}) async-start(f32[16,4,128]{2,1,0:T(4,128)} %bitcast.4), calls=%async_computation | async-start | bytes 65536 | tf_op jit(solution)/shard_map/all_to_all | solution.py:570
